TPU v7x, 32 devices: a whole 2x2x4 slice. The times are simulated.
32 devices in a mesh: sub: 2 (over y), front: 16 (over z, x, core).
Axes of the slice: x: 2, y: 2, z: 4, core: 2. Of those that a mesh axis runs over, the one named last changes fastest.
Arguments:
- rhs_root: float32 [22528, 128], P(('sub', 'front')), may hold values from -6 to 6
- rhs_level: float32 [11264, 128], P(('sub', 'front')), may hold values from -6 to 6
- root_inverse: bfloat16 [22528, 22528], P('front', 'sub'), as said below
- level_inverse: bfloat16 [11264, 11264], P('front', 'sub'), as said below
- coupling_t: bfloat16 [11264, 2816], P('front', 'sub'), may hold values from -0.078125 to 0.078125
- coupling_rows: int32 [16, 22], P('front', 'sub'), may hold values from 0 to 175, as said below
Outputs:
- root_potential: float32 [22528, 128], P(('sub', 'front'))
- level_potential: float32 [11264, 128], P(('sub', 'front'))
Inputs may be any that keep to these rules, and one draw needn't show every extreme that they name: `root_inverse`: zero above the diagonal; diagonal entries between 0.5 and 1.5. `level_inverse`: zero above the diagonal; diagonal entries between 0.5 and 1.5. `coupling_rows`: entry [p, j] lies in the range of 88 blocks that starts at block (j // 11) * 88; the 11 entries of one panel in one range are distinct; every row block is named by some panel.
All inputs are finite; a program needn't handle non-finite values.
Results may differ from a plain program's by a relative error of at most 0.02.
Values may be sent and summed in bfloat16 or wider, within the bound.
No kernel may reach another device: no remote copies, remote signals or barrier semaphores. Data moves between devices by JAX's collectives and lax.ppermute only.
A program may use at most 128 MiB of HBM per device.

v0:
```python
import jax
import jax.numpy as jnp
from jax import lax
from jax.sharding import PartitionSpec as P

RB = 128


HIGHEST_PRECISION = lax.Precision.HIGHEST


def gather_columns(pieces):
    return lax.all_gather(pieces, "front", axis=0, tiled=True)


def gather_rows(pieces):
    return lax.all_gather(pieces, "sub", axis=0, tiled=True)


def share_sub(summand):
    return lax.psum_scatter(
        summand.astype(jnp.bfloat16), "sub", scatter_dimension=0, tiled=True
    ).astype(jnp.float32)


def share_front(summand):
    return lax.psum_scatter(summand, "front", scatter_dimension=0, tiled=True)


def transposed_product(matrix, vector):
    return lax.dot_general(
        matrix, vector, (((0,), (0,)), ((), ())), preferred_element_type=jnp.float32
    )


def body(rhs_root, rhs_level, root_inverse, level_inverse, coupling_t, coupling_rows):
    rhs_count = rhs_root.shape[1]
    block_count = root_inverse.shape[1] // RB
    slot_count = coupling_t.shape[1] // RB
    level_cols = gather_columns(rhs_level.astype(jnp.bfloat16))
    forward_level = share_sub(
        jnp.dot(level_inverse, level_cols, preferred_element_type=jnp.float32)
    )
    level_rows = gather_rows(forward_level.astype(jnp.bfloat16))
    local_block = coupling_rows[0] % block_count
    selector = (
        lax.broadcasted_iota(jnp.int32, (block_count, slot_count), 0) == local_block[None, :]
    ).astype(jnp.float32)
    pushed = transposed_product(coupling_t, level_rows).reshape(slot_count, RB, rhs_count)
    update = jnp.einsum("bk,kin->bin", selector, pushed, precision=HIGHEST_PRECISION).reshape(
        block_count * RB, rhs_count
    )
    shifted = rhs_root - share_front(update)
    root_cols = gather_columns(shifted.astype(jnp.bfloat16))
    forward_root = share_sub(jnp.dot(root_inverse, root_cols, preferred_element_type=jnp.float32))
    root_rows = gather_rows(forward_root.astype(jnp.bfloat16))
    root_potential = share_front(transposed_product(root_inverse, root_rows))
    potential_cols = gather_columns(root_potential.astype(jnp.bfloat16))
    picked = potential_cols.reshape(block_count, RB, rhs_count)[local_block]
    pulled = jnp.dot(
        coupling_t, picked.reshape(slot_count * RB, rhs_count), preferred_element_type=jnp.float32
    )
    corrected = forward_level - share_sub(pulled)
    corrected_rows = gather_rows(corrected.astype(jnp.bfloat16))
    level_potential = share_front(transposed_product(level_inverse, corrected_rows))
    return (root_potential, level_potential)


def solution(mesh):
    return jax.shard_map(
        body,
        mesh=mesh,
        in_specs=(
            P(("sub", "front"), None),
            P(("sub", "front"), None),
            P("front", "sub"),
            P("front", "sub"),
            P("front", "sub"),
            P("front", "sub"),
        ),
        out_specs=(P(("sub", "front"), None), P(("sub", "front"), None)),
        check_vma=False,
    )
```

profile of v0, /device:TPU:0, one launch (start us, length us, event | category | flops | bytes accessed | tf_op | source)
XLA Modules:
  0.0 495.1 jit_solution(1017090353970349401)
XLA Ops:
  7.2 0.0 copy-start
  7.2 0.0 all-gather.4.cloned.1.call-start
  7.2 1.7 convert_element_type.37
  8.9 0.0 all-gather.4.cloned.1.call-update
  9.0 0.0 reduce-scatter.13.cloned.1.call-start
  9.0 43.9 %all-gather.4.cloned.1.call-done = bf16[5632,128]{1,0:T(8,128)(2,1)} async-done(((bf16[352,128]{1,0:T(8,128)(2,1)}), bf16[5632,128]{1,0:T(8,128)(2,1)}) %all-gather.4.cloned.1.call-update) | async-done | bytes 1441808 | tf_op jit(solution)/shard_map/all_gather | solution.py:13
  52.9 6.5 %convolution_convert_fusion.2 = bf16[704,128]{1,0:T(8,128)(2,1)} fusion(bf16[704,5632]{1,0:T(8,128)(2,1)} %param.9, bf16[5632,128]{1,0:T(8,128)(2,1)} %all-gather.4.cloned.1.call-done), kind=kOutput, calls=%fused_computation.7 | convolution fusion | flops 1015111680 | bytes 9551872 | tf_op jit(solution)/shard_map/dot_general | solution.py:42
  59.4 0.0 reduce-scatter.13.cloned.1.call-update
  59.4 0.0 reduce-scatter.15.cloned.1.call-start
  59.5 9.7 %reduce-scatter.13.cloned.1.call-done = bf16[352,128]{1,0:T(8,128)(2,1)} async-done(((bf16[704,128]{1,0:T(8,128)(2,1)}), bf16[352,128]{1,0:T(8,128)(2,1)}) %reduce-scatter.13.cloned.1.call-update) | async-done | bytes 90128 | tf_op jit(solution)/shard_map/reduce_scatter | solution.py:21
  69.2 5.4 %all_gather.19 = bf16[704,128]{1,0:T(8,128)(2,1)S(1)} all-gather(bf16[352,128]{1,0:T(8,128)(2,1)} %reduce-scatter.13.cloned.1.call-done), channel_id=1, replica_groups=mesh['sub'=2,'front'=16] {'sub'}, dimensions={0}, use_global_device_ids=true | all-gather | bytes 270336 | tf_op jit(solution)/shard_map/all_gather | solution.py:17
  74.6 0.5 convolution_bitcast_fusion.2
  75.1 0.3 copy.24
  75.3 2.5 fusion.2
  77.9 3.5 copy.26
  81.4 0.0 reduce-scatter.15.cloned.1.call-update
  81.4 0.0 all-gather.6.cloned.1.call-start
  81.5 81.7 %reduce-scatter.15.cloned.1.call-done = f32[704,128]{1,0:T(8,128)} async-done(((f32[11264,128]{1,0:T(8,128)}), f32[704,128]{1,0:T(8,128)}) %reduce-scatter.15.cloned.1.call-update) | async-done | bytes 360464 | tf_op jit(solution)/shard_map/reduce_scatter | solution.py:27
  163.2 1.7 subtract_convert_fusion
  164.9 0.0 all-gather.6.cloned.1.call-update
  164.9 0.0 reduce-scatter.19.cloned.1.call-start
  165.0 44.5 %all-gather.6.cloned.1.call-done = bf16[11264,128]{1,0:T(8,128)(2,1)} async-done(((bf16[704,128]{1,0:T(8,128)(2,1)}), bf16[11264,128]{1,0:T(8,128)(2,1)}) %all-gather.6.cloned.1.call-update) | async-done | bytes 2883600 | tf_op jit(solution)/shard_map/all_gather | solution.py:13
  209.5 15.8 %fusion = bf16[1408,128]{0,1:T(8,128)(2,1)S(1)} fusion(bf16[11264,128]{1,0:T(8,128)(2,1)} %all-gather.6.cloned.1.call-done, bf16[1408,11264]{1,0:T(8,128)(2,1)} %param.8), kind=kOutput, calls=%fused_computation.5 | convolution fusion | flops 4060266496 | bytes 34963456 | tf_op jit(solution)/shard_map/dot_general | solution.py:55
  225.3 0.9 copy.31
  226.2 0.0 reduce-scatter.19.cloned.1.call-update
  226.2 0.0 reduce-scatter.21.cloned.1.call-start
  226.3 11.2 %reduce-scatter.19.cloned.1.call-done = bf16[704,128]{1,0:T(8,128)(2,1)} async-done(((bf16[1408,128]{1,0:T(8,128)(2,1)}), bf16[704,128]{1,0:T(8,128)(2,1)}) %reduce-scatter.19.cloned.1.call-update) | async-done | bytes 180240 | tf_op jit(solution)/shard_map/reduce_scatter | solution.py:21
  237.5 7.2 %all_gather.21 = bf16[1408,128]{1,0:T(8,128)(2,1)S(1)} all-gather(bf16[704,128]{1,0:T(8,128)(2,1)} %reduce-scatter.19.cloned.1.call-done), channel_id=1, replica_groups=mesh['sub'=2,'front'=16] {'sub'}, dimensions={0}, use_global_device_ids=true | all-gather | bytes 540672 | tf_op jit(solution)/shard_map/all_gather | solution.py:17
  244.6 15.4 %convolution_bitcast_fusion = f32[11264,128]{0,1:T(8,128)} fusion(bf16[1408,128]{1,0:T(8,128)(2,1)S(1)} %all_gather.21, bf16[1408,11264]{1,0:T(8,128)(2,1)} %param.8), kind=kOutput, calls=%fused_computation.1 | convolution fusion | flops 4060086272 | bytes 37847040 | tf_op jit(solution)/shard_map/dot_general | solution.py:31
  260.1 6.2 %copy.33 = f32[11264,128]{1,0:T(8,128)} copy(f32[11264,128]{0,1:T(8,128)} %convolution_bitcast_fusion) | data formatting | bytes 11534336
  266.3 0.0 reduce-scatter.21.cloned.1.call-update
  266.3 0.0 all-gather.8.cloned.1.call-start
  266.4 81.6 %reduce-scatter.21.cloned.1.call-done = f32[704,128]{1,0:T(8,128)} async-done(((f32[11264,128]{1,0:T(8,128)}), f32[704,128]{1,0:T(8,128)}) %reduce-scatter.21.cloned.1.call-update) | async-done | bytes 360464
  348.0 1.7 convert_element_type.43
  349.7 0.0 all-gather.8.cloned.1.call-update
  349.7 0.0 reduce-scatter.17.cloned.1.call-start
  349.8 44.6 %all-gather.8.cloned.1.call-done = bf16[11264,128]{1,0:T(8,128)(2,1)} async-done(((bf16[704,128]{1,0:T(8,128)(2,1)}), bf16[11264,128]{1,0:T(8,128)(2,1)}) %all-gather.8.cloned.1.call-update) | async-done | bytes 2883600 | tf_op jit(solution)/shard_map/all_gather | solution.py:13
  394.5 2.4 gather_fusion
  396.9 1.4 fusion.1
  398.2 0.0 reduce-scatter.17.cloned.1.call-update
  398.3 0.0 reduce-scatter.23.cloned.1.call-start
  398.3 9.2 %reduce-scatter.17.cloned.1.call-done = bf16[352,128]{1,0:T(8,128)(2,1)} async-done(((bf16[704,128]{1,0:T(8,128)(2,1)}), bf16[352,128]{1,0:T(8,128)(2,1)}) %reduce-scatter.17.cloned.1.call-update) | async-done | bytes 90128 | tf_op jit(solution)/shard_map/reduce_scatter | solution.py:21
  407.5 0.9 subtract_convert_fusion.1
  408.4 5.2 %all_gather.23 = bf16[704,128]{1,0:T(8,128)(2,1)S(1)} all-gather(bf16[352,128]{1,0:T(8,128)(2,1)S(1)} %subtract_convert_fusion.1), channel_id=1, replica_groups=mesh['sub'=2,'front'=16] {'sub'}, dimensions={0}, use_global_device_ids=true | all-gather | bytes 270336 | tf_op jit(solution)/shard_map/all_gather | solution.py:17
  413.7 6.2 %convolution_bitcast_fusion.1 = f32[5632,128]{0,1:T(8,128)} fusion(bf16[704,128]{1,0:T(8,128)(2,1)S(1)} %all_gather.23, bf16[704,5632]{1,0:T(8,128)(2,1)} %param.9), kind=kOutput, calls=%fused_computation.2 | convolution fusion | flops 1015021568 | bytes 10993664 | tf_op jit(solution)/shard_map/dot_general | solution.py:31
  419.8 3.4 copy.35
  423.2 0.0 reduce-scatter.23.cloned.1.call-update
  423.2 65.3 %reduce-scatter.23.cloned.1.call-done = f32[352,128]{1,0:T(8,128)} async-done(((f32[5632,128]{1,0:T(8,128)}), f32[352,128]{1,0:T(8,128)}) %reduce-scatter.23.cloned.1.call-update) | async-done | bytes 180240
  (10 shorter events, 0.0 us)
Async XLA Ops:
  7.2 67.4 %copy-start = (bf16[704,1408]{1,0:T(8,128)(2,1)S(1)}, bf16[704,1408]{1,0:T(8,128)(2,1)}, u32[]{:S(2)}) copy-start(bf16[704,1408]{1,0:T(8,128)(2,1)} %param.10) | copy-start | bytes 5947396
  7.2 52.3 %copy-start.3 = (s32[1,11]{1,0:T(1,128)S(1)}, s32[1,11]{1,0:T(1,128)}, u32[]{:S(2)}) copy-start(s32[1,11]{1,0:T(1,128)} %param.11) | copy-start | bytes 136
  7.2 45.7 %all-gather.4.cloned.1.call-start = ((), (), s32[]{:S(2)}) async-start(), calls=%async_computation.6 | async-start | bytes 1531904 | tf_op jit(solution)/shard_map/all_gather | solution.py:13
  9.0 60.2 %reduce-scatter.13.cloned.1.call-start = ((), (), s32[]{:S(2)}) async-start(), calls=%async_computation.7 | async-start | bytes 270336 | tf_op jit(solution)/shard_map/reduce_scatter | solution.py:21
  59.4 103.8 %reduce-scatter.15.cloned.1.call-start = ((), (), s32[]{:S(2)}) async-start(), calls=%async_computation.8 | async-start | bytes 6127616 | tf_op jit(solution)/shard_map/reduce_scatter | solution.py:27
  81.4 81.8 %copy-start.1 = (f32[704,128]{1,0:T(8,128)S(1)}, f32[704,128]{1,0:T(8,128)}, u32[]{:S(2)}) copy-start(f32[704,128]{1,0:T(8,128)} %param.6) | copy-start | bytes 1081348
  81.4 128.0 %all-gather.6.cloned.1.call-start = ((), (), s32[]{:S(2)}) async-start(), calls=%async_computation.9 | async-start | bytes 3063808 | tf_op jit(solution)/shard_map/all_gather | solution.py:13
  164.9 72.5 %reduce-scatter.19.cloned.1.call-start = ((), (), s32[]{:S(2)}) async-start(), calls=%async_computation.12 | async-start | bytes 540672 | tf_op jit(solution)/shard_map/reduce_scatter | solution.py:21
  226.2 121.8 %reduce-scatter.21.cloned.1.call-start = ((), (), s32[]{:S(2)}) async-start(), calls=%async_computation.13 | async-start | bytes 6127616
  266.3 141.2 %copy-start.2 = (bf16[352,128]{1,0:T(8,128)(2,1)S(1)}, bf16[352,128]{1,0:T(8,128)(2,1)}, u32[]{:S(2)}) copy-start(bf16[352,128]{1,0:T(8,128)(2,1)} %reduce-scatter.13.cloned.1.call-done) | copy-start | bytes 270340
  266.3 128.1 %all-gather.8.cloned.1.call-start = ((), (), s32[]{:S(2)}) async-start(), calls=%async_computation.10 | async-start | bytes 3063808 | tf_op jit(solution)/shard_map/all_gather | solution.py:13
  349.7 57.8 %reduce-scatter.17.cloned.1.call-start = ((), (), s32[]{:S(2)}) async-start(), calls=%async_computation.11 | async-start | bytes 270336 | tf_op jit(solution)/shard_map/reduce_scatter | solution.py:21
  398.3 90.3 %reduce-scatter.23.cloned.1.call-start = ((), (), s32[]{:S(2)}) async-start(), calls=%async_computation.14 | async-start | bytes 3063808
Sparse Core Ops, SparseCore 0:
  10.9 41.9 all-gather.3
  59.5 9.5 reduce-scatter.12
  81.6 81.6 reduce-scatter.14
  165.9 43.5 all-gather.5
  226.3 11.0 reduce-scatter.18
  266.5 81.5 reduce-scatter.20
  350.9 43.5 all-gather.7
  398.4 9.0 reduce-scatter.16
  423.4 65.1 reduce-scatter.22
where the time goes:
time: 496 us; the launch traced here: 495 us
  waiting for transfers between devices  392 us (79%)
  matrix products  48.3 us (10%)
  blocking collectives  17.8 us (4%)
  local copies, waits for them, and re-layouts  16.8 us (3%)
  between operations  13.9 us (3%)
  other arithmetic  6.02 us (1%)
    unnamed x11, waiting for transfers between devices  147 us
    all_gather x3, waiting for transfers between devices, gather_columns(): return lax.all_gather(pieces, 'front', axis=0, tiled=True)  133 us
    reduce_scatter x1, waiting for transfers between devices, share_front(): return lax.psum_scatter(summand, 'front', scatter_dimension=0, tiled=True)  81.7 us
    reduce_scatter x3, waiting for transfers between devices, share_sub(): lax.psum_scatter(summand.astype(jnp.bfloat16), 'sub', scatter_dimension=0...  30.1 us
    dot_general x3, matrix products, transposed_product(): lax.dot_general(matrix, vector, (((0,), (0,)), ((), ())), preferred_eleme...  22.1 us
    all_gather x3, blocking collectives, gather_rows(): return lax.all_gather(pieces, 'sub', axis=0, tiled=True)  17.8 us
    dot_general x1, matrix products, body(): jnp.dot(root_inverse, root_cols, preferred_element_type=jnp.float32)  15.8 us
    unnamed x11, local copies, waits for them, and re-layouts  10.6 us
  transfers between devices with their start and end apart: 9, of which 9 were waited for; matrix products, arithmetic and copies ran while one was open for 0% of the time, Pallas kernels for 0%

commit v1 on v0

--- a/solution.py
+++ b/solution.py
@@ -1,12 +1,27 @@
+import functools
+
 import jax
 import jax.numpy as jnp
 from jax import lax
+from jax.experimental import pallas as pl
+from jax.experimental.pallas import tpu as pltpu
 from jax.sharding import PartitionSpec as P
 
 RB = 128
-
-
+NX = 2
+NC = 2
+F32 = jnp.float32
+BF16 = jnp.bfloat16
 HIGHEST_PRECISION = lax.Precision.HIGHEST
+VMEM = pl.BlockSpec(memory_space=pltpu.VMEM)
+SMEM = pl.BlockSpec(memory_space=pltpu.SMEM)
+VMEM_LIMIT = 48 * 1024 * 1024
+
+
+def transposed_product(matrix, vector):
+    return lax.dot_general(
+        matrix, vector, (((0,), (0,)), ((), ())), preferred_element_type=jnp.float32
+    )
 
 
 def gather_columns(pieces):
@@ -27,13 +42,7 @@
     return lax.psum_scatter(summand, "front", scatter_dimension=0, tiled=True)
 
 
-def transposed_product(matrix, vector):
-    return lax.dot_general(
-        matrix, vector, (((0,), (0,)), ((), ())), preferred_element_type=jnp.float32
-    )
-
-
-def body(rhs_root, rhs_level, root_inverse, level_inverse, coupling_t, coupling_rows):
+def general_body(rhs_root, rhs_level, root_inverse, level_inverse, coupling_t, coupling_rows):
     rhs_count = rhs_root.shape[1]
     block_count = root_inverse.shape[1] // RB
     slot_count = coupling_t.shape[1] // RB
@@ -64,6 +73,287 @@
     corrected_rows = gather_rows(corrected.astype(jnp.bfloat16))
     level_potential = share_front(transposed_product(level_inverse, corrected_rows))
     return (root_potential, level_potential)
+
+
+def z_shift(value, shift, nz):
+    width = NX * NC
+    count = nz * width
+    return lax.ppermute(
+        value, "front", [(i, (i + shift * width) % count) for i in range(count)]
+    )
+
+
+def x_swap(value, nz):
+    return lax.ppermute(value, "front", [(i, i ^ NC) for i in range(nz * NX * NC)])
+
+
+def c_swap(value, nz):
+    return lax.ppermute(value, "front", [(i, i ^ 1) for i in range(nz * NX * NC)])
+
+
+def sub_swap(value):
+    return lax.ppermute(value, "sub", [(0, 1), (1, 0)])
+
+
+def gather_pieces(own, nz):
+    along_z = [own] + [z_shift(own, -k, nz) for k in range(1, nz)]
+    pieces = []
+    for held in along_z:
+        across = x_swap(held, nz)
+        pieces += [held, c_swap(held, nz), across, c_swap(across, nz)]
+    return pieces
+
+
+def scatter_sum(keep, send, nz):
+    total = None
+    for k in list(range(1, nz)) + [0]:
+        arrived = c_swap(send[k], nz)
+        near = keep[k][0].astype(F32) + arrived[0].astype(F32)
+        far = keep[k][1].astype(F32) + arrived[1].astype(F32)
+        partial = near + x_swap(far.astype(BF16), nz).astype(F32)
+        if k:
+            partial = z_shift(partial.astype(BF16), k, nz).astype(F32)
+        total = partial if total is None else total + partial
+    return total
+
+
+def places(nz):
+    me = lax.axis_index("front")
+    z, x, c = me // (NX * NC), (me // NC) % NX, me % NC
+    return jnp.stack(
+        [
+            (((z + k) % nz) * NX + (x ^ xr)) * NC + (c ^ cr)
+            for k in range(nz)
+            for xr in range(NX)
+            for cr in range(NC)
+        ]
+    ).astype(jnp.int32)
+
+
+def assemble(place, pieces, whole):
+    rows = pieces[0].shape[0]
+    for i, piece in enumerate(pieces):
+        whole[pl.ds(pl.multiple_of(place[i] * rows, rows), rows), :] = piece[...]
+
+
+def distribute(place, whole, keep, send):
+    nz = len(keep)
+    rows = keep[0].shape[1]
+    for k in range(nz):
+        for xr in range(NX):
+            for cr, out in ((0, keep[k]), (1, send[k])):
+                i = (k * NX + xr) * NC + cr
+                out[xr] = whole[
+                    pl.ds(pl.multiple_of(place[i] * rows, rows), rows), :
+                ].astype(out.dtype)
+
+
+def forward_kernel(count, place, *refs):
+    pieces, (matrix, out, out_b, whole) = refs[:count], refs[count:]
+    step = pl.program_id(0)
+    depth = matrix.shape[1]
+
+    @pl.when(step == 0)
+    def _():
+        assemble(place, pieces, whole)
+        out[...] = jnp.zeros_like(out)
+
+    cols = whole[pl.ds(pl.multiple_of(step * depth, depth), depth), :]
+    out[...] += jnp.dot(matrix[...], cols, preferred_element_type=F32)
+
+    @pl.when(step == pl.num_programs(0) - 1)
+    def _():
+        out_b[...] = out[...].astype(BF16)
+
+
+def forward_product(place, pieces, matrix, depth):
+    rows, width = matrix.shape
+    n = pieces[0].shape[1]
+    whole_spec = lambda shape: pl.BlockSpec(shape, lambda i, *_: (0,) * len(shape))
+    return pl.pallas_call(
+        functools.partial(forward_kernel, len(pieces)),
+        out_shape=(
+            jax.ShapeDtypeStruct((rows, n), F32),
+            jax.ShapeDtypeStruct((rows, n), BF16),
+        ),
+        grid_spec=pltpu.PrefetchScalarGridSpec(
+            num_scalar_prefetch=1,
+            grid=(width // depth,),
+            in_specs=[whole_spec(p.shape) for p in pieces]
+            + [pl.BlockSpec((rows, depth), lambda i, *_: (0, i))],
+            out_specs=(whole_spec((rows, n)), whole_spec((rows, n))),
+            scratch_shapes=[pltpu.VMEM((width, n), BF16)],
+        ),
+        compiler_params=pltpu.CompilerParams(vmem_limit_bytes=VMEM_LIMIT),
+        cost_estimate=pl.CostEstimate(
+            flops=2 * rows * width * n, bytes_accessed=2 * rows * width, transcendentals=0
+        ),
+        name="forward_product",
+    )(place, *pieces, matrix)
+
+
+def backward_kernel(nz, subtract, place, own, arrived, base, matrix, *refs):
+    keep, send, (vector, whole) = refs[:nz], refs[nz : 2 * nz], refs[2 * nz :]
+    step = pl.program_id(0)
+    width = matrix.shape[1]
+
+    @pl.when(step == 0)
+    def _():
+        total = own[...] + arrived[...].astype(F32)
+        if subtract:
+            total = base[...] - total
+        vector[...] = total.T.astype(BF16)
+
+    product = jnp.dot(vector[...], matrix[...], preferred_element_type=F32)
+    whole[pl.ds(pl.multiple_of(step * width, width), width), :] = product.T
+
+    @pl.when(step == pl.num_programs(0) - 1)
+    def _():
+        distribute(place, whole, keep, send)
+
+
+def backward_product(place, own, arrived, base, matrix, block, nz):
+    rows, width = matrix.shape
+    n = own.shape[1]
+    part = width // (nz * NX * NC)
+    subtract = base is not None
+    if base is None:
+        base = jnp.zeros((8, 128), F32)
+    whole_spec = lambda shape: pl.BlockSpec(shape, lambda i, *_: (0,) * len(shape))
+    outs = pl.pallas_call(
+        functools.partial(backward_kernel, nz, subtract),
+        out_shape=[jax.ShapeDtypeStruct((NX, part, n), F32)] * nz
+        + [jax.ShapeDtypeStruct((NX, part, n), BF16)] * nz,
+        grid_spec=pltpu.PrefetchScalarGridSpec(
+            num_scalar_prefetch=1,
+            grid=(width // block,),
+            in_specs=[whole_spec(own.shape), whole_spec(own.shape), whole_spec(base.shape)]
+            + [pl.BlockSpec((rows, block), lambda i, *_: (0, i))],
+            out_specs=[whole_spec((NX, part, n))] * (2 * nz),
+            scratch_shapes=[pltpu.VMEM((n, rows), BF16), pltpu.VMEM((width, n), F32)],
+        ),
+        compiler_params=pltpu.CompilerParams(vmem_limit_bytes=VMEM_LIMIT),
+        cost_estimate=pl.CostEstimate(
+            flops=2 * rows * width * n, bytes_accessed=2 * rows * width, transcendentals=0
+        ),
+        name="backward_product",
+    )(place, own, arrived, base, matrix)
+    return outs[:nz], outs[nz:]
+
+
+def push_kernel(nz, place, block, own, arrived, coupling, *refs):
+    total_out, keep, send, (whole,) = refs[0], refs[1 : nz + 1], refs[nz + 1 : 2 * nz + 1], refs[2 * nz + 1 :]
+    total = own[...] + arrived[...].astype(F32)
+    total_out[...] = total
+    pushed = jnp.dot(total.T.astype(BF16), coupling[...], preferred_element_type=F32).T
+    whole[...] = jnp.zeros_like(whole)
+    for j in range(coupling.shape[1] // RB):
+        start = pl.multiple_of(block[j] * RB, RB)
+        whole[pl.ds(start, RB), :] = pushed[j * RB : (j + 1) * RB, :]
+    distribute(place, whole, keep, send)
+
+
+def push_product(place, block, own, arrived, coupling, width, nz):
+    n = own.shape[1]
+    part = width // (nz * NX * NC)
+    outs = pl.pallas_call(
+        functools.partial(push_kernel, nz),
+        out_shape=[jax.ShapeDtypeStruct(own.shape, F32)]
+        + [jax.ShapeDtypeStruct((NX, part, n), F32)] * nz
+        + [jax.ShapeDtypeStruct((NX, part, n), BF16)] * nz,
+        in_specs=[SMEM, SMEM, VMEM, VMEM, VMEM],
+        out_specs=[VMEM] * (2 * nz + 1),
+        scratch_shapes=[pltpu.VMEM((width, n), F32)],
+        compiler_params=pltpu.CompilerParams(vmem_limit_bytes=VMEM_LIMIT),
+        name="push_product",
+    )(place, block, own, arrived, coupling)
+    return outs[0], outs[1 : nz + 1], outs[nz + 1 :]
+
+
+def pull_kernel(count, place, block, *refs):
+    pieces, (coupling, out, out_b, whole, picked) = refs[:count], refs[count:]
+    assemble(place, pieces, whole)
+    for j in range(coupling.shape[1] // RB):
+        start = pl.multiple_of(block[j] * RB, RB)
+        picked[j * RB : (j + 1) * RB, :] = whole[pl.ds(start, RB), :]
+    out[...] = jnp.dot(coupling[...], picked[...], preferred_element_type=F32)
+    out_b[...] = out[...].astype(BF16)
+
+
+def pull_product(place, block, pieces, coupling):
+    rows, width = coupling.shape
+    part, n = pieces[0].shape
+    return pl.pallas_call(
+        functools.partial(pull_kernel, len(pieces)),
+        out_shape=(
+            jax.ShapeDtypeStruct((rows, n), F32),
+            jax.ShapeDtypeStruct((rows, n), BF16),
+        ),
+        in_specs=[SMEM, SMEM] + [VMEM] * (len(pieces) + 1),
+        out_specs=(VMEM, VMEM),
+        scratch_shapes=[
+            pltpu.VMEM((part * len(pieces), n), BF16),
+            pltpu.VMEM((width, n), BF16),
+        ],
+        compiler_params=pltpu.CompilerParams(vmem_limit_bytes=VMEM_LIMIT),
+        name="pull_product",
+    )(place, block, *pieces, coupling)
+
+
+def column_block(width):
+    for parts in (8, 4, 2, 1):
+        if width % (parts * 128) == 0 and width // parts >= 1024:
+            return width // parts
+    return width
+
+
+def two_level_body(rhs_root, rhs_level, root_inverse, level_inverse, coupling_t, coupling_rows):
+    nz = lax.axis_size("front") // (NX * NC)
+    width = root_inverse.shape[1]
+    place = places(nz)
+    block = coupling_rows[0] % (width // RB)
+
+    level_pieces = gather_pieces(rhs_level.astype(BF16), nz)
+    own, own_b = forward_product(
+        place, level_pieces, level_inverse, column_block(level_inverse.shape[1])
+    )
+    forward_level, keep, send = push_product(
+        place, block, own, sub_swap(own_b), coupling_t, width, nz
+    )
+    shifted = rhs_root - scatter_sum(keep, send, nz)
+
+    root_pieces = gather_pieces(shifted.astype(BF16), nz)
+    own, own_b = forward_product(place, root_pieces, root_inverse, column_block(width))
+    keep, send = backward_product(
+        place, own, sub_swap(own_b), None, root_inverse, column_block(width), nz
+    )
+    root_potential = scatter_sum(keep, send, nz)
+
+    potential_pieces = gather_pieces(root_potential.astype(BF16), nz)
+    own, own_b = pull_product(place, block, potential_pieces, coupling_t)
+    keep, send = backward_product(
+        place,
+        own,
+        sub_swap(own_b),
+        forward_level,
+        level_inverse,
+        column_block(level_inverse.shape[1]),
+        nz,
+    )
+    level_potential = scatter_sum(keep, send, nz)
+    return (root_potential, level_potential)
+
+
+def body(rhs_root, rhs_level, root_inverse, level_inverse, coupling_t, coupling_rows):
+    fits = (
+        lax.axis_size("sub") == 2
+        and lax.axis_size("front") % (2 * NX * NC) == 0
+        and all(a.shape[0] % 16 == 0 for a in (rhs_root, rhs_level, root_inverse, level_inverse))
+        and all(a.shape[1] % 128 == 0 for a in (rhs_root, root_inverse, level_inverse, coupling_t))
+        and root_inverse.size * 2 <= 34 * 1024 * 1024
+    )
+    chosen = two_level_body if fits else general_body
+    return chosen(rhs_root, rhs_level, root_inverse, level_inverse, coupling_t, coupling_rows)
 
 
 def solution(mesh):

time: 496 us -> 224 us (0.45)
  waiting for transfers between devices: 392 us -> 84.5 us
  starting transfers between devices: 0.37 us -> 86.6 us
  matrix products: 48.3 us -> 0 us
  Pallas kernels: 0 us -> 47.2 us
  blocking collectives: 17.8 us -> 0 us
  local copies, waits for them, and re-layouts: 16.8 us -> 0.11 us
  between operations: 13.9 us -> 0.97 us
    unnamed x11 -> x0, waiting for transfers between devices: 147 us -> none
    all_gather x3 -> x0, waiting for transfers between devices: 133 us -> none  [gather_columns(): return lax.all_gather(pieces, 'front', axis=0, tiled=True)]
    reduce_scatter x4 -> x0, waiting for transfers between devices: 112 us -> none  [the longest x1 81.7 us: share_front(): return lax.psum_scatter(summand, 'front', scatter_dimension=0, tiled=True)]
    ppermute x0 -> x81, starting transfers between devices: none -> 86.6 us  [the longest x18 47.2 us: z_shift(): lax.ppermute(value, 'front', [(i, (i + shift * width) % count) for i in r...]
    ppermute x0 -> x81, waiting for transfers between devices: none -> 84.5 us  [the longest x18 30.8 us: z_shift(): lax.ppermute(value, 'front', [(i, (i + shift * width) % count) for i in r...]
    dot_general x7 -> x0, matrix products: 48.3 us -> none  [the longest x3 22.1 us: transposed_product(): lax.dot_general(matrix, vector, (((0,), (0,)), ((), ())), preferred_eleme...]
    pallas_call x0 -> x6, Pallas kernels: none -> 47.2 us  [the longest x2 22.1 us: forward_product(): pl.pallas_call(functools.partial(forward_kernel, len(pieces)), out_shape=...]
    all_gather x3 -> x0, blocking collectives: 17.8 us -> none  [gather_rows(): return lax.all_gather(pieces, 'sub', axis=0, tiled=True)]
  transfers between devices with their start and end apart: 9 -> 81, of which waited for: 9 -> 32; matrix products, arithmetic and copies ran while one was open for 0% -> 0% of each run, Pallas kernels for 0% -> 0%
where the time goes in v1:
time: 224 us; the launch traced here: 223 us
  starting transfers between devices  86.6 us (39%)
  waiting for transfers between devices  84.5 us (38%)
  Pallas kernels  47.2 us (21%)
  other arithmetic  3.63 us (2%)
    ppermute x18, starting transfers between devices, z_shift(): lax.ppermute(value, 'front', [(i, (i + shift * width) % count) for i in r...  47.2 us
    ppermute x18, waiting for transfers between devices, z_shift(): lax.ppermute(value, 'front', [(i, (i + shift * width) % count) for i in r...  30.8 us
    ppermute x24, waiting for transfers between devices, x_swap(): lax.ppermute(value, 'front', [(i, i ^ NC) for i in range(nz * NX * NC)])  28.9 us
    ppermute x24, starting transfers between devices, x_swap(): lax.ppermute(value, 'front', [(i, i ^ NC) for i in range(nz * NX * NC)])  27.9 us
    pallas_call x2, Pallas kernels, forward_product(): pl.pallas_call(functools.partial(forward_kernel, len(pieces)), out_shape=...  22.1 us
    pallas_call x2, Pallas kernels, backward_product(): pl.pallas_call(functools.partial(backward_kernel, nz, subtract), out_shap...  20.9 us
    ppermute x3, waiting for transfers between devices, sub_swap(): return lax.ppermute(value, 'sub', [(0, 1), (1, 0)])  19.1 us
    ppermute x36, starting transfers between devices, c_swap(): lax.ppermute(value, 'front', [(i, i ^ 1) for i in range(nz * NX * NC)])  6.82 us
  transfers between devices with their start and end apart: 81, of which 32 were waited for; matrix products, arithmetic and copies ran while one was open for 0% of the time, Pallas kernels for 0%

profile of v1, /device:TPU:0, one launch (start us, length us, event | category | flops | bytes accessed | tf_op | source)
XLA Modules:
  0.0 223.1 jit_solution(5636427336969065915)
XLA Ops:
  1.6 3.1 %collective-permute-start.11 = (bf16[352,128]{1,0:T(8,128)(2,1)S(1)}, bf16[352,128]{1,0:T(8,128)(2,1)S(1)}, u32[]{:S(2)}, u32[]{:S(2)}) collective-permute-start(bf16[352,128]{1,0:T(8,128)(2,1)S(1)} %convert_element_type.267.refs_0_), channel_id=1, source_target_pairs={{0,4},{1,5},{2,6},{3,7},{4,8},{5,9},{6,10},{7,11},{8,12},{9,13},{1... | collective-permute-start | bytes 270344 | tf_op jit(solution)/shard_map/ppermute | solution.py:81
  4.7 2.6 %collective-permute-start.7 = (bf16[352,128]{1,0:T(8,128)(2,1)S(1)}, bf16[352,128]{1,0:T(8,128)(2,1)S(1)}, u32[]{:S(2)}, u32[]{:S(2)}) collective-permute-start(bf16[352,128]{1,0:T(8,128)(2,1)S(1)} %convert_element_type.267.refs_0_), channel_id=1, source_target_pairs={{0,8},{1,9},{2,10},{3,11},{4,12},{5,13},{6,14},{7,15},{8,0},{9,1},... | collective-permute-start | bytes 270344 | tf_op jit(solution)/shard_map/ppermute | solution.py:81
  11.6 1.7 collective-permute-done.7.refs_8_
  16.1 2.5 %collective-permute-done.9.refs_10_ = bf16[352,128]{1,0:T(8,128)(2,1)S(1)} collective-permute-done((bf16[352,128]{1,0:T(8,128)(2,1)S(1)}, bf16[352,128]{1,0:T(8,128)(2,1)S(1)}, u32[]{:S(2)}, u32[]{:S(2)}) %collective-permute-start.9) | collective-permute-done | bytes 90144 | tf_op jit(solution)/shard_map/ppermute | solution.py:87
  21.5 6.1 %forward_product.2 = (f32[704,128]{1,0:T(8,128)S(1)}, bf16[704,128]{1,0:T(8,128)(2,1)S(1)}) custom-call(s32[16]{0:T(128)S(1)} %stack.67.place, bf16[352,128]{1,0:T(8,128)(2,1)S(1)} %convert_element_type.267.refs_0_, bf16[352,128]{1,0:T(8,128)(2,1)S(1)} %collective-permute-done.refs_1_, bf16[352,128]{1,0:T(8,128)(2,1)S(1)} %collective-permute-done.1.refs_2_, ...), custom_call_target="tpu_custom_call" | custom-call | flops 1015021568 | bytes 7929856 | tf_op jit(solution)/shard_map/forward_product/pallas_call | solution.py:173
  27.6 1.6 collective-permute-start.15
  29.2 5.1 %collective-permute-done.15.arrived = bf16[704,128]{1,0:T(8,128)(2,1)S(1)} collective-permute-done((bf16[704,128]{1,0:T(8,128)(2,1)S(1)}, bf16[704,128]{1,0:T(8,128)(2,1)S(1)}, u32[]{:S(2)}, u32[]{:S(2)}) %collective-permute-start.15) | collective-permute-done | bytes 180256 | tf_op jit(solution)/shard_map/ppermute | solution.py:95
  34.3 2.9 %push_product.1 = (f32[704,128]{1,0:T(8,128)S(1)}, f32[2,704,128]{2,1,0:T(8,128)S(1)}, f32[2,704,128]{2,1,0:T(8,128)S(1)}, f32[2,704,128]{2,1,0:T(8,128)S(1)}, f...) custom-call(s32[16]{0:T(128)S(1)} %stack.67.place, ...), custom_call_target="tpu_custom_call" | custom-call | tf_op jit(solution)/shard_map/push_product/pallas_call | solution.py:259
  38.9 1.5 collective-permute-start.17
  41.2 1.6 collective-permute-start.23
  43.4 3.0 %collective-permute-done.17 = bf16[704,128]{1,0:T(8,128)(2,1)S(1)} collective-permute-done((bf16[704,128]{1,0:T(8,128)(2,1)S(1)}, bf16[704,128]{1,0:T(8,128)(2,1)S(1)}, u32[]{:S(2)}, u32[]{:S(2)}) %collective-permute-start.17) | collective-permute-done | bytes 180256 | tf_op jit(solution)/shard_map/ppermute | solution.py:87
  46.5 2.0 collective-permute-start.18
  48.5 1.8 collective-permute-done.20
  50.3 3.3 %collective-permute-start.21 = (bf16[704,128]{1,0:T(8,128)(2,1)S(1)}, bf16[704,128]{1,0:T(8,128)(2,1)S(1)}, u32[]{:S(2)}, u32[]{:S(2)}) collective-permute-start(bf16[704,128]{1,0:T(8,128)(2,1)S(1)} %fusion.8), channel_id=1, source_target_pairs={{0,8},{1,9},{2,10},{3,11},{4,12},{5,13},{6,14},{7,15},{8,0},{9,1},... | collective-permute-start | bytes 540680 | tf_op jit(solution)/shard_map/ppermute | solution.py:81
  54.2 3.6 %collective-permute-start.24 = (bf16[704,128]{1,0:T(8,128)(2,1)S(1)}, bf16[704,128]{1,0:T(8,128)(2,1)S(1)}, u32[]{:S(2)}, u32[]{:S(2)}) collective-permute-start(bf16[704,128]{1,0:T(8,128)(2,1)S(1)} %fusion.7), channel_id=1, source_target_pairs={{0,12},{1,13},{2,14},{3,15},{4,0},{5,1},{6,2},{7,3},{8,4},{9,5},{1... | collective-permute-start | bytes 540680 | tf_op jit(solution)/shard_map/ppermute | solution.py:81
  57.8 3.9 %collective-permute-done.21 = bf16[704,128]{1,0:T(8,128)(2,1)S(1)} collective-permute-done((bf16[704,128]{1,0:T(8,128)(2,1)S(1)}, bf16[704,128]{1,0:T(8,128)(2,1)S(1)}, u32[]{:S(2)}, u32[]{:S(2)}) %collective-permute-start.21) | collective-permute-done | bytes 180256 | tf_op jit(solution)/shard_map/ppermute | solution.py:81
  61.7 1.5 collective-permute-done.24
  63.3 2.9 %collective-permute-start.38 = (bf16[704,128]{1,0:T(8,128)(2,1)S(1)}, bf16[704,128]{1,0:T(8,128)(2,1)S(1)}, u32[]{:S(2)}, u32[]{:S(2)}) collective-permute-start(bf16[704,128]{1,0:T(8,128)(2,1)S(1)} %fusion.6.refs_0_), channel_id=1, source_target_pairs={{0,4},{1,5},{2,6},{3,7},{4,8},{5,9},{6,10},{7,11},{8,12},{9,13},{1... | collective-permute-start | bytes 540680 | tf_op jit(solution)/shard_map/ppermute | solution.py:81
  66.2 2.3 %collective-permute-start.34 = (bf16[704,128]{1,0:T(8,128)(2,1)S(1)}, bf16[704,128]{1,0:T(8,128)(2,1)S(1)}, u32[]{:S(2)}, u32[]{:S(2)}) collective-permute-start(bf16[704,128]{1,0:T(8,128)(2,1)S(1)} %fusion.6.refs_0_), channel_id=1, source_target_pairs={{0,8},{1,9},{2,10},{3,11},{4,12},{5,13},{6,14},{7,15},{8,0},{9,1},... | collective-permute-start | bytes 540680 | tf_op jit(solution)/shard_map/ppermute | solution.py:81
  70.1 3.3 %collective-permute-done.38.refs_12_ = bf16[704,128]{1,0:T(8,128)(2,1)S(1)} collective-permute-done((bf16[704,128]{1,0:T(8,128)(2,1)S(1)}, bf16[704,128]{1,0:T(8,128)(2,1)S(1)}, u32[]{:S(2)}, u32[]{:S(2)}) %collective-permute-start.38) | collective-permute-done | bytes 180256 | tf_op jit(solution)/shard_map/ppermute | solution.py:81
  74.8 5.2 %collective-permute-done.34.refs_8_ = bf16[704,128]{1,0:T(8,128)(2,1)S(1)} collective-permute-done((bf16[704,128]{1,0:T(8,128)(2,1)S(1)}, bf16[704,128]{1,0:T(8,128)(2,1)S(1)}, u32[]{:S(2)}, u32[]{:S(2)}) %collective-permute-start.34) | collective-permute-done | bytes 180256 | tf_op jit(solution)/shard_map/ppermute | solution.py:81
  82.8 4.6 %collective-permute-done.36.refs_10_ = bf16[704,128]{1,0:T(8,128)(2,1)S(1)} collective-permute-done((bf16[704,128]{1,0:T(8,128)(2,1)S(1)}, bf16[704,128]{1,0:T(8,128)(2,1)S(1)}, u32[]{:S(2)}, u32[]{:S(2)}) %collective-permute-start.36) | collective-permute-done | bytes 180256 | tf_op jit(solution)/shard_map/ppermute | solution.py:87
  87.9 3.0 %collective-permute-done.32.refs_6_ = bf16[704,128]{1,0:T(8,128)(2,1)S(1)} collective-permute-done((bf16[704,128]{1,0:T(8,128)(2,1)S(1)}, bf16[704,128]{1,0:T(8,128)(2,1)S(1)}, u32[]{:S(2)}, u32[]{:S(2)}) %collective-permute-start.32) | collective-permute-done | bytes 180256 | tf_op jit(solution)/shard_map/ppermute | solution.py:87
  92.2 16.0 %forward_product.3 = (f32[1408,128]{1,0:T(8,128)S(1)}, bf16[1408,128]{1,0:T(8,128)(2,1)S(1)}) custom-call(s32[16]{0:T(128)S(1)} %stack.67.place, bf16[704,128]{1,0:T(8,128)(2,1)S(1)} %fusion.6.refs_0_, bf16[704,128]{1,0:T(8,128)(2,1)S(1)} %collective-permute-done.27.refs_1_, bf16[704,128]{1,0:T(8,128)(2,1)S(1)} %collective-permute-done.28.refs_2_, ...), custom_call_target="tpu_custom_call" | custom-call | flops 4060086272 | bytes 31719424 | tf_op jit(solution)/shard_map/forward_product/pallas_call | solution.py:173
  108.3 1.6 collective-permute-start.42
  109.9 8.9 %collective-permute-done.42.arrived = bf16[1408,128]{1,0:T(8,128)(2,1)S(1)} collective-permute-done((bf16[1408,128]{1,0:T(8,128)(2,1)S(1)}, bf16[1408,128]{1,0:T(8,128)(2,1)S(1)}, u32[]{:S(2)}, u32[]{:S(2)}) %collective-permute-start.42) | collective-permute-done | bytes 360480 | tf_op jit(solution)/shard_map/ppermute | solution.py:95
  118.8 15.0 %backward_product.2 = (f32[2,704,128]{2,1,0:T(8,128)S(1)}, f32[2,704,128]{2,1,0:T(8,128)S(1)}, f32[2,704,128]{2,1,0:T(8,128)S(1)}, f32[2,704,128]{2,1,0:T(8,128)...) custom-call(s32[16]{0:T(128)S(1)} %stack.67.place, ...), custom_call_target="tpu_custom_call" | custom-call | flops 4060086272 | bytes 31719424 | tf_op jit(solution)/shard_map/backward_product/pallas_call | solution.py:223
  137.8 1.5 collective-permute-start.50
  140.0 3.0 %collective-permute-done.44 = bf16[704,128]{1,0:T(8,128)(2,1)S(1)} collective-permute-done((bf16[704,128]{1,0:T(8,128)(2,1)S(1)}, bf16[704,128]{1,0:T(8,128)(2,1)S(1)}, u32[]{:S(2)}, u32[]{:S(2)}) %collective-permute-start.44) | collective-permute-done | bytes 180256 | tf_op jit(solution)/shard_map/ppermute | solution.py:87
  143.1 3.9 %collective-permute-start.45 = (bf16[704,128]{1,0:T(8,128)(2,1)S(1)}, bf16[704,128]{1,0:T(8,128)(2,1)S(1)}, u32[]{:S(2)}, u32[]{:S(2)}) collective-permute-start(bf16[704,128]{1,0:T(8,128)(2,1)S(1)} %fusion.3), channel_id=1, source_target_pairs={{0,4},{1,5},{2,6},{3,7},{4,8},{5,9},{6,10},{7,11},{8,12},{9,13},{1... | collective-permute-start | bytes 540680 | tf_op jit(solution)/shard_map/ppermute | solution.py:81
  147.1 2.8 %collective-permute-start.48 = (bf16[704,128]{1,0:T(8,128)(2,1)S(1)}, bf16[704,128]{1,0:T(8,128)(2,1)S(1)}, u32[]{:S(2)}, u32[]{:S(2)}) collective-permute-start(bf16[704,128]{1,0:T(8,128)(2,1)S(1)} %fusion.2), channel_id=1, source_target_pairs={{0,8},{1,9},{2,10},{3,11},{4,12},{5,13},{6,14},{7,15},{8,0},{9,1},... | collective-permute-start | bytes 540680 | tf_op jit(solution)/shard_map/ppermute | solution.py:81
  150.8 5.0 %collective-permute-start.51 = (bf16[704,128]{1,0:T(8,128)(2,1)S(1)}, bf16[704,128]{1,0:T(8,128)(2,1)S(1)}, u32[]{:S(2)}, u32[]{:S(2)}) collective-permute-start(bf16[704,128]{1,0:T(8,128)(2,1)S(1)} %fusion.1), channel_id=1, source_target_pairs={{0,12},{1,13},{2,14},{3,15},{4,0},{5,1},{6,2},{7,3},{8,4},{9,5},{1... | collective-permute-start | bytes 540680 | tf_op jit(solution)/shard_map/ppermute | solution.py:81
  155.8 3.5 %collective-permute-done.48 = bf16[704,128]{1,0:T(8,128)(2,1)S(1)} collective-permute-done((bf16[704,128]{1,0:T(8,128)(2,1)S(1)}, bf16[704,128]{1,0:T(8,128)(2,1)S(1)}, u32[]{:S(2)}, u32[]{:S(2)}) %collective-permute-start.48) | collective-permute-done | bytes 180256 | tf_op jit(solution)/shard_map/ppermute | solution.py:81
  161.5 2.8 %collective-permute-start.65 = (bf16[704,128]{1,0:T(8,128)(2,1)S(1)}, bf16[704,128]{1,0:T(8,128)(2,1)S(1)}, u32[]{:S(2)}, u32[]{:S(2)}) collective-permute-start(bf16[704,128]{1,0:T(8,128)(2,1)S(1)} %get-tuple-element.64.refs_0_), channel_id=1, source_target_pairs={{0,4},{1,5},{2,6},{3,7},{4,8},{5,9},{6,10},{7,11},{8,12},{9,13},{1... | collective-permute-start | bytes 540680 | tf_op jit(solution)/shard_map/ppermute | solution.py:81
  164.3 2.0 collective-permute-start.61
  168.2 3.2 %collective-permute-done.65.refs_12_ = bf16[704,128]{1,0:T(8,128)(2,1)S(1)} collective-permute-done((bf16[704,128]{1,0:T(8,128)(2,1)S(1)}, bf16[704,128]{1,0:T(8,128)(2,1)S(1)}, u32[]{:S(2)}, u32[]{:S(2)}) %collective-permute-start.65) | collective-permute-done | bytes 180256 | tf_op jit(solution)/shard_map/ppermute | solution.py:81
  172.8 4.6 %collective-permute-done.61.refs_8_ = bf16[704,128]{1,0:T(8,128)(2,1)S(1)} collective-permute-done((bf16[704,128]{1,0:T(8,128)(2,1)S(1)}, bf16[704,128]{1,0:T(8,128)(2,1)S(1)}, u32[]{:S(2)}, u32[]{:S(2)}) %collective-permute-start.61) | collective-permute-done | bytes 180256 | tf_op jit(solution)/shard_map/ppermute | solution.py:81
  180.1 4.6 %collective-permute-done.63.refs_10_ = bf16[704,128]{1,0:T(8,128)(2,1)S(1)} collective-permute-done((bf16[704,128]{1,0:T(8,128)(2,1)S(1)}, bf16[704,128]{1,0:T(8,128)(2,1)S(1)}, u32[]{:S(2)}, u32[]{:S(2)}) %collective-permute-start.63) | collective-permute-done | bytes 180256 | tf_op jit(solution)/shard_map/ppermute | solution.py:87
  185.2 3.0 %collective-permute-done.59.refs_6_ = bf16[704,128]{1,0:T(8,128)(2,1)S(1)} collective-permute-done((bf16[704,128]{1,0:T(8,128)(2,1)S(1)}, bf16[704,128]{1,0:T(8,128)(2,1)S(1)}, u32[]{:S(2)}, u32[]{:S(2)}) %collective-permute-start.59) | collective-permute-done | bytes 180256 | tf_op jit(solution)/shard_map/ppermute | solution.py:87
  191.0 1.6 collective-permute-start.69
  192.6 5.1 %collective-permute-done.69.arrived = bf16[704,128]{1,0:T(8,128)(2,1)S(1)} collective-permute-done((bf16[704,128]{1,0:T(8,128)(2,1)S(1)}, bf16[704,128]{1,0:T(8,128)(2,1)S(1)}, u32[]{:S(2)}, u32[]{:S(2)}) %collective-permute-start.69) | collective-permute-done | bytes 180256 | tf_op jit(solution)/shard_map/ppermute | solution.py:95
  197.7 5.9 %backward_product.3 = (f32[2,352,128]{2,1,0:T(8,128)S(1)}, f32[2,352,128]{2,1,0:T(8,128)S(1)}, f32[2,352,128]{2,1,0:T(8,128)S(1)}, f32[2,352,128]{2,1,0:T(8,128)...) custom-call(s32[16]{0:T(128)S(1)} %stack.67.place, ...), custom_call_target="tpu_custom_call" | custom-call | flops 1015021568 | bytes 7929856 | tf_op jit(solution)/shard_map/backward_product/pallas_call | solution.py:223
  205.1 1.5 collective-permute-start.71
  207.3 1.5 collective-permute-start.77
  210.5 3.9 %collective-permute-start.72 = (bf16[352,128]{1,0:T(8,128)(2,1)S(1)}, bf16[352,128]{1,0:T(8,128)(2,1)S(1)}, u32[]{:S(2)}, u32[]{:S(2)}) collective-permute-start(bf16[352,128]{1,0:T(8,128)(2,1)S(1)} %fusion.21), channel_id=1, source_target_pairs={{0,4},{1,5},{2,6},{3,7},{4,8},{5,9},{6,10},{7,11},{8,12},{9,13},{1... | collective-permute-start | bytes 270344 | tf_op jit(solution)/shard_map/ppermute | solution.py:81
  214.4 2.2 %collective-permute-start.75 = (bf16[352,128]{1,0:T(8,128)(2,1)S(1)}, bf16[352,128]{1,0:T(8,128)(2,1)S(1)}, u32[]{:S(2)}, u32[]{:S(2)}) collective-permute-start(bf16[352,128]{1,0:T(8,128)(2,1)S(1)} %fusion.20), channel_id=1, source_target_pairs={{0,8},{1,9},{2,10},{3,11},{4,12},{5,13},{6,14},{7,15},{8,0},{9,1},... | collective-permute-start | bytes 270344 | tf_op jit(solution)/shard_map/ppermute | solution.py:81
  216.7 3.1 %collective-permute-start.78 = (bf16[352,128]{1,0:T(8,128)(2,1)S(1)}, bf16[352,128]{1,0:T(8,128)(2,1)S(1)}, u32[]{:S(2)}, u32[]{:S(2)}) collective-permute-start(bf16[352,128]{1,0:T(8,128)(2,1)S(1)} %fusion.19), channel_id=1, source_target_pairs={{0,12},{1,13},{2,14},{3,15},{4,0},{5,1},{6,2},{7,3},{8,4},{9,5},{1... | collective-permute-start | bytes 270344 | tf_op jit(solution)/shard_map/ppermute | solution.py:81
  219.9 2.5 %collective-permute-done.75 = bf16[352,128]{1,0:T(8,128)(2,1)S(1)} collective-permute-done((bf16[352,128]{1,0:T(8,128)(2,1)S(1)}, bf16[352,128]{1,0:T(8,128)(2,1)S(1)}, u32[]{:S(2)}, u32[]{:S(2)}) %collective-permute-start.75) | collective-permute-done | bytes 90144 | tf_op jit(solution)/shard_map/ppermute | solution.py:81
  (154 shorter events, 44.9 us)
Async XLA Ops:
  1.6 8.5 %collective-permute-start.11 = (bf16[352,128]{1,0:T(8,128)(2,1)S(1)}, bf16[352,128]{1,0:T(8,128)(2,1)S(1)}, u32[]{:S(2)}, u32[]{:S(2)}) collective-permute-start(bf16[352,128]{1,0:T(8,128)(2,1)S(1)} %convert_element_type.267.refs_0_), channel_id=1, source_target_pairs={{0,4},{1,5},{2,6},{3,7},{4,8},{5,9},{6,10},{7,11},{8,12},{9,13},{1... | collective-permute-start | bytes 270344 | tf_op jit(solution)/shard_map/ppermute | solution.py:81
  4.7 8.6 %collective-permute-start.7 = (bf16[352,128]{1,0:T(8,128)(2,1)S(1)}, bf16[352,128]{1,0:T(8,128)(2,1)S(1)}, u32[]{:S(2)}, u32[]{:S(2)}) collective-permute-start(bf16[352,128]{1,0:T(8,128)(2,1)S(1)} %convert_element_type.267.refs_0_), channel_id=1, source_target_pairs={{0,8},{1,9},{2,10},{3,11},{4,12},{5,13},{6,14},{7,15},{8,0},{9,1},... | collective-permute-start | bytes 270344 | tf_op jit(solution)/shard_map/ppermute | solution.py:81
  7.2 6.2 %collective-permute-start.3 = (bf16[352,128]{1,0:T(8,128)(2,1)S(1)}, bf16[352,128]{1,0:T(8,128)(2,1)S(1)}, u32[]{:S(2)}, u32[]{:S(2)}) collective-permute-start(bf16[352,128]{1,0:T(8,128)(2,1)S(1)} %convert_element_type.267.refs_0_), channel_id=1, source_target_pairs={{0,12},{1,13},{2,14},{3,15},{4,0},{5,1},{6,2},{7,3},{8,4},{9,5},{1... | collective-permute-start | bytes 270344 | tf_op jit(solution)/shard_map/ppermute | solution.py:81
  8.6 6.4 %collective-permute-start.1 = (bf16[352,128]{1,0:T(8,128)(2,1)S(1)}, bf16[352,128]{1,0:T(8,128)(2,1)S(1)}, u32[]{:S(2)}, u32[]{:S(2)}) collective-permute-start(bf16[352,128]{1,0:T(8,128)(2,1)S(1)} %convert_element_type.267.refs_0_), channel_id=1, source_target_pairs={{0,2},{1,3},{2,0},{3,1},{4,6},{5,7},{6,4},{7,5},{8,10},{9,11},{10,... | collective-permute-start | bytes 270344 | tf_op jit(solution)/shard_map/ppermute | solution.py:87
  27.6 6.7 %collective-permute-start.15 = (bf16[704,128]{1,0:T(8,128)(2,1)S(1)}, bf16[704,128]{1,0:T(8,128)(2,1)S(1)}, u32[]{:S(2)}, u32[]{:S(2)}) collective-permute-start(bf16[704,128]{1,0:T(8,128)(2,1)S(1)} %get-tuple-element.34), channel_id=1, source_target_pairs={{0,16},{16,0},{1,17},{17,1},{2,18},{18,2},{3,19},{19,3},{4,20},{20... | collective-permute-start | bytes 540680 | tf_op jit(solution)/shard_map/ppermute | solution.py:95
  38.9 7.5 %collective-permute-start.17 = (bf16[704,128]{1,0:T(8,128)(2,1)S(1)}, bf16[704,128]{1,0:T(8,128)(2,1)S(1)}, u32[]{:S(2)}, u32[]{:S(2)}) collective-permute-start(bf16[704,128]{1,0:T(8,128)(2,1)S(1)} %fusion.10), channel_id=1, source_target_pairs={{0,2},{1,3},{2,0},{3,1},{4,6},{5,7},{6,4},{7,5},{8,10},{9,11},{10,... | collective-permute-start | bytes 540680 | tf_op jit(solution)/shard_map/ppermute | solution.py:87
  40.5 9.7 %collective-permute-start.20 = (bf16[704,128]{1,0:T(8,128)(2,1)S(1)}, bf16[704,128]{1,0:T(8,128)(2,1)S(1)}, u32[]{:S(2)}, u32[]{:S(2)}) collective-permute-start(bf16[704,128]{1,0:T(8,128)(2,1)S(1)} %fusion.11), channel_id=1, source_target_pairs={{0,2},{1,3},{2,0},{3,1},{4,6},{5,7},{6,4},{7,5},{8,10},{9,11},{10,... | collective-permute-start | bytes 540680 | tf_op jit(solution)/shard_map/ppermute | solution.py:87
  41.2 12.9 %collective-permute-start.23 = (bf16[704,128]{1,0:T(8,128)(2,1)S(1)}, bf16[704,128]{1,0:T(8,128)(2,1)S(1)}, u32[]{:S(2)}, u32[]{:S(2)}) collective-permute-start(bf16[704,128]{1,0:T(8,128)(2,1)S(1)} %fusion.12), channel_id=1, source_target_pairs={{0,2},{1,3},{2,0},{3,1},{4,6},{5,7},{6,4},{7,5},{8,10},{9,11},{10,... | collective-permute-start | bytes 540680 | tf_op jit(solution)/shard_map/ppermute | solution.py:87
  42.8 15.0 %collective-permute-start.26 = (bf16[704,128]{1,0:T(8,128)(2,1)S(1)}, bf16[704,128]{1,0:T(8,128)(2,1)S(1)}, u32[]{:S(2)}, u32[]{:S(2)}) collective-permute-start(bf16[704,128]{1,0:T(8,128)(2,1)S(1)} %fusion.13), channel_id=1, source_target_pairs={{0,2},{1,3},{2,0},{3,1},{4,6},{5,7},{6,4},{7,5},{8,10},{9,11},{10,... | collective-permute-start | bytes 540680 | tf_op jit(solution)/shard_map/ppermute | solution.py:87
  46.5 11.4 %collective-permute-start.18 = (bf16[704,128]{1,0:T(8,128)(2,1)S(1)}, bf16[704,128]{1,0:T(8,128)(2,1)S(1)}, u32[]{:S(2)}, u32[]{:S(2)}) collective-permute-start(bf16[704,128]{1,0:T(8,128)(2,1)S(1)} %fusion.9), channel_id=1, source_target_pairs={{0,4},{1,5},{2,6},{3,7},{4,8},{5,9},{6,10},{7,11},{8,12},{9,13},{1... | collective-permute-start | bytes 540680 | tf_op jit(solution)/shard_map/ppermute | solution.py:81
  50.3 11.3 %collective-permute-start.21 = (bf16[704,128]{1,0:T(8,128)(2,1)S(1)}, bf16[704,128]{1,0:T(8,128)(2,1)S(1)}, u32[]{:S(2)}, u32[]{:S(2)}) collective-permute-start(bf16[704,128]{1,0:T(8,128)(2,1)S(1)} %fusion.8), channel_id=1, source_target_pairs={{0,8},{1,9},{2,10},{3,11},{4,12},{5,13},{6,14},{7,15},{8,0},{9,1},... | collective-permute-start | bytes 540680 | tf_op jit(solution)/shard_map/ppermute | solution.py:81
  54.2 9.0 %collective-permute-start.24 = (bf16[704,128]{1,0:T(8,128)(2,1)S(1)}, bf16[704,128]{1,0:T(8,128)(2,1)S(1)}, u32[]{:S(2)}, u32[]{:S(2)}) collective-permute-start(bf16[704,128]{1,0:T(8,128)(2,1)S(1)} %fusion.7), channel_id=1, source_target_pairs={{0,12},{1,13},{2,14},{3,15},{4,0},{5,1},{6,2},{7,3},{8,4},{9,5},{1... | collective-permute-start | bytes 540680 | tf_op jit(solution)/shard_map/ppermute | solution.py:81
  63.3 10.1 %collective-permute-start.38 = (bf16[704,128]{1,0:T(8,128)(2,1)S(1)}, bf16[704,128]{1,0:T(8,128)(2,1)S(1)}, u32[]{:S(2)}, u32[]{:S(2)}) collective-permute-start(bf16[704,128]{1,0:T(8,128)(2,1)S(1)} %fusion.6.refs_0_), channel_id=1, source_target_pairs={{0,4},{1,5},{2,6},{3,7},{4,8},{5,9},{6,10},{7,11},{8,12},{9,13},{1... | collective-permute-start | bytes 540680 | tf_op jit(solution)/shard_map/ppermute | solution.py:81
  66.2 13.8 %collective-permute-start.34 = (bf16[704,128]{1,0:T(8,128)(2,1)S(1)}, bf16[704,128]{1,0:T(8,128)(2,1)S(1)}, u32[]{:S(2)}, u32[]{:S(2)}) collective-permute-start(bf16[704,128]{1,0:T(8,128)(2,1)S(1)} %fusion.6.refs_0_), channel_id=1, source_target_pairs={{0,8},{1,9},{2,10},{3,11},{4,12},{5,13},{6,14},{7,15},{8,0},{9,1},... | collective-permute-start | bytes 540680 | tf_op jit(solution)/shard_map/ppermute | solution.py:81
  68.5 11.5 %collective-permute-start.30 = (bf16[704,128]{1,0:T(8,128)(2,1)S(1)}, bf16[704,128]{1,0:T(8,128)(2,1)S(1)}, u32[]{:S(2)}, u32[]{:S(2)}) collective-permute-start(bf16[704,128]{1,0:T(8,128)(2,1)S(1)} %fusion.6.refs_0_), channel_id=1, source_target_pairs={{0,12},{1,13},{2,14},{3,15},{4,0},{5,1},{6,2},{7,3},{8,4},{9,5},{1... | collective-permute-start | bytes 540680 | tf_op jit(solution)/shard_map/ppermute | solution.py:81
  68.7 12.8 %collective-permute-start.28 = (bf16[704,128]{1,0:T(8,128)(2,1)S(1)}, bf16[704,128]{1,0:T(8,128)(2,1)S(1)}, u32[]{:S(2)}, u32[]{:S(2)}) collective-permute-start(bf16[704,128]{1,0:T(8,128)(2,1)S(1)} %fusion.6.refs_0_), channel_id=1, source_target_pairs={{0,2},{1,3},{2,0},{3,1},{4,6},{5,7},{6,4},{7,5},{8,10},{9,11},{10,... | collective-permute-start | bytes 540680 | tf_op jit(solution)/shard_map/ppermute | solution.py:87
  70.1 11.5 %collective-permute-start.27 = (bf16[704,128]{1,0:T(8,128)(2,1)S(1)}, bf16[704,128]{1,0:T(8,128)(2,1)S(1)}, u32[]{:S(2)}, u32[]{:S(2)}) collective-permute-start(bf16[704,128]{1,0:T(8,128)(2,1)S(1)} %fusion.6.refs_0_), channel_id=1, source_target_pairs={{0,1},{1,0},{2,3},{3,2},{4,5},{5,4},{6,7},{7,6},{8,9},{9,8},{10,11... | collective-permute-start | bytes 540680 | tf_op jit(solution)/shard_map/ppermute | solution.py:91
  73.4 8.8 %collective-permute-start.40 = (bf16[704,128]{1,0:T(8,128)(2,1)S(1)}, bf16[704,128]{1,0:T(8,128)(2,1)S(1)}, u32[]{:S(2)}, u32[]{:S(2)}) collective-permute-start(bf16[704,128]{1,0:T(8,128)(2,1)S(1)} %collective-permute-done.38.refs_12_), channel_id=1, source_target_pairs={{0,2},{1,3},{2,0},{3,1},{4,6},{5,7},{6,4},{7,5},{8,10},{9,11},{10,... | collective-permute-start | bytes 540680 | tf_op jit(solution)/shard_map/ppermute | solution.py:87
  80.0 7.3 %collective-permute-start.36 = (bf16[704,128]{1,0:T(8,128)(2,1)S(1)}, bf16[704,128]{1,0:T(8,128)(2,1)S(1)}, u32[]{:S(2)}, u32[]{:S(2)}) collective-permute-start(bf16[704,128]{1,0:T(8,128)(2,1)S(1)} %collective-permute-done.34.refs_8_), channel_id=1, source_target_pairs={{0,2},{1,3},{2,0},{3,1},{4,6},{5,7},{6,4},{7,5},{8,10},{9,11},{10,... | collective-permute-start | bytes 540680 | tf_op jit(solution)/shard_map/ppermute | solution.py:87
  81.4 5.9 %collective-permute-start.35 = (bf16[704,128]{1,0:T(8,128)(2,1)S(1)}, bf16[704,128]{1,0:T(8,128)(2,1)S(1)}, u32[]{:S(2)}, u32[]{:S(2)}) collective-permute-start(bf16[704,128]{1,0:T(8,128)(2,1)S(1)} %collective-permute-done.34.refs_8_), channel_id=1, source_target_pairs={{0,1},{1,0},{2,3},{3,2},{4,5},{5,4},{6,7},{7,6},{8,9},{9,8},{10,11... | collective-permute-start | bytes 540680 | tf_op jit(solution)/shard_map/ppermute | solution.py:91
  81.7 9.2 %collective-permute-start.32 = (bf16[704,128]{1,0:T(8,128)(2,1)S(1)}, bf16[704,128]{1,0:T(8,128)(2,1)S(1)}, u32[]{:S(2)}, u32[]{:S(2)}) collective-permute-start(bf16[704,128]{1,0:T(8,128)(2,1)S(1)} %collective-permute-done.30.refs_4_), channel_id=1, source_target_pairs={{0,2},{1,3},{2,0},{3,1},{4,6},{5,7},{6,4},{7,5},{8,10},{9,11},{10,... | collective-permute-start | bytes 540680 | tf_op jit(solution)/shard_map/ppermute | solution.py:87
  82.3 8.6 %collective-permute-start.31 = (bf16[704,128]{1,0:T(8,128)(2,1)S(1)}, bf16[704,128]{1,0:T(8,128)(2,1)S(1)}, u32[]{:S(2)}, u32[]{:S(2)}) collective-permute-start(bf16[704,128]{1,0:T(8,128)(2,1)S(1)} %collective-permute-done.30.refs_4_), channel_id=1, source_target_pairs={{0,1},{1,0},{2,3},{3,2},{4,5},{5,4},{6,7},{7,6},{8,9},{9,8},{10,11... | collective-permute-start | bytes 540680 | tf_op jit(solution)/shard_map/ppermute | solution.py:91
  82.3 8.6 %collective-permute-start.29 = (bf16[704,128]{1,0:T(8,128)(2,1)S(1)}, bf16[704,128]{1,0:T(8,128)(2,1)S(1)}, u32[]{:S(2)}, u32[]{:S(2)}) collective-permute-start(bf16[704,128]{1,0:T(8,128)(2,1)S(1)} %collective-permute-done.28.refs_2_), channel_id=1, source_target_pairs={{0,1},{1,0},{2,3},{3,2},{4,5},{5,4},{6,7},{7,6},{8,9},{9,8},{10,11... | collective-permute-start | bytes 540680 | tf_op jit(solution)/shard_map/ppermute | solution.py:91
  108.3 10.5 %collective-permute-start.42 = (bf16[1408,128]{1,0:T(8,128)(2,1)S(1)}, bf16[1408,128]{1,0:T(8,128)(2,1)S(1)}, u32[]{:S(2)}, u32[]{:S(2)}) collective-permute-start(bf16[1408,128]{1,0:T(8,128)(2,1)S(1)} %get-tuple-element.44), channel_id=1, source_target_pairs={{0,16},{16,0},{1,17},{17,1},{2,18},{18,2},{3,19},{19,3},{4,20},{20... | collective-permute-start | bytes 1081352 | tf_op jit(solution)/shard_map/ppermute | solution.py:95
  135.6 7.5 %collective-permute-start.44 = (bf16[704,128]{1,0:T(8,128)(2,1)S(1)}, bf16[704,128]{1,0:T(8,128)(2,1)S(1)}, u32[]{:S(2)}, u32[]{:S(2)}) collective-permute-start(bf16[704,128]{1,0:T(8,128)(2,1)S(1)} %fusion.14), channel_id=1, source_target_pairs={{0,2},{1,3},{2,0},{3,1},{4,6},{5,7},{6,4},{7,5},{8,10},{9,11},{10,... | collective-permute-start | bytes 540680 | tf_op jit(solution)/shard_map/ppermute | solution.py:87
  137.1 9.9 %collective-permute-start.47 = (bf16[704,128]{1,0:T(8,128)(2,1)S(1)}, bf16[704,128]{1,0:T(8,128)(2,1)S(1)}, u32[]{:S(2)}, u32[]{:S(2)}) collective-permute-start(bf16[704,128]{1,0:T(8,128)(2,1)S(1)} %fusion.15), channel_id=1, source_target_pairs={{0,2},{1,3},{2,0},{3,1},{4,6},{5,7},{6,4},{7,5},{8,10},{9,11},{10,... | collective-permute-start | bytes 540680 | tf_op jit(solution)/shard_map/ppermute | solution.py:87
  137.8 12.9 %collective-permute-start.50 = (bf16[704,128]{1,0:T(8,128)(2,1)S(1)}, bf16[704,128]{1,0:T(8,128)(2,1)S(1)}, u32[]{:S(2)}, u32[]{:S(2)}) collective-permute-start(bf16[704,128]{1,0:T(8,128)(2,1)S(1)} %fusion.16), channel_id=1, source_target_pairs={{0,2},{1,3},{2,0},{3,1},{4,6},{5,7},{6,4},{7,5},{8,10},{9,11},{10,... | collective-permute-start | bytes 540680 | tf_op jit(solution)/shard_map/ppermute | solution.py:87
  139.4 16.4 %collective-permute-start.53 = (bf16[704,128]{1,0:T(8,128)(2,1)S(1)}, bf16[704,128]{1,0:T(8,128)(2,1)S(1)}, u32[]{:S(2)}, u32[]{:S(2)}) collective-permute-start(bf16[704,128]{1,0:T(8,128)(2,1)S(1)} %fusion.17), channel_id=1, source_target_pairs={{0,2},{1,3},{2,0},{3,1},{4,6},{5,7},{6,4},{7,5},{8,10},{9,11},{10,... | collective-permute-start | bytes 540680 | tf_op jit(solution)/shard_map/ppermute | solution.py:87
  143.1 12.7 %collective-permute-start.45 = (bf16[704,128]{1,0:T(8,128)(2,1)S(1)}, bf16[704,128]{1,0:T(8,128)(2,1)S(1)}, u32[]{:S(2)}, u32[]{:S(2)}) collective-permute-start(bf16[704,128]{1,0:T(8,128)(2,1)S(1)} %fusion.3), channel_id=1, source_target_pairs={{0,4},{1,5},{2,6},{3,7},{4,8},{5,9},{6,10},{7,11},{8,12},{9,13},{1... | collective-permute-start | bytes 540680 | tf_op jit(solution)/shard_map/ppermute | solution.py:81
  147.1 12.3 %collective-permute-start.48 = (bf16[704,128]{1,0:T(8,128)(2,1)S(1)}, bf16[704,128]{1,0:T(8,128)(2,1)S(1)}, u32[]{:S(2)}, u32[]{:S(2)}) collective-permute-start(bf16[704,128]{1,0:T(8,128)(2,1)S(1)} %fusion.2), channel_id=1, source_target_pairs={{0,8},{1,9},{2,10},{3,11},{4,12},{5,13},{6,14},{7,15},{8,0},{9,1},... | collective-permute-start | bytes 540680 | tf_op jit(solution)/shard_map/ppermute | solution.py:81
  150.8 9.9 %collective-permute-start.51 = (bf16[704,128]{1,0:T(8,128)(2,1)S(1)}, bf16[704,128]{1,0:T(8,128)(2,1)S(1)}, u32[]{:S(2)}, u32[]{:S(2)}) collective-permute-start(bf16[704,128]{1,0:T(8,128)(2,1)S(1)} %fusion.1), channel_id=1, source_target_pairs={{0,12},{1,13},{2,14},{3,15},{4,0},{5,1},{6,2},{7,3},{8,4},{9,5},{1... | collective-permute-start | bytes 540680 | tf_op jit(solution)/shard_map/ppermute | solution.py:81
  161.5 9.8 %collective-permute-start.65 = (bf16[704,128]{1,0:T(8,128)(2,1)S(1)}, bf16[704,128]{1,0:T(8,128)(2,1)S(1)}, u32[]{:S(2)}, u32[]{:S(2)}) collective-permute-start(bf16[704,128]{1,0:T(8,128)(2,1)S(1)} %get-tuple-element.64.refs_0_), channel_id=1, source_target_pairs={{0,4},{1,5},{2,6},{3,7},{4,8},{5,9},{6,10},{7,11},{8,12},{9,13},{1... | collective-permute-start | bytes 540680 | tf_op jit(solution)/shard_map/ppermute | solution.py:81
  164.3 13.0 %collective-permute-start.61 = (bf16[704,128]{1,0:T(8,128)(2,1)S(1)}, bf16[704,128]{1,0:T(8,128)(2,1)S(1)}, u32[]{:S(2)}, u32[]{:S(2)}) collective-permute-start(bf16[704,128]{1,0:T(8,128)(2,1)S(1)} %get-tuple-element.64.refs_0_), channel_id=1, source_target_pairs={{0,8},{1,9},{2,10},{3,11},{4,12},{5,13},{6,14},{7,15},{8,0},{9,1},... | collective-permute-start | bytes 540680 | tf_op jit(solution)/shard_map/ppermute | solution.py:81
  166.3 11.0 %collective-permute-start.57 = (bf16[704,128]{1,0:T(8,128)(2,1)S(1)}, bf16[704,128]{1,0:T(8,128)(2,1)S(1)}, u32[]{:S(2)}, u32[]{:S(2)}) collective-permute-start(bf16[704,128]{1,0:T(8,128)(2,1)S(1)} %get-tuple-element.64.refs_0_), channel_id=1, source_target_pairs={{0,12},{1,13},{2,14},{3,15},{4,0},{5,1},{6,2},{7,3},{8,4},{9,5},{1... | collective-permute-start | bytes 540680 | tf_op jit(solution)/shard_map/ppermute | solution.py:81
  166.7 12.1 %collective-permute-start.55 = (bf16[704,128]{1,0:T(8,128)(2,1)S(1)}, bf16[704,128]{1,0:T(8,128)(2,1)S(1)}, u32[]{:S(2)}, u32[]{:S(2)}) collective-permute-start(bf16[704,128]{1,0:T(8,128)(2,1)S(1)} %get-tuple-element.64.refs_0_), channel_id=1, source_target_pairs={{0,2},{1,3},{2,0},{3,1},{4,6},{5,7},{6,4},{7,5},{8,10},{9,11},{10,... | collective-permute-start | bytes 540680 | tf_op jit(solution)/shard_map/ppermute | solution.py:87
  168.1 10.9 %collective-permute-start.54 = (bf16[704,128]{1,0:T(8,128)(2,1)S(1)}, bf16[704,128]{1,0:T(8,128)(2,1)S(1)}, u32[]{:S(2)}, u32[]{:S(2)}) collective-permute-start(bf16[704,128]{1,0:T(8,128)(2,1)S(1)} %get-tuple-element.64.refs_0_), channel_id=1, source_target_pairs={{0,1},{1,0},{2,3},{3,2},{4,5},{5,4},{6,7},{7,6},{8,9},{9,8},{10,11... | collective-permute-start | bytes 540680 | tf_op jit(solution)/shard_map/ppermute | solution.py:91
  171.3 8.3 %collective-permute-start.67 = (bf16[704,128]{1,0:T(8,128)(2,1)S(1)}, bf16[704,128]{1,0:T(8,128)(2,1)S(1)}, u32[]{:S(2)}, u32[]{:S(2)}) collective-permute-start(bf16[704,128]{1,0:T(8,128)(2,1)S(1)} %collective-permute-done.65.refs_12_), channel_id=1, source_target_pairs={{0,2},{1,3},{2,0},{3,1},{4,6},{5,7},{6,4},{7,5},{8,10},{9,11},{10,... | collective-permute-start | bytes 540680 | tf_op jit(solution)/shard_map/ppermute | solution.py:87
  177.3 7.3 %collective-permute-start.63 = (bf16[704,128]{1,0:T(8,128)(2,1)S(1)}, bf16[704,128]{1,0:T(8,128)(2,1)S(1)}, u32[]{:S(2)}, u32[]{:S(2)}) collective-permute-start(bf16[704,128]{1,0:T(8,128)(2,1)S(1)} %collective-permute-done.61.refs_8_), channel_id=1, source_target_pairs={{0,2},{1,3},{2,0},{3,1},{4,6},{5,7},{6,4},{7,5},{8,10},{9,11},{10,... | collective-permute-start | bytes 540680 | tf_op jit(solution)/shard_map/ppermute | solution.py:87
  178.8 5.9 %collective-permute-start.62 = (bf16[704,128]{1,0:T(8,128)(2,1)S(1)}, bf16[704,128]{1,0:T(8,128)(2,1)S(1)}, u32[]{:S(2)}, u32[]{:S(2)}) collective-permute-start(bf16[704,128]{1,0:T(8,128)(2,1)S(1)} %collective-permute-done.61.refs_8_), channel_id=1, source_target_pairs={{0,1},{1,0},{2,3},{3,2},{4,5},{5,4},{6,7},{7,6},{8,9},{9,8},{10,11... | collective-permute-start | bytes 540680 | tf_op jit(solution)/shard_map/ppermute | solution.py:91
  179.0 9.1 %collective-permute-start.59 = (bf16[704,128]{1,0:T(8,128)(2,1)S(1)}, bf16[704,128]{1,0:T(8,128)(2,1)S(1)}, u32[]{:S(2)}, u32[]{:S(2)}) collective-permute-start(bf16[704,128]{1,0:T(8,128)(2,1)S(1)} %collective-permute-done.57.refs_4_), channel_id=1, source_target_pairs={{0,2},{1,3},{2,0},{3,1},{4,6},{5,7},{6,4},{7,5},{8,10},{9,11},{10,... | collective-permute-start | bytes 540680 | tf_op jit(solution)/shard_map/ppermute | solution.py:87
  179.6 8.6 %collective-permute-start.58 = (bf16[704,128]{1,0:T(8,128)(2,1)S(1)}, bf16[704,128]{1,0:T(8,128)(2,1)S(1)}, u32[]{:S(2)}, u32[]{:S(2)}) collective-permute-start(bf16[704,128]{1,0:T(8,128)(2,1)S(1)} %collective-permute-done.57.refs_4_), channel_id=1, source_target_pairs={{0,1},{1,0},{2,3},{3,2},{4,5},{5,4},{6,7},{7,6},{8,9},{9,8},{10,11... | collective-permute-start | bytes 540680 | tf_op jit(solution)/shard_map/ppermute | solution.py:91
  179.6 8.6 %collective-permute-start.56 = (bf16[704,128]{1,0:T(8,128)(2,1)S(1)}, bf16[704,128]{1,0:T(8,128)(2,1)S(1)}, u32[]{:S(2)}, u32[]{:S(2)}) collective-permute-start(bf16[704,128]{1,0:T(8,128)(2,1)S(1)} %collective-permute-done.55.refs_2_), channel_id=1, source_target_pairs={{0,1},{1,0},{2,3},{3,2},{4,5},{5,4},{6,7},{7,6},{8,9},{9,8},{10,11... | collective-permute-start | bytes 540680 | tf_op jit(solution)/shard_map/ppermute | solution.py:91
  191.0 6.7 %collective-permute-start.69 = (bf16[704,128]{1,0:T(8,128)(2,1)S(1)}, bf16[704,128]{1,0:T(8,128)(2,1)S(1)}, u32[]{:S(2)}, u32[]{:S(2)}) collective-permute-start(bf16[704,128]{1,0:T(8,128)(2,1)S(1)} %get-tuple-element.54), channel_id=1, source_target_pairs={{0,16},{16,0},{1,17},{17,1},{2,18},{18,2},{3,19},{19,3},{4,20},{20... | collective-permute-start | bytes 540680 | tf_op jit(solution)/shard_map/ppermute | solution.py:95
  206.7 7.7 %collective-permute-start.74 = (bf16[352,128]{1,0:T(8,128)(2,1)S(1)}, bf16[352,128]{1,0:T(8,128)(2,1)S(1)}, u32[]{:S(2)}, u32[]{:S(2)}) collective-permute-start(bf16[352,128]{1,0:T(8,128)(2,1)S(1)} %fusion.23), channel_id=1, source_target_pairs={{0,2},{1,3},{2,0},{3,1},{4,6},{5,7},{6,4},{7,5},{8,10},{9,11},{10,... | collective-permute-start | bytes 270344 | tf_op jit(solution)/shard_map/ppermute | solution.py:87
  207.3 9.4 %collective-permute-start.77 = (bf16[352,128]{1,0:T(8,128)(2,1)S(1)}, bf16[352,128]{1,0:T(8,128)(2,1)S(1)}, u32[]{:S(2)}, u32[]{:S(2)}) collective-permute-start(bf16[352,128]{1,0:T(8,128)(2,1)S(1)} %fusion.24), channel_id=1, source_target_pairs={{0,2},{1,3},{2,0},{3,1},{4,6},{5,7},{6,4},{7,5},{8,10},{9,11},{10,... | collective-permute-start | bytes 270344 | tf_op jit(solution)/shard_map/ppermute | solution.py:87
  208.9 11.0 %collective-permute-start.80 = (bf16[352,128]{1,0:T(8,128)(2,1)S(1)}, bf16[352,128]{1,0:T(8,128)(2,1)S(1)}, u32[]{:S(2)}, u32[]{:S(2)}) collective-permute-start(bf16[352,128]{1,0:T(8,128)(2,1)S(1)} %fusion.25), channel_id=1, source_target_pairs={{0,2},{1,3},{2,0},{3,1},{4,6},{5,7},{6,4},{7,5},{8,10},{9,11},{10,... | collective-permute-start | bytes 270344 | tf_op jit(solution)/shard_map/ppermute | solution.py:87
  210.5 9.4 %collective-permute-start.72 = (bf16[352,128]{1,0:T(8,128)(2,1)S(1)}, bf16[352,128]{1,0:T(8,128)(2,1)S(1)}, u32[]{:S(2)}, u32[]{:S(2)}) collective-permute-start(bf16[352,128]{1,0:T(8,128)(2,1)S(1)} %fusion.21), channel_id=1, source_target_pairs={{0,4},{1,5},{2,6},{3,7},{4,8},{5,9},{6,10},{7,11},{8,12},{9,13},{1... | collective-permute-start | bytes 270344 | tf_op jit(solution)/shard_map/ppermute | solution.py:81
  214.4 7.9 %collective-permute-start.75 = (bf16[352,128]{1,0:T(8,128)(2,1)S(1)}, bf16[352,128]{1,0:T(8,128)(2,1)S(1)}, u32[]{:S(2)}, u32[]{:S(2)}) collective-permute-start(bf16[352,128]{1,0:T(8,128)(2,1)S(1)} %fusion.20), channel_id=1, source_target_pairs={{0,8},{1,9},{2,10},{3,11},{4,12},{5,13},{6,14},{7,15},{8,0},{9,1},... | collective-permute-start | bytes 270344 | tf_op jit(solution)/shard_map/ppermute | solution.py:81
  (36 other events, 239.6 us)

commit v2 on v1

--- a/solution.py
+++ b/solution.py
@@ -15,7 +15,7 @@
 HIGHEST_PRECISION = lax.Precision.HIGHEST
 VMEM = pl.BlockSpec(memory_space=pltpu.VMEM)
 SMEM = pl.BlockSpec(memory_space=pltpu.SMEM)
-VMEM_LIMIT = 48 * 1024 * 1024
+VMEM_LIMIT = 14 * 1024 * 1024
 
 
 def transposed_product(matrix, vector):
@@ -104,9 +104,13 @@
     return pieces
 
 
+def scatter_order(nz):
+    return sorted(range(nz), key=lambda k: -min(k, nz - k))
+
+
 def scatter_sum(keep, send, nz):
     total = None
-    for k in list(range(1, nz)) + [0]:
+    for k in scatter_order(nz):
         arrived = c_swap(send[k], nz)
         near = keep[k][0].astype(F32) + arrived[0].astype(F32)
         far = keep[k][1].astype(F32) + arrived[1].astype(F32)
@@ -148,97 +152,119 @@
                 ].astype(out.dtype)
 
 
-def forward_kernel(count, place, *refs):
-    pieces, (matrix, out, out_b, whole) = refs[:count], refs[count:]
-    step = pl.program_id(0)
-    depth = matrix.shape[1]
-
-    @pl.when(step == 0)
-    def _():
-        assemble(place, pieces, whole)
-        out[...] = jnp.zeros_like(out)
-
-    cols = whole[pl.ds(pl.multiple_of(step * depth, depth), depth), :]
-    out[...] += jnp.dot(matrix[...], cols, preferred_element_type=F32)
-
-    @pl.when(step == pl.num_programs(0) - 1)
-    def _():
-        out_b[...] = out[...].astype(BF16)
-
-
-def forward_product(place, pieces, matrix, depth):
-    rows, width = matrix.shape
-    n = pieces[0].shape[1]
-    whole_spec = lambda shape: pl.BlockSpec(shape, lambda i, *_: (0,) * len(shape))
+def column_step(width):
+    for step in (1408, 1024, 704, 512, 256):
+        if width % step == 0 and step % 128 == 0:
+            return step
+    return width
+
+
+def forward_kernel(k, fresh, last, place, *refs):
+    pieces, (matrix, acc, out, *outs_b), (cols,) = refs[: NX * NC], refs[NX * NC : -1], refs[-1:]
+    rows = pieces[0].shape[0]
+    depth = NX * NC * rows
+    for i, piece in enumerate(pieces):
+        at = place[k * NX * NC + i] % (NX * NC)
+        cols[pl.ds(pl.multiple_of(at * rows, rows), rows), :] = piece[...]
+    total = None if fresh else acc[...]
+    step = column_step(depth)
+    for j in range(depth // step):
+        product = jnp.dot(
+            matrix[:, j * step : (j + 1) * step],
+            cols[j * step : (j + 1) * step, :],
+            preferred_element_type=F32,
+        )
+        total = product if total is None else total + product
+    out[...] = total
+    if last:
+        outs_b[0][...] = total.astype(BF16)
+
+
+def forward_product(place, pieces, blocks, nz):
+    rows = blocks[0].shape[0]
+    part, n = pieces[0].shape
+    group = NX * NC
+    acc = jnp.zeros((8, n), F32)
+    order = [0, 1, nz - 1] + list(range(2, nz - 1)) if nz > 2 else list(range(nz))
+    for i, k in enumerate(order):
+        fresh, last = i == 0, i == nz - 1
+        outs = pl.pallas_call(
+            functools.partial(forward_kernel, k, fresh, last),
+            out_shape=[jax.ShapeDtypeStruct((rows, n), F32)]
+            + [jax.ShapeDtypeStruct((rows, n), BF16)] * last,
+            in_specs=[SMEM] + [VMEM] * (group + 2),
+            out_specs=[VMEM] * (1 + last),
+            scratch_shapes=[pltpu.VMEM((group * part, n), BF16)],
+            compiler_params=pltpu.CompilerParams(vmem_limit_bytes=VMEM_LIMIT),
+            cost_estimate=pl.CostEstimate(
+                flops=2 * rows * group * part * n,
+                bytes_accessed=2 * rows * group * part,
+                transcendentals=0,
+            ),
+            name="forward_product",
+        )(place, *pieces[k * group : (k + 1) * group], blocks[k], acc)
+        acc = outs[0]
+    return outs
+
+
+def backward_kernel(k, place, vector, matrix, keep, send, whole):
+    part = keep.shape[1]
+    depth = NX * NC * part
+    step = column_step(depth)
+    for j in range(depth // step):
+        whole[j * step : (j + 1) * step, :] = jnp.dot(
+            vector[...], matrix[:, j * step : (j + 1) * step], preferred_element_type=F32
+        ).T
+    for xr in range(NX):
+        for cr, out in ((0, keep), (1, send)):
+            at = place[(k * NX + xr) * NC + cr] % (NX * NC)
+            out[xr] = whole[pl.ds(pl.multiple_of(at * part, part), part), :].astype(out.dtype)
+
+
+def backward_product(place, vector, blocks, nz):
+    rows, depth = blocks[0].shape
+    n = vector.shape[0]
+    group = NX * NC
+    part = depth // group
+    keep, send = [None] * nz, [None] * nz
+    for k in scatter_order(nz):
+        keep[k], send[k] = pl.pallas_call(
+            functools.partial(backward_kernel, k),
+            out_shape=[
+                jax.ShapeDtypeStruct((NX, part, n), F32),
+                jax.ShapeDtypeStruct((NX, part, n), BF16),
+            ],
+            in_specs=[SMEM, VMEM, VMEM],
+            out_specs=[VMEM, VMEM],
+            scratch_shapes=[pltpu.VMEM((group * part, n), F32)],
+            compiler_params=pltpu.CompilerParams(vmem_limit_bytes=VMEM_LIMIT),
+            cost_estimate=pl.CostEstimate(
+                flops=2 * rows * group * part * n,
+                bytes_accessed=2 * rows * group * part,
+                transcendentals=0,
+            ),
+            name="backward_product",
+        )(place, vector, blocks[k])
+    return keep, send
+
+
+def turn_kernel(subtract, own, arrived, base, vector):
+    total = own[...] + arrived[...].astype(F32)
+    if subtract:
+        total = base[...] - total
+    vector[...] = total.T.astype(BF16)
+
+
+def turn(own, arrived, base=None):
+    rows, n = own.shape
+    subtract = base is not None
     return pl.pallas_call(
-        functools.partial(forward_kernel, len(pieces)),
-        out_shape=(
-            jax.ShapeDtypeStruct((rows, n), F32),
-            jax.ShapeDtypeStruct((rows, n), BF16),
-        ),
-        grid_spec=pltpu.PrefetchScalarGridSpec(
-            num_scalar_prefetch=1,
-            grid=(width // depth,),
-            in_specs=[whole_spec(p.shape) for p in pieces]
-            + [pl.BlockSpec((rows, depth), lambda i, *_: (0, i))],
-            out_specs=(whole_spec((rows, n)), whole_spec((rows, n))),
-            scratch_shapes=[pltpu.VMEM((width, n), BF16)],
-        ),
-        compiler_params=pltpu.CompilerParams(vmem_limit_bytes=VMEM_LIMIT),
-        cost_estimate=pl.CostEstimate(
-            flops=2 * rows * width * n, bytes_accessed=2 * rows * width, transcendentals=0
-        ),
-        name="forward_product",
-    )(place, *pieces, matrix)
-
-
-def backward_kernel(nz, subtract, place, own, arrived, base, matrix, *refs):
-    keep, send, (vector, whole) = refs[:nz], refs[nz : 2 * nz], refs[2 * nz :]
-    step = pl.program_id(0)
-    width = matrix.shape[1]
-
-    @pl.when(step == 0)
-    def _():
-        total = own[...] + arrived[...].astype(F32)
-        if subtract:
-            total = base[...] - total
-        vector[...] = total.T.astype(BF16)
-
-    product = jnp.dot(vector[...], matrix[...], preferred_element_type=F32)
-    whole[pl.ds(pl.multiple_of(step * width, width), width), :] = product.T
-
-    @pl.when(step == pl.num_programs(0) - 1)
-    def _():
-        distribute(place, whole, keep, send)
-
-
-def backward_product(place, own, arrived, base, matrix, block, nz):
-    rows, width = matrix.shape
-    n = own.shape[1]
-    part = width // (nz * NX * NC)
-    subtract = base is not None
-    if base is None:
-        base = jnp.zeros((8, 128), F32)
-    whole_spec = lambda shape: pl.BlockSpec(shape, lambda i, *_: (0,) * len(shape))
-    outs = pl.pallas_call(
-        functools.partial(backward_kernel, nz, subtract),
-        out_shape=[jax.ShapeDtypeStruct((NX, part, n), F32)] * nz
-        + [jax.ShapeDtypeStruct((NX, part, n), BF16)] * nz,
-        grid_spec=pltpu.PrefetchScalarGridSpec(
-            num_scalar_prefetch=1,
-            grid=(width // block,),
-            in_specs=[whole_spec(own.shape), whole_spec(own.shape), whole_spec(base.shape)]
-            + [pl.BlockSpec((rows, block), lambda i, *_: (0, i))],
-            out_specs=[whole_spec((NX, part, n))] * (2 * nz),
-            scratch_shapes=[pltpu.VMEM((n, rows), BF16), pltpu.VMEM((width, n), F32)],
-        ),
-        compiler_params=pltpu.CompilerParams(vmem_limit_bytes=VMEM_LIMIT),
-        cost_estimate=pl.CostEstimate(
-            flops=2 * rows * width * n, bytes_accessed=2 * rows * width, transcendentals=0
-        ),
-        name="backward_product",
-    )(place, own, arrived, base, matrix)
-    return outs[:nz], outs[nz:]
+        functools.partial(turn_kernel, subtract),
+        out_shape=jax.ShapeDtypeStruct((n, rows), BF16),
+        in_specs=[VMEM] * 3,
+        out_specs=VMEM,
+        name="turn",
+    )(own, arrived, base if subtract else jnp.zeros((8, n), F32))
 
 
 def push_kernel(nz, place, block, own, arrived, coupling, *refs):
@@ -300,11 +326,42 @@
     )(place, block, *pieces, coupling)
 
 
-def column_block(width):
-    for parts in (8, 4, 2, 1):
-        if width % (parts * 128) == 0 and width // parts >= 1024:
-            return width // parts
-    return width
+def load_kernel(k, parts, place, matrix, out, arrived):
+    rows, depth = out.shape
+    first = place[k * NX * NC] // (NX * NC)
+    cols = pl.ds(pl.multiple_of(first * depth, 128), depth)
+    height = rows // parts
+    copies = [
+        pltpu.make_async_copy(
+            matrix.at[pl.ds(i * height, height), cols],
+            out.at[pl.ds(i * height, height), :],
+            arrived.at[i],
+        )
+        for i in range(parts)
+    ]
+    for copy in copies:
+        copy.start()
+    for copy in copies:
+        copy.wait()
+
+
+def load_block(place, matrix, k, nz, name):
+    rows, width = matrix.shape
+    depth = width // nz
+    parts = max(p for p in (1, 2, 4, 8, 11) if rows % (16 * p) == 0)
+    block = pl.pallas_call(
+        functools.partial(load_kernel, k, parts),
+        out_shape=pltpu.VMEM((rows, depth), matrix.dtype),
+        in_specs=[SMEM, pl.BlockSpec(memory_space=pltpu.HBM)],
+        out_specs=VMEM,
+        scratch_shapes=[pltpu.SemaphoreType.DMA((parts,))],
+        compiler_params=pltpu.CompilerParams(vmem_limit_bytes=VMEM_LIMIT),
+        cost_estimate=pl.CostEstimate(
+            flops=0, bytes_accessed=4 * rows * depth, transcendentals=0
+        ),
+        name=name,
+    )(place, pltpu.with_memory_space_constraint(matrix, pltpu.HBM))
+    return pltpu.with_memory_space_constraint(block, pltpu.VMEM)
 
 
 def two_level_body(rhs_root, rhs_level, root_inverse, level_inverse, coupling_t, coupling_rows):
@@ -312,33 +369,26 @@
     width = root_inverse.shape[1]
     place = places(nz)
     block = coupling_rows[0] % (width // RB)
+    level_blocks = [load_block(place, level_inverse, k, nz, "load_level") for k in range(nz)]
+    level_again = [load_block(place, level_inverse, k, nz, "load_level_again") for k in range(nz)]
+    root_blocks = [load_block(place, root_inverse, k, nz, "load_root") for k in range(nz)]
 
     level_pieces = gather_pieces(rhs_level.astype(BF16), nz)
-    own, own_b = forward_product(
-        place, level_pieces, level_inverse, column_block(level_inverse.shape[1])
-    )
+    own, own_b = forward_product(place, level_pieces, level_blocks, nz)
     forward_level, keep, send = push_product(
         place, block, own, sub_swap(own_b), coupling_t, width, nz
     )
     shifted = rhs_root - scatter_sum(keep, send, nz)
 
     root_pieces = gather_pieces(shifted.astype(BF16), nz)
-    own, own_b = forward_product(place, root_pieces, root_inverse, column_block(width))
-    keep, send = backward_product(
-        place, own, sub_swap(own_b), None, root_inverse, column_block(width), nz
-    )
+    own, own_b = forward_product(place, root_pieces, root_blocks, nz)
+    keep, send = backward_product(place, turn(own, sub_swap(own_b)), root_blocks, nz)
     root_potential = scatter_sum(keep, send, nz)
 
     potential_pieces = gather_pieces(root_potential.astype(BF16), nz)
     own, own_b = pull_product(place, block, potential_pieces, coupling_t)
     keep, send = backward_product(
-        place,
-        own,
-        sub_swap(own_b),
-        forward_level,
-        level_inverse,
-        column_block(level_inverse.shape[1]),
-        nz,
+        place, turn(own, sub_swap(own_b), forward_level), level_again, nz
     )
     level_potential = scatter_sum(keep, send, nz)
     return (root_potential, level_potential)

time: 224 us -> 253 us (1.13)
  starting transfers between devices: 86.6 us -> 56 us
  Pallas kernels: 47.2 us -> 77.7 us
  waiting for transfers between devices: 84.5 us -> 102 us
  local copies, waits for them, and re-layouts: 0.11 us -> 11 us
    pallas_call x4 -> x30, Pallas kernels: 42.9 us -> 74.5 us  [the longest x12 40.3 us: load_block(): pl.pallas_call(functools.partial(load_kernel, k, parts), out_shape=pltpu....]
    ppermute x18, starting transfers between devices: 47.2 us -> 20 us  [z_shift(): lax.ppermute(value, 'front', [(i, (i + shift * width) % count) for i in r...]
    ppermute x18, waiting for transfers between devices: 30.8 us -> 46.6 us  [z_shift(): lax.ppermute(value, 'front', [(i, (i + shift * width) % count) for i in r...]
    unnamed x6 -> x42, local copies, waits for them, and re-layouts: 0.02 us -> 10.9 us
    ppermute x24, waiting for transfers between devices: 28.9 us -> 36.1 us  [x_swap(): lax.ppermute(value, 'front', [(i, i ^ NC) for i in range(nz * NX * NC)])]
    ppermute x36, waiting for transfers between devices: 5.69 us -> 2.08 us  [c_swap(): lax.ppermute(value, 'front', [(i, i ^ 1) for i in range(nz * NX * NC)])]
    ppermute x24, starting transfers between devices: 27.9 us -> 24.4 us  [x_swap(): lax.ppermute(value, 'front', [(i, i ^ NC) for i in range(nz * NX * NC)])]
  transfers between devices with their start and end apart: 81 -> 81, of which waited for: 32 -> 36; matrix products, arithmetic and copies ran while one was open for 0% -> 0% of each run, Pallas kernels for 0% -> 25%
where the time goes in v2:
time: 253 us; the launch traced here: 252 us
  waiting for transfers between devices  102 us (40%)
  Pallas kernels  77.7 us (31%)
  starting transfers between devices  56 us (22%)
  local copies, waits for them, and re-layouts  11 us (4%)
  other arithmetic  3.62 us (1%)
    ppermute x18, waiting for transfers between devices, z_shift(): lax.ppermute(value, 'front', [(i, (i + shift * width) % count) for i in r...  46.6 us
    pallas_call x12, Pallas kernels, load_block(): pl.pallas_call(functools.partial(load_kernel, k, parts), out_shape=pltpu....  40.3 us
    ppermute x24, waiting for transfers between devices, x_swap(): lax.ppermute(value, 'front', [(i, i ^ NC) for i in range(nz * NX * NC)])  36.1 us
    ppermute x24, starting transfers between devices, x_swap(): lax.ppermute(value, 'front', [(i, i ^ NC) for i in range(nz * NX * NC)])  24.4 us
    ppermute x18, starting transfers between devices, z_shift(): lax.ppermute(value, 'front', [(i, (i + shift * width) % count) for i in r...  20 us
    ppermute x3, waiting for transfers between devices, sub_swap(): return lax.ppermute(value, 'sub', [(0, 1), (1, 0)])  17.7 us
    pallas_call x8, Pallas kernels, forward_product(): pl.pallas_call(functools.partial(forward_kernel, k, fresh, last), out_sha...  16.7 us
    pallas_call x8, Pallas kernels, backward_product(): pl.pallas_call(functools.partial(backward_kernel, k), out_shape=[jax.Shap...  13.4 us
  transfers between devices with their start and end apart: 81, of which 36 were waited for; matrix products, arithmetic and copies ran while one was open for 0% of the time, Pallas kernels for 25%

profile of v2, /device:TPU:0, one launch (start us, length us, event | category | flops | bytes accessed | tf_op | source)
XLA Modules:
  0.0 252.1 jit_solution(5206314195256989579)
XLA Ops:
  1.6 5.1 %collective-permute-start.8 = (bf16[352,128]{1,0:T(8,128)(2,1)S(1)}, bf16[352,128]{1,0:T(8,128)(2,1)S(1)}, u32[]{:S(2)}, u32[]{:S(2)}) collective-permute-start(bf16[352,128]{1,0:T(8,128)(2,1)S(1)} %convert_element_type.267.refs_0_), channel_id=1, source_target_pairs={{0,12},{1,13},{2,14},{3,15},{4,0},{5,1},{6,2},{7,3},{8,4},{9,5},{1... | collective-permute-start | bytes 270344 | tf_op jit(solution)/shard_map/ppermute | solution.py:81
  11.2 4.2 %collective-permute-done.4.refs_0_ = bf16[352,128]{1,0:T(8,128)(2,1)S(1)} collective-permute-done((bf16[352,128]{1,0:T(8,128)(2,1)S(1)}, bf16[352,128]{1,0:T(8,128)(2,1)S(1)}, u32[]{:S(2)}, u32[]{:S(2)}) %collective-permute-start.4) | collective-permute-done | bytes 90144 | tf_op jit(solution)/shard_map/ppermute | solution.py:81
  22.3 2.2 load_level.7.refs_4_
  24.5 2.2 load_level.6.refs_4_
  26.8 2.2 load_level.5.refs_4_
  29.0 2.2 load_level.4.refs_4_
  38.0 5.4 %collective-permute-done.15.arrived = bf16[704,128]{1,0:T(8,128)(2,1)S(1)} collective-permute-done((bf16[704,128]{1,0:T(8,128)(2,1)S(1)}, bf16[704,128]{1,0:T(8,128)(2,1)S(1)}, u32[]{:S(2)}, u32[]{:S(2)}) %collective-permute-start.15) | collective-permute-done | bytes 180256 | tf_op jit(solution)/shard_map/ppermute | solution.py:95
  51.6 3.0 %collective-permute-done.17 = bf16[704,128]{1,0:T(8,128)(2,1)S(1)} collective-permute-done((bf16[704,128]{1,0:T(8,128)(2,1)S(1)}, bf16[704,128]{1,0:T(8,128)(2,1)S(1)}, u32[]{:S(2)}, u32[]{:S(2)}) %collective-permute-start.17) | collective-permute-done | bytes 180256 | tf_op jit(solution)/shard_map/ppermute | solution.py:87
  54.7 3.7 %collective-permute-done.20 = bf16[704,128]{1,0:T(8,128)(2,1)S(1)} collective-permute-done((bf16[704,128]{1,0:T(8,128)(2,1)S(1)}, bf16[704,128]{1,0:T(8,128)(2,1)S(1)}, u32[]{:S(2)}, u32[]{:S(2)}) %collective-permute-start.20) | collective-permute-done | bytes 180256 | tf_op jit(solution)/shard_map/ppermute | solution.py:87
  58.5 3.7 %collective-permute-done.23 = bf16[704,128]{1,0:T(8,128)(2,1)S(1)} collective-permute-done((bf16[704,128]{1,0:T(8,128)(2,1)S(1)}, bf16[704,128]{1,0:T(8,128)(2,1)S(1)}, u32[]{:S(2)}, u32[]{:S(2)}) %collective-permute-start.23) | collective-permute-done | bytes 180256 | tf_op jit(solution)/shard_map/ppermute | solution.py:87
  65.3 2.3 collective-permute-done.18
  67.6 3.2 %collective-permute-done.24 = bf16[704,128]{1,0:T(8,128)(2,1)S(1)} collective-permute-done((bf16[704,128]{1,0:T(8,128)(2,1)S(1)}, bf16[704,128]{1,0:T(8,128)(2,1)S(1)}, u32[]{:S(2)}, u32[]{:S(2)}) %collective-permute-start.24) | collective-permute-done | bytes 180256 | tf_op jit(solution)/shard_map/ppermute | solution.py:81
  75.3 2.1 collective-permute-done.35.refs_0_
  78.4 5.1 %collective-permute-done.31.refs_0_ = bf16[704,128]{1,0:T(8,128)(2,1)S(1)} collective-permute-done((bf16[704,128]{1,0:T(8,128)(2,1)S(1)}, bf16[704,128]{1,0:T(8,128)(2,1)S(1)}, u32[]{:S(2)}, u32[]{:S(2)}) %collective-permute-start.31) | collective-permute-done | bytes 180256 | tf_op jit(solution)/shard_map/ppermute | solution.py:81
  84.1 5.0 %collective-permute-done.27.refs_0_ = bf16[704,128]{1,0:T(8,128)(2,1)S(1)} collective-permute-done((bf16[704,128]{1,0:T(8,128)(2,1)S(1)}, bf16[704,128]{1,0:T(8,128)(2,1)S(1)}, u32[]{:S(2)}, u32[]{:S(2)}) %collective-permute-start.27) | collective-permute-done | bytes 180256 | tf_op jit(solution)/shard_map/ppermute | solution.py:81
  90.1 4.0 %load_root.7.refs_4_.matrix = bf16[1408,2816]{1,0:T(8,128)(2,1)S(1)} custom-call(s32[16]{0:T(128)S(1)} %stack.67.place, bf16[1408,11264]{1,0:T(8,128)(2,1)} %matrix.19), custom_call_target="tpu_custom_call" | custom-call | bytes 15859712 | tf_op jit(solution)/shard_map/load_root/pallas_call | solution.py:352
  94.1 6.2 %load_root.6.refs_4_.matrix = bf16[1408,2816]{1,0:T(8,128)(2,1)S(1)} custom-call(s32[16]{0:T(128)S(1)} %stack.67.place, bf16[1408,11264]{1,0:T(8,128)(2,1)} %matrix.19), custom_call_target="tpu_custom_call" | custom-call | bytes 15859712 | tf_op jit(solution)/shard_map/load_root/pallas_call | solution.py:352
  100.3 6.2 %load_root.5.refs_4_.matrix = bf16[1408,2816]{1,0:T(8,128)(2,1)S(1)} custom-call(s32[16]{0:T(128)S(1)} %stack.67.place, bf16[1408,11264]{1,0:T(8,128)(2,1)} %matrix.19), custom_call_target="tpu_custom_call" | custom-call | bytes 15859712 | tf_op jit(solution)/shard_map/load_root/pallas_call | solution.py:352
  106.4 6.2 %load_root.4.refs_4_.matrix = bf16[1408,2816]{1,0:T(8,128)(2,1)S(1)} custom-call(s32[16]{0:T(128)S(1)} %stack.67.place, bf16[1408,11264]{1,0:T(8,128)(2,1)} %matrix.19), custom_call_target="tpu_custom_call" | custom-call | bytes 15859712 | tf_op jit(solution)/shard_map/load_root/pallas_call | solution.py:352
  113.3 2.9 %forward_product.12.refs_5_ = f32[1408,128]{1,0:T(8,128)S(1)} custom-call(s32[16]{0:T(128)S(1)} %stack.67.place, bf16[704,128]{1,0:T(8,128)(2,1)S(1)} %fusion.6.refs_0_, bf16[704,128]{1,0:T(8,128)(2,1)S(1)} %collective-permute-done.39.refs_1_, bf16[704,128]{1,0:T(8,128)(2,1)S(1)} %collective-permute-done.40.refs_2_, ...), custom_call_target="tpu_custom_call" | custom-call | flops 1015021568 | bytes 7929856 | tf_op jit(solution)/shard_map/forward_product/pallas_call | solution.py:191
  116.8 2.9 %forward_product.13.refs_5_ = f32[1408,128]{1,0:T(8,128)S(1)} custom-call(s32[16]{0:T(128)S(1)} %stack.67.place, bf16[704,128]{1,0:T(8,128)(2,1)S(1)} %collective-permute-done.35.refs_0_, bf16[704,128]{1,0:T(8,128)(2,1)S(1)} %collective-permute-done.36.refs_1_, bf16[704,128]{1,0:T(8,128)(2,1)S(1)} %collective-permute-done.37.refs_2_, ...), custom_call_target="tpu_custom_call" | custom-call | flops 1015021568 | bytes 7929856 | tf_op jit(solution)/shard_map/forward_product/pallas_call | solution.py:191
  119.7 2.9 %forward_product.14.refs_5_ = f32[1408,128]{1,0:T(8,128)S(1)} custom-call(s32[16]{0:T(128)S(1)} %stack.67.place, bf16[704,128]{1,0:T(8,128)(2,1)S(1)} %collective-permute-done.31.refs_0_, bf16[704,128]{1,0:T(8,128)(2,1)S(1)} %collective-permute-done.32.refs_1_, bf16[704,128]{1,0:T(8,128)(2,1)S(1)} %collective-permute-done.33.refs_2_, ...), custom_call_target="tpu_custom_call" | custom-call | flops 1015021568 | bytes 7929856 | tf_op jit(solution)/shard_map/forward_product/pallas_call | solution.py:191
  122.7 2.9 %forward_product.15 = (f32[1408,128]{1,0:T(8,128)S(1)}, bf16[1408,128]{1,0:T(8,128)(2,1)S(1)}) custom-call(s32[16]{0:T(128)S(1)} %stack.67.place, bf16[704,128]{1,0:T(8,128)(2,1)S(1)} %collective-permute-done.27.refs_0_, bf16[704,128]{1,0:T(8,128)(2,1)S(1)} %collective-permute-done.28.refs_1_, bf16[704,128]{1,0:T(8,128)(2,1)S(1)} %collective-permute-done.29.refs_2_, ...), custom_call_target="tpu_custom_call" | custom-call | flops 1015021568 | bytes 7929856 | tf_op jit(solution)/shard_map/forward_product/pallas_call | solution.py:191
  128.0 9.2 %collective-permute-done.42.arrived = bf16[1408,128]{1,0:T(8,128)(2,1)S(1)} collective-permute-done((bf16[1408,128]{1,0:T(8,128)(2,1)S(1)}, bf16[1408,128]{1,0:T(8,128)(2,1)S(1)}, u32[]{:S(2)}, u32[]{:S(2)}) %collective-permute-start.42) | collective-permute-done | bytes 360480 | tf_op jit(solution)/shard_map/ppermute | solution.py:95
  138.0 2.1 turn.2.vector
  140.1 3.2 %copy-done.5 = bf16[1408,2816]{1,0:T(8,128)(2,1)S(1)} copy-done((bf16[1408,2816]{1,0:T(8,128)(2,1)S(1)}, bf16[1408,2816]{1,0:T(8,128)(2,1)}, u32[]{:S(2)}) %copy-start.5) | copy-done | bytes 7929880
  144.3 2.1 backward_product.8
  146.6 3.4 %copy-done.3 = bf16[1408,2816]{1,0:T(8,128)(2,1)S(1)} copy-done((bf16[1408,2816]{1,0:T(8,128)(2,1)S(1)}, bf16[1408,2816]{1,0:T(8,128)(2,1)}, u32[]{:S(2)}) %copy-start.3) | copy-done | bytes 7929880
  150.0 2.4 backward_product.9
  152.9 2.1 backward_product.10
  155.1 2.1 backward_product.11
  162.3 3.0 %collective-permute-done.44 = bf16[704,128]{1,0:T(8,128)(2,1)S(1)} collective-permute-done((bf16[704,128]{1,0:T(8,128)(2,1)S(1)}, bf16[704,128]{1,0:T(8,128)(2,1)S(1)}, u32[]{:S(2)}, u32[]{:S(2)}) %collective-permute-start.44) | collective-permute-done | bytes 180256 | tf_op jit(solution)/shard_map/ppermute | solution.py:87
  165.5 3.7 %collective-permute-done.47 = bf16[704,128]{1,0:T(8,128)(2,1)S(1)} collective-permute-done((bf16[704,128]{1,0:T(8,128)(2,1)S(1)}, bf16[704,128]{1,0:T(8,128)(2,1)S(1)}, u32[]{:S(2)}, u32[]{:S(2)}) %collective-permute-start.47) | collective-permute-done | bytes 180256 | tf_op jit(solution)/shard_map/ppermute | solution.py:87
  169.3 3.7 %collective-permute-done.50 = bf16[704,128]{1,0:T(8,128)(2,1)S(1)} collective-permute-done((bf16[704,128]{1,0:T(8,128)(2,1)S(1)}, bf16[704,128]{1,0:T(8,128)(2,1)S(1)}, u32[]{:S(2)}, u32[]{:S(2)}) %collective-permute-start.50) | collective-permute-done | bytes 180256 | tf_op jit(solution)/shard_map/ppermute | solution.py:87
  173.1 2.0 collective-permute-start.51
  176.0 2.7 %collective-permute-done.45 = bf16[704,128]{1,0:T(8,128)(2,1)S(1)} collective-permute-done((bf16[704,128]{1,0:T(8,128)(2,1)S(1)}, bf16[704,128]{1,0:T(8,128)(2,1)S(1)}, u32[]{:S(2)}, u32[]{:S(2)}) %collective-permute-start.45) | collective-permute-done | bytes 180256 | tf_op jit(solution)/shard_map/ppermute | solution.py:81
  178.7 3.3 %collective-permute-done.51 = bf16[704,128]{1,0:T(8,128)(2,1)S(1)} collective-permute-done((bf16[704,128]{1,0:T(8,128)(2,1)S(1)}, bf16[704,128]{1,0:T(8,128)(2,1)S(1)}, u32[]{:S(2)}, u32[]{:S(2)}) %collective-permute-start.51) | collective-permute-done | bytes 180256 | tf_op jit(solution)/shard_map/ppermute | solution.py:81
  187.0 3.1 %collective-permute-done.57.refs_4_ = bf16[704,128]{1,0:T(8,128)(2,1)S(1)} collective-permute-done((bf16[704,128]{1,0:T(8,128)(2,1)S(1)}, bf16[704,128]{1,0:T(8,128)(2,1)S(1)}, u32[]{:S(2)}, u32[]{:S(2)}) %collective-permute-start.57) | collective-permute-done | bytes 180256 | tf_op jit(solution)/shard_map/ppermute | solution.py:81
  191.0 9.6 %collective-permute-done.61.refs_8_ = bf16[704,128]{1,0:T(8,128)(2,1)S(1)} collective-permute-done((bf16[704,128]{1,0:T(8,128)(2,1)S(1)}, bf16[704,128]{1,0:T(8,128)(2,1)S(1)}, u32[]{:S(2)}, u32[]{:S(2)}) %collective-permute-start.61) | collective-permute-done | bytes 180256 | tf_op jit(solution)/shard_map/ppermute | solution.py:81
  203.2 4.5 %collective-permute-done.63.refs_10_ = bf16[704,128]{1,0:T(8,128)(2,1)S(1)} collective-permute-done((bf16[704,128]{1,0:T(8,128)(2,1)S(1)}, bf16[704,128]{1,0:T(8,128)(2,1)S(1)}, u32[]{:S(2)}, u32[]{:S(2)}) %collective-permute-start.63) | collective-permute-done | bytes 180256 | tf_op jit(solution)/shard_map/ppermute | solution.py:87
  214.5 2.2 load_level_again.4.matrix
  216.8 3.0 %collective-permute-done.69.arrived = bf16[704,128]{1,0:T(8,128)(2,1)S(1)} collective-permute-done((bf16[704,128]{1,0:T(8,128)(2,1)S(1)}, bf16[704,128]{1,0:T(8,128)(2,1)S(1)}, u32[]{:S(2)}, u32[]{:S(2)}) %collective-permute-start.69) | collective-permute-done | bytes 180256 | tf_op jit(solution)/shard_map/ppermute | solution.py:95
  220.4 2.0 turn.3.vector
  224.6 2.2 load_level_again.5.matrix
  226.9 2.2 load_level_again.6.matrix
  229.1 2.2 load_level_again.7.matrix
  245.5 2.0 collective-permute-start.78
  247.5 3.3 %collective-permute-done.72 = bf16[352,128]{1,0:T(8,128)(2,1)S(1)} collective-permute-done((bf16[352,128]{1,0:T(8,128)(2,1)S(1)}, bf16[352,128]{1,0:T(8,128)(2,1)S(1)}, u32[]{:S(2)}, u32[]{:S(2)}) %collective-permute-start.72) | collective-permute-done | bytes 90144 | tf_op jit(solution)/shard_map/ppermute | solution.py:81
  (218 shorter events, 83.4 us)
Async XLA Ops:
  1.6 8.0 %collective-permute-start.8 = (bf16[352,128]{1,0:T(8,128)(2,1)S(1)}, bf16[352,128]{1,0:T(8,128)(2,1)S(1)}, u32[]{:S(2)}, u32[]{:S(2)}) collective-permute-start(bf16[352,128]{1,0:T(8,128)(2,1)S(1)} %convert_element_type.267.refs_0_), channel_id=1, source_target_pairs={{0,12},{1,13},{2,14},{3,15},{4,0},{5,1},{6,2},{7,3},{8,4},{9,5},{1... | collective-permute-start | bytes 270344 | tf_op jit(solution)/shard_map/ppermute | solution.py:81
  8.2 7.2 %collective-permute-start.4 = (bf16[352,128]{1,0:T(8,128)(2,1)S(1)}, bf16[352,128]{1,0:T(8,128)(2,1)S(1)}, u32[]{:S(2)}, u32[]{:S(2)}) collective-permute-start(bf16[352,128]{1,0:T(8,128)(2,1)S(1)} %convert_element_type.267.refs_0_), channel_id=1, source_target_pairs={{0,4},{1,5},{2,6},{3,7},{4,8},{5,9},{6,10},{7,11},{8,12},{9,13},{1... | collective-permute-start | bytes 270344 | tf_op jit(solution)/shard_map/ppermute | solution.py:81
  8.2 7.8 %collective-permute-start.12 = (bf16[352,128]{1,0:T(8,128)(2,1)S(1)}, bf16[352,128]{1,0:T(8,128)(2,1)S(1)}, u32[]{:S(2)}, u32[]{:S(2)}) collective-permute-start(bf16[352,128]{1,0:T(8,128)(2,1)S(1)} %convert_element_type.267.refs_0_), channel_id=1, source_target_pairs={{0,1},{1,0},{2,3},{3,2},{4,5},{5,4},{6,7},{7,6},{8,9},{9,8},{10,11... | collective-permute-start | bytes 270344 | tf_op jit(solution)/shard_map/ppermute | solution.py:91
  8.2 9.5 %collective-permute-start = (bf16[352,128]{1,0:T(8,128)(2,1)S(1)}, bf16[352,128]{1,0:T(8,128)(2,1)S(1)}, u32[]{:S(2)}, u32[]{:S(2)}) collective-permute-start(bf16[352,128]{1,0:T(8,128)(2,1)S(1)} %convert_element_type.267.refs_0_), channel_id=1, source_target_pairs={{0,8},{1,9},{2,10},{3,11},{4,12},{5,13},{6,14},{7,15},{8,0},{9,1},... | collective-permute-start | bytes 270344 | tf_op jit(solution)/shard_map/ppermute | solution.py:81
  9.6 8.6 %collective-permute-start.10 = (bf16[352,128]{1,0:T(8,128)(2,1)S(1)}, bf16[352,128]{1,0:T(8,128)(2,1)S(1)}, u32[]{:S(2)}, u32[]{:S(2)}) collective-permute-start(bf16[352,128]{1,0:T(8,128)(2,1)S(1)} %collective-permute-done.8.refs_0_), channel_id=1, source_target_pairs={{0,2},{1,3},{2,0},{3,1},{4,6},{5,7},{6,4},{7,5},{8,10},{9,11},{10,... | collective-permute-start | bytes 270344 | tf_op jit(solution)/shard_map/ppermute | solution.py:87
  18.2 14.4 %collective-permute-start.11 = (bf16[352,128]{1,0:T(8,128)(2,1)S(1)}, bf16[352,128]{1,0:T(8,128)(2,1)S(1)}, u32[]{:S(2)}, u32[]{:S(2)}) collective-permute-start(bf16[352,128]{1,0:T(8,128)(2,1)S(1)} %collective-permute-done.10.refs_2_), channel_id=1, source_target_pairs={{0,1},{1,0},{2,3},{3,2},{4,5},{5,4},{6,7},{7,6},{8,9},{9,8},{10,11... | collective-permute-start | bytes 270344 | tf_op jit(solution)/shard_map/ppermute | solution.py:91
  18.2 15.6 %collective-permute-start.5 = (bf16[352,128]{1,0:T(8,128)(2,1)S(1)}, bf16[352,128]{1,0:T(8,128)(2,1)S(1)}, u32[]{:S(2)}, u32[]{:S(2)}) collective-permute-start(bf16[352,128]{1,0:T(8,128)(2,1)S(1)} %collective-permute-done.4.refs_0_), channel_id=1, source_target_pairs={{0,1},{1,0},{2,3},{3,2},{4,5},{5,4},{6,7},{7,6},{8,9},{9,8},{10,11... | collective-permute-start | bytes 270344 | tf_op jit(solution)/shard_map/ppermute | solution.py:91
  19.9 13.9 %collective-permute-start.7 = (bf16[352,128]{1,0:T(8,128)(2,1)S(1)}, bf16[352,128]{1,0:T(8,128)(2,1)S(1)}, u32[]{:S(2)}, u32[]{:S(2)}) collective-permute-start(bf16[352,128]{1,0:T(8,128)(2,1)S(1)} %collective-permute-done.6.refs_2_), channel_id=1, source_target_pairs={{0,1},{1,0},{2,3},{3,2},{4,5},{5,4},{6,7},{7,6},{8,9},{9,8},{10,11... | collective-permute-start | bytes 270344 | tf_op jit(solution)/shard_map/ppermute | solution.py:91
  19.9 15.2 %collective-permute-start.1 = (bf16[352,128]{1,0:T(8,128)(2,1)S(1)}, bf16[352,128]{1,0:T(8,128)(2,1)S(1)}, u32[]{:S(2)}, u32[]{:S(2)}) collective-permute-start(bf16[352,128]{1,0:T(8,128)(2,1)S(1)} %collective-permute-done.refs_0_), channel_id=1, source_target_pairs={{0,1},{1,0},{2,3},{3,2},{4,5},{5,4},{6,7},{7,6},{8,9},{9,8},{10,11... | collective-permute-start | bytes 270344 | tf_op jit(solution)/shard_map/ppermute | solution.py:91
  22.2 12.9 %collective-permute-start.3 = (bf16[352,128]{1,0:T(8,128)(2,1)S(1)}, bf16[352,128]{1,0:T(8,128)(2,1)S(1)}, u32[]{:S(2)}, u32[]{:S(2)}) collective-permute-start(bf16[352,128]{1,0:T(8,128)(2,1)S(1)} %collective-permute-done.2.refs_2_), channel_id=1, source_target_pairs={{0,1},{1,0},{2,3},{3,2},{4,5},{5,4},{6,7},{7,6},{8,9},{9,8},{10,11... | collective-permute-start | bytes 270344 | tf_op jit(solution)/shard_map/ppermute | solution.py:91
  47.1 7.5 %collective-permute-start.17 = (bf16[704,128]{1,0:T(8,128)(2,1)S(1)}, bf16[704,128]{1,0:T(8,128)(2,1)S(1)}, u32[]{:S(2)}, u32[]{:S(2)}) collective-permute-start(bf16[704,128]{1,0:T(8,128)(2,1)S(1)} %fusion.10), channel_id=1, source_target_pairs={{0,2},{1,3},{2,0},{3,1},{4,6},{5,7},{6,4},{7,5},{8,10},{9,11},{10,... | collective-permute-start | bytes 540680 | tf_op jit(solution)/shard_map/ppermute | solution.py:87
  47.7 10.7 %collective-permute-start.20 = (bf16[704,128]{1,0:T(8,128)(2,1)S(1)}, bf16[704,128]{1,0:T(8,128)(2,1)S(1)}, u32[]{:S(2)}, u32[]{:S(2)}) collective-permute-start(bf16[704,128]{1,0:T(8,128)(2,1)S(1)} %fusion.11), channel_id=1, source_target_pairs={{0,2},{1,3},{2,0},{3,1},{4,6},{5,7},{6,4},{7,5},{8,10},{9,11},{10,... | collective-permute-start | bytes 540680 | tf_op jit(solution)/shard_map/ppermute | solution.py:87
  49.3 12.9 %collective-permute-start.23 = (bf16[704,128]{1,0:T(8,128)(2,1)S(1)}, bf16[704,128]{1,0:T(8,128)(2,1)S(1)}, u32[]{:S(2)}, u32[]{:S(2)}) collective-permute-start(bf16[704,128]{1,0:T(8,128)(2,1)S(1)} %fusion.12), channel_id=1, source_target_pairs={{0,2},{1,3},{2,0},{3,1},{4,6},{5,7},{6,4},{7,5},{8,10},{9,11},{10,... | collective-permute-start | bytes 540680 | tf_op jit(solution)/shard_map/ppermute | solution.py:87
  50.0 15.3 %collective-permute-start.26 = (bf16[704,128]{1,0:T(8,128)(2,1)S(1)}, bf16[704,128]{1,0:T(8,128)(2,1)S(1)}, u32[]{:S(2)}, u32[]{:S(2)}) collective-permute-start(bf16[704,128]{1,0:T(8,128)(2,1)S(1)} %fusion.13), channel_id=1, source_target_pairs={{0,2},{1,3},{2,0},{3,1},{4,6},{5,7},{6,4},{7,5},{8,10},{9,11},{10,... | collective-permute-start | bytes 540680 | tf_op jit(solution)/shard_map/ppermute | solution.py:87
  54.6 13.0 %collective-permute-start.18 = (bf16[704,128]{1,0:T(8,128)(2,1)S(1)}, bf16[704,128]{1,0:T(8,128)(2,1)S(1)}, u32[]{:S(2)}, u32[]{:S(2)}) collective-permute-start(bf16[704,128]{1,0:T(8,128)(2,1)S(1)} %fusion.9), channel_id=1, source_target_pairs={{0,8},{1,9},{2,10},{3,11},{4,12},{5,13},{6,14},{7,15},{8,0},{9,1},... | collective-permute-start | bytes 540680 | tf_op jit(solution)/shard_map/ppermute | solution.py:81
  58.5 9.1 %collective-permute-start.21 = (bf16[704,128]{1,0:T(8,128)(2,1)S(1)}, bf16[704,128]{1,0:T(8,128)(2,1)S(1)}, u32[]{:S(2)}, u32[]{:S(2)}) collective-permute-start(bf16[704,128]{1,0:T(8,128)(2,1)S(1)} %fusion.8), channel_id=1, source_target_pairs={{0,4},{1,5},{2,6},{3,7},{4,8},{5,9},{6,10},{7,11},{8,12},{9,13},{1... | collective-permute-start | bytes 540680 | tf_op jit(solution)/shard_map/ppermute | solution.py:81
  62.3 8.4 %collective-permute-start.24 = (bf16[704,128]{1,0:T(8,128)(2,1)S(1)}, bf16[704,128]{1,0:T(8,128)(2,1)S(1)}, u32[]{:S(2)}, u32[]{:S(2)}) collective-permute-start(bf16[704,128]{1,0:T(8,128)(2,1)S(1)} %fusion.7), channel_id=1, source_target_pairs={{0,12},{1,13},{2,14},{3,15},{4,0},{5,1},{6,2},{7,3},{8,4},{9,5},{1... | collective-permute-start | bytes 540680 | tf_op jit(solution)/shard_map/ppermute | solution.py:81
  73.2 10.3 %collective-permute-start.31 = (bf16[704,128]{1,0:T(8,128)(2,1)S(1)}, bf16[704,128]{1,0:T(8,128)(2,1)S(1)}, u32[]{:S(2)}, u32[]{:S(2)}) collective-permute-start(bf16[704,128]{1,0:T(8,128)(2,1)S(1)} %fusion.6.refs_0_), channel_id=1, source_target_pairs={{0,4},{1,5},{2,6},{3,7},{4,8},{5,9},{6,10},{7,11},{8,12},{9,13},{1... | collective-permute-start | bytes 540680 | tf_op jit(solution)/shard_map/ppermute | solution.py:81
  73.7 10.3 %collective-permute-start.39 = (bf16[704,128]{1,0:T(8,128)(2,1)S(1)}, bf16[704,128]{1,0:T(8,128)(2,1)S(1)}, u32[]{:S(2)}, u32[]{:S(2)}) collective-permute-start(bf16[704,128]{1,0:T(8,128)(2,1)S(1)} %fusion.6.refs_0_), channel_id=1, source_target_pairs={{0,1},{1,0},{2,3},{3,2},{4,5},{5,4},{6,7},{7,6},{8,9},{9,8},{10,11... | collective-permute-start | bytes 540680 | tf_op jit(solution)/shard_map/ppermute | solution.py:91
  73.7 15.4 %collective-permute-start.27 = (bf16[704,128]{1,0:T(8,128)(2,1)S(1)}, bf16[704,128]{1,0:T(8,128)(2,1)S(1)}, u32[]{:S(2)}, u32[]{:S(2)}) collective-permute-start(bf16[704,128]{1,0:T(8,128)(2,1)S(1)} %fusion.6.refs_0_), channel_id=1, source_target_pairs={{0,8},{1,9},{2,10},{3,11},{4,12},{5,13},{6,14},{7,15},{8,0},{9,1},... | collective-permute-start | bytes 540680 | tf_op jit(solution)/shard_map/ppermute | solution.py:81
  77.4 12.7 %collective-permute-start.37 = (bf16[704,128]{1,0:T(8,128)(2,1)S(1)}, bf16[704,128]{1,0:T(8,128)(2,1)S(1)}, u32[]{:S(2)}, u32[]{:S(2)}) collective-permute-start(bf16[704,128]{1,0:T(8,128)(2,1)S(1)} %collective-permute-done.35.refs_0_), channel_id=1, source_target_pairs={{0,2},{1,3},{2,0},{3,1},{4,6},{5,7},{6,4},{7,5},{8,10},{9,11},{10,... | collective-permute-start | bytes 540680 | tf_op jit(solution)/shard_map/ppermute | solution.py:87
  78.4 34.2 %collective-permute-start.41 = (bf16[704,128]{1,0:T(8,128)(2,1)S(1)}, bf16[704,128]{1,0:T(8,128)(2,1)S(1)}, u32[]{:S(2)}, u32[]{:S(2)}) collective-permute-start(bf16[704,128]{1,0:T(8,128)(2,1)S(1)} %collective-permute-done.40.refs_2_), channel_id=1, source_target_pairs={{0,1},{1,0},{2,3},{3,2},{4,5},{5,4},{6,7},{7,6},{8,9},{9,8},{10,11... | collective-permute-start | bytes 540680 | tf_op jit(solution)/shard_map/ppermute | solution.py:91
  83.5 29.7 %collective-permute-start.33 = (bf16[704,128]{1,0:T(8,128)(2,1)S(1)}, bf16[704,128]{1,0:T(8,128)(2,1)S(1)}, u32[]{:S(2)}, u32[]{:S(2)}) collective-permute-start(bf16[704,128]{1,0:T(8,128)(2,1)S(1)} %collective-permute-done.31.refs_0_), channel_id=1, source_target_pairs={{0,2},{1,3},{2,0},{3,1},{4,6},{5,7},{6,4},{7,5},{8,10},{9,11},{10,... | collective-permute-start | bytes 540680 | tf_op jit(solution)/shard_map/ppermute | solution.py:87
  84.1 32.1 %collective-permute-start.36 = (bf16[704,128]{1,0:T(8,128)(2,1)S(1)}, bf16[704,128]{1,0:T(8,128)(2,1)S(1)}, u32[]{:S(2)}, u32[]{:S(2)}) collective-permute-start(bf16[704,128]{1,0:T(8,128)(2,1)S(1)} %collective-permute-done.35.refs_0_), channel_id=1, source_target_pairs={{0,1},{1,0},{2,3},{3,2},{4,5},{5,4},{6,7},{7,6},{8,9},{9,8},{10,11... | collective-permute-start | bytes 540680 | tf_op jit(solution)/shard_map/ppermute | solution.py:91
  89.1 27.6 %collective-permute-start.29 = (bf16[704,128]{1,0:T(8,128)(2,1)S(1)}, bf16[704,128]{1,0:T(8,128)(2,1)S(1)}, u32[]{:S(2)}, u32[]{:S(2)}) collective-permute-start(bf16[704,128]{1,0:T(8,128)(2,1)S(1)} %collective-permute-done.27.refs_0_), channel_id=1, source_target_pairs={{0,2},{1,3},{2,0},{3,1},{4,6},{5,7},{6,4},{7,5},{8,10},{9,11},{10,... | collective-permute-start | bytes 540680 | tf_op jit(solution)/shard_map/ppermute | solution.py:87
  90.1 26.7 %collective-permute-start.38 = (bf16[704,128]{1,0:T(8,128)(2,1)S(1)}, bf16[704,128]{1,0:T(8,128)(2,1)S(1)}, u32[]{:S(2)}, u32[]{:S(2)}) collective-permute-start(bf16[704,128]{1,0:T(8,128)(2,1)S(1)} %collective-permute-done.37.refs_2_), channel_id=1, source_target_pairs={{0,1},{1,0},{2,3},{3,2},{4,5},{5,4},{6,7},{7,6},{8,9},{9,8},{10,11... | collective-permute-start | bytes 540680 | tf_op jit(solution)/shard_map/ppermute | solution.py:91
  126.5 10.8 %collective-permute-start.42 = (bf16[1408,128]{1,0:T(8,128)(2,1)S(1)}, bf16[1408,128]{1,0:T(8,128)(2,1)S(1)}, u32[]{:S(2)}, u32[]{:S(2)}) collective-permute-start(bf16[1408,128]{1,0:T(8,128)(2,1)S(1)} %get-tuple-element.44), channel_id=1, source_target_pairs={{0,16},{16,0},{1,17},{17,1},{2,18},{18,2},{3,19},{19,3},{4,20},{20... | collective-permute-start | bytes 1081352 | tf_op jit(solution)/shard_map/ppermute | solution.py:95
  146.5 11.3 %collective-permute-start.43 = (bf16[2,704,128]{2,1,0:T(8,128)(2,1)S(1)}, bf16[2,704,128]{2,1,0:T(8,128)(2,1)S(1)}, u32[]{:S(2)}, u32[]{:S(2)}) collective-permute-start(bf16[2,704,128]{2,1,0:T(8,128)(2,1)S(1)} %get-tuple-element.46), channel_id=1, source_target_pairs={{0,1},{1,0},{2,3},{3,2},{4,5},{5,4},{6,7},{7,6},{8,9},{9,8},{10,11... | collective-permute-start | bytes 1081352 | tf_op jit(solution)/shard_map/ppermute | solution.py:91
  157.8 7.5 %collective-permute-start.44 = (bf16[704,128]{1,0:T(8,128)(2,1)S(1)}, bf16[704,128]{1,0:T(8,128)(2,1)S(1)}, u32[]{:S(2)}, u32[]{:S(2)}) collective-permute-start(bf16[704,128]{1,0:T(8,128)(2,1)S(1)} %fusion.14), channel_id=1, source_target_pairs={{0,2},{1,3},{2,0},{3,1},{4,6},{5,7},{6,4},{7,5},{8,10},{9,11},{10,... | collective-permute-start | bytes 540680 | tf_op jit(solution)/shard_map/ppermute | solution.py:87
  159.0 10.1 %collective-permute-start.47 = (bf16[704,128]{1,0:T(8,128)(2,1)S(1)}, bf16[704,128]{1,0:T(8,128)(2,1)S(1)}, u32[]{:S(2)}, u32[]{:S(2)}) collective-permute-start(bf16[704,128]{1,0:T(8,128)(2,1)S(1)} %fusion.15), channel_id=1, source_target_pairs={{0,2},{1,3},{2,0},{3,1},{4,6},{5,7},{6,4},{7,5},{8,10},{9,11},{10,... | collective-permute-start | bytes 540680 | tf_op jit(solution)/shard_map/ppermute | solution.py:87
  160.1 12.9 %collective-permute-start.50 = (bf16[704,128]{1,0:T(8,128)(2,1)S(1)}, bf16[704,128]{1,0:T(8,128)(2,1)S(1)}, u32[]{:S(2)}, u32[]{:S(2)}) collective-permute-start(bf16[704,128]{1,0:T(8,128)(2,1)S(1)} %fusion.16), channel_id=1, source_target_pairs={{0,2},{1,3},{2,0},{3,1},{4,6},{5,7},{6,4},{7,5},{8,10},{9,11},{10,... | collective-permute-start | bytes 540680 | tf_op jit(solution)/shard_map/ppermute | solution.py:87
  161.3 14.7 %collective-permute-start.53 = (bf16[704,128]{1,0:T(8,128)(2,1)S(1)}, bf16[704,128]{1,0:T(8,128)(2,1)S(1)}, u32[]{:S(2)}, u32[]{:S(2)}) collective-permute-start(bf16[704,128]{1,0:T(8,128)(2,1)S(1)} %fusion.17), channel_id=1, source_target_pairs={{0,2},{1,3},{2,0},{3,1},{4,6},{5,7},{6,4},{7,5},{8,10},{9,11},{10,... | collective-permute-start | bytes 540680 | tf_op jit(solution)/shard_map/ppermute | solution.py:87
  165.4 13.3 %collective-permute-start.45 = (bf16[704,128]{1,0:T(8,128)(2,1)S(1)}, bf16[704,128]{1,0:T(8,128)(2,1)S(1)}, u32[]{:S(2)}, u32[]{:S(2)}) collective-permute-start(bf16[704,128]{1,0:T(8,128)(2,1)S(1)} %fusion.3), channel_id=1, source_target_pairs={{0,8},{1,9},{2,10},{3,11},{4,12},{5,13},{6,14},{7,15},{8,0},{9,1},... | collective-permute-start | bytes 540680 | tf_op jit(solution)/shard_map/ppermute | solution.py:81
  169.3 9.4 %collective-permute-start.48 = (bf16[704,128]{1,0:T(8,128)(2,1)S(1)}, bf16[704,128]{1,0:T(8,128)(2,1)S(1)}, u32[]{:S(2)}, u32[]{:S(2)}) collective-permute-start(bf16[704,128]{1,0:T(8,128)(2,1)S(1)} %fusion.2), channel_id=1, source_target_pairs={{0,4},{1,5},{2,6},{3,7},{4,8},{5,9},{6,10},{7,11},{8,12},{9,13},{1... | collective-permute-start | bytes 540680 | tf_op jit(solution)/shard_map/ppermute | solution.py:81
  173.1 8.9 %collective-permute-start.51 = (bf16[704,128]{1,0:T(8,128)(2,1)S(1)}, bf16[704,128]{1,0:T(8,128)(2,1)S(1)}, u32[]{:S(2)}, u32[]{:S(2)}) collective-permute-start(bf16[704,128]{1,0:T(8,128)(2,1)S(1)} %fusion.1), channel_id=1, source_target_pairs={{0,12},{1,13},{2,14},{3,15},{4,0},{5,1},{6,2},{7,3},{8,4},{9,5},{1... | collective-permute-start | bytes 540680 | tf_op jit(solution)/shard_map/ppermute | solution.py:81
  182.9 7.2 %collective-permute-start.57 = (bf16[704,128]{1,0:T(8,128)(2,1)S(1)}, bf16[704,128]{1,0:T(8,128)(2,1)S(1)}, u32[]{:S(2)}, u32[]{:S(2)}) collective-permute-start(bf16[704,128]{1,0:T(8,128)(2,1)S(1)} %get-tuple-element.64.refs_0_), channel_id=1, source_target_pairs={{0,12},{1,13},{2,14},{3,15},{4,0},{5,1},{6,2},{7,3},{8,4},{9,5},{1... | collective-permute-start | bytes 540680 | tf_op jit(solution)/shard_map/ppermute | solution.py:81
  184.2 16.4 %collective-permute-start.61 = (bf16[704,128]{1,0:T(8,128)(2,1)S(1)}, bf16[704,128]{1,0:T(8,128)(2,1)S(1)}, u32[]{:S(2)}, u32[]{:S(2)}) collective-permute-start(bf16[704,128]{1,0:T(8,128)(2,1)S(1)} %get-tuple-element.64.refs_0_), channel_id=1, source_target_pairs={{0,8},{1,9},{2,10},{3,11},{4,12},{5,13},{6,14},{7,15},{8,0},{9,1},... | collective-permute-start | bytes 540680 | tf_op jit(solution)/shard_map/ppermute | solution.py:81
  185.0 16.5 %collective-permute-start.65 = (bf16[704,128]{1,0:T(8,128)(2,1)S(1)}, bf16[704,128]{1,0:T(8,128)(2,1)S(1)}, u32[]{:S(2)}, u32[]{:S(2)}) collective-permute-start(bf16[704,128]{1,0:T(8,128)(2,1)S(1)} %get-tuple-element.64.refs_0_), channel_id=1, source_target_pairs={{0,4},{1,5},{2,6},{3,7},{4,8},{5,9},{6,10},{7,11},{8,12},{9,13},{1... | collective-permute-start | bytes 540680 | tf_op jit(solution)/shard_map/ppermute | solution.py:81
  185.9 16.7 %collective-permute-start.55 = (bf16[704,128]{1,0:T(8,128)(2,1)S(1)}, bf16[704,128]{1,0:T(8,128)(2,1)S(1)}, u32[]{:S(2)}, u32[]{:S(2)}) collective-permute-start(bf16[704,128]{1,0:T(8,128)(2,1)S(1)} %get-tuple-element.64.refs_0_), channel_id=1, source_target_pairs={{0,2},{1,3},{2,0},{3,1},{4,6},{5,7},{6,4},{7,5},{8,10},{9,11},{10,... | collective-permute-start | bytes 540680 | tf_op jit(solution)/shard_map/ppermute | solution.py:87
  187.0 15.6 %collective-permute-start.54 = (bf16[704,128]{1,0:T(8,128)(2,1)S(1)}, bf16[704,128]{1,0:T(8,128)(2,1)S(1)}, u32[]{:S(2)}, u32[]{:S(2)}) collective-permute-start(bf16[704,128]{1,0:T(8,128)(2,1)S(1)} %get-tuple-element.64.refs_0_), channel_id=1, source_target_pairs={{0,1},{1,0},{2,3},{3,2},{4,5},{5,4},{6,7},{7,6},{8,9},{9,8},{10,11... | collective-permute-start | bytes 540680 | tf_op jit(solution)/shard_map/ppermute | solution.py:91
  190.1 13.1 %collective-permute-start.59 = (bf16[704,128]{1,0:T(8,128)(2,1)S(1)}, bf16[704,128]{1,0:T(8,128)(2,1)S(1)}, u32[]{:S(2)}, u32[]{:S(2)}) collective-permute-start(bf16[704,128]{1,0:T(8,128)(2,1)S(1)} %collective-permute-done.57.refs_4_), channel_id=1, source_target_pairs={{0,2},{1,3},{2,0},{3,1},{4,6},{5,7},{6,4},{7,5},{8,10},{9,11},{10,... | collective-permute-start | bytes 540680 | tf_op jit(solution)/shard_map/ppermute | solution.py:87
  201.4 8.2 %collective-permute-start.67 = (bf16[704,128]{1,0:T(8,128)(2,1)S(1)}, bf16[704,128]{1,0:T(8,128)(2,1)S(1)}, u32[]{:S(2)}, u32[]{:S(2)}) collective-permute-start(bf16[704,128]{1,0:T(8,128)(2,1)S(1)} %collective-permute-done.65.refs_12_), channel_id=1, source_target_pairs={{0,2},{1,3},{2,0},{3,1},{4,6},{5,7},{6,4},{7,5},{8,10},{9,11},{10,... | collective-permute-start | bytes 540680 | tf_op jit(solution)/shard_map/ppermute | solution.py:87
  202.6 7.5 %collective-permute-start.58 = (bf16[704,128]{1,0:T(8,128)(2,1)S(1)}, bf16[704,128]{1,0:T(8,128)(2,1)S(1)}, u32[]{:S(2)}, u32[]{:S(2)}) collective-permute-start(bf16[704,128]{1,0:T(8,128)(2,1)S(1)} %collective-permute-done.57.refs_4_), channel_id=1, source_target_pairs={{0,1},{1,0},{2,3},{3,2},{4,5},{5,4},{6,7},{7,6},{8,9},{9,8},{10,11... | collective-permute-start | bytes 540680 | tf_op jit(solution)/shard_map/ppermute | solution.py:91
  224.5 11.5 %collective-permute-start.70 = (bf16[2,352,128]{2,1,0:T(8,128)(2,1)S(1)}, bf16[2,352,128]{2,1,0:T(8,128)(2,1)S(1)}, u32[]{:S(2)}, u32[]{:S(2)}) collective-permute-start(bf16[2,352,128]{2,1,0:T(8,128)(2,1)S(1)} %get-tuple-element.57), channel_id=1, source_target_pairs={{0,1},{1,0},{2,3},{3,2},{4,5},{5,4},{6,7},{7,6},{8,9},{9,8},{10,11... | collective-permute-start | bytes 540680 | tf_op jit(solution)/shard_map/ppermute | solution.py:91
  238.3 7.2 %collective-permute-start.77 = (bf16[352,128]{1,0:T(8,128)(2,1)S(1)}, bf16[352,128]{1,0:T(8,128)(2,1)S(1)}, u32[]{:S(2)}, u32[]{:S(2)}) collective-permute-start(bf16[352,128]{1,0:T(8,128)(2,1)S(1)} %fusion.24), channel_id=1, source_target_pairs={{0,2},{1,3},{2,0},{3,1},{4,6},{5,7},{6,4},{7,5},{8,10},{9,11},{10,... | collective-permute-start | bytes 270344 | tf_op jit(solution)/shard_map/ppermute | solution.py:87
  239.2 8.3 %collective-permute-start.80 = (bf16[352,128]{1,0:T(8,128)(2,1)S(1)}, bf16[352,128]{1,0:T(8,128)(2,1)S(1)}, u32[]{:S(2)}, u32[]{:S(2)}) collective-permute-start(bf16[352,128]{1,0:T(8,128)(2,1)S(1)} %fusion.25), channel_id=1, source_target_pairs={{0,2},{1,3},{2,0},{3,1},{4,6},{5,7},{6,4},{7,5},{8,10},{9,11},{10,... | collective-permute-start | bytes 270344 | tf_op jit(solution)/shard_map/ppermute | solution.py:87
  241.6 9.2 %collective-permute-start.72 = (bf16[352,128]{1,0:T(8,128)(2,1)S(1)}, bf16[352,128]{1,0:T(8,128)(2,1)S(1)}, u32[]{:S(2)}, u32[]{:S(2)}) collective-permute-start(bf16[352,128]{1,0:T(8,128)(2,1)S(1)} %fusion.21), channel_id=1, source_target_pairs={{0,8},{1,9},{2,10},{3,11},{4,12},{5,13},{6,14},{7,15},{8,0},{9,1},... | collective-permute-start | bytes 270344 | tf_op jit(solution)/shard_map/ppermute | solution.py:81
  243.6 7.2 %collective-permute-start.75 = (bf16[352,128]{1,0:T(8,128)(2,1)S(1)}, bf16[352,128]{1,0:T(8,128)(2,1)S(1)}, u32[]{:S(2)}, u32[]{:S(2)}) collective-permute-start(bf16[352,128]{1,0:T(8,128)(2,1)S(1)} %fusion.20), channel_id=1, source_target_pairs={{0,4},{1,5},{2,6},{3,7},{4,8},{5,9},{6,10},{7,11},{8,12},{9,13},{1... | collective-permute-start | bytes 270344 | tf_op jit(solution)/shard_map/ppermute | solution.py:81
  (54 other events, 387.0 us)

commit v3 on v1

--- a/solution.py
+++ b/solution.py
@@ -2,6 +2,7 @@
 
 import jax
 import jax.numpy as jnp
+import numpy as np
 from jax import lax
 from jax.experimental import pallas as pl
 from jax.experimental.pallas import tpu as pltpu
@@ -15,7 +16,7 @@
 HIGHEST_PRECISION = lax.Precision.HIGHEST
 VMEM = pl.BlockSpec(memory_space=pltpu.VMEM)
 SMEM = pl.BlockSpec(memory_space=pltpu.SMEM)
-VMEM_LIMIT = 48 * 1024 * 1024
+VMEM_LIMIT = 32 * 1024 * 1024
 
 
 def transposed_product(matrix, vector):
@@ -95,18 +96,79 @@
     return lax.ppermute(value, "sub", [(0, 1), (1, 0)])
 
 
+def after(value, *others):
+    return lax.optimization_barrier((value, *others))[0]
+
+
 def gather_pieces(own, nz):
-    along_z = [own] + [z_shift(own, -k, nz) for k in range(1, nz)]
-    pieces = []
-    for held in along_z:
-        across = x_swap(held, nz)
-        pieces += [held, c_swap(held, nz), across, c_swap(across, nz)]
-    return pieces
+    order = near_first(nz)
+    held = {0: own}
+    for k in order[1:]:
+        held[k] = z_shift(own, -k, nz)
+    pieces = {}
+    for k in order:
+        across = x_swap(held[k], nz)
+        pieces[k] = [held[k], c_swap(held[k], nz), across, c_swap(across, nz)]
+    return [piece for k in range(nz) for piece in pieces[k]]
+
+
+def by_arrival(items, nz):
+    group = NX * NC
+    return [items[k * group + i] for k in near_first(nz) for i in range(group)]
+
+
+def near_first(nz):
+    return sorted(range(nz), key=lambda k: min(k, nz - k))
+
+
+def gather_product(place, own, matrix, nz):
+    group = NX * NC
+    at = Spots(nz)
+    pieces = gather_pieces(own, nz)
+    acc = acc_b = jnp.zeros((matrix.shape[0], own.shape[1]), F32)
+    for k in near_first(nz):
+        block = pieces[k * group : (k + 1) * group]
+        acc, acc_b = unit_product(place, [at.blocks + k], at.near, [block], matrix, acc)
+    return acc, acc_b
+
+
+def ring_step(value, way, nz):
+    count = NX * nz
+    chip = lambda p: (p * NX if p < nz else (count - 1 - p) * NX + 1)
+    pairs = [
+        (chip(p) * NC + c, chip((p + way) % count) * NC + c)
+        for p in range(count)
+        for c in range(NC)
+    ]
+    return lax.ppermute(value, "front", pairs)
+
+
+def ring_product(place, own, matrix, nz):
+    count = NX * nz
+    at = Spots(nz)
+    acc = acc_b = jnp.zeros((matrix.shape[0], own.shape[1]), F32)
+    held = {0: own}
+    for step in range(nz + 1):
+        if step:
+            held = {j: after(piece, acc) for j, piece in held.items()}
+        units = [[piece, c_swap(piece, nz)] for piece in held.values()]
+        following = {}
+        if step < nz:
+            following[(-step - 1) % count] = ring_step(held[(-step) % count], 1, nz)
+            if step < nz - 1:
+                following[step + 1] = ring_step(held[step], -1, nz)
+        acc, acc_b = unit_product(place, [at.ring + j for j in held], at.core, units, matrix, acc)
+        held = following
+    return acc, acc_b
+
+
+def far_first(nz):
+    return near_first(nz)[::-1]
 
 
 def scatter_sum(keep, send, nz):
     total = None
-    for k in list(range(1, nz)) + [0]:
+    for k in far_first(nz):
         arrived = c_swap(send[k], nz)
         near = keep[k][0].astype(F32) + arrived[0].astype(F32)
         far = keep[k][1].astype(F32) + arrived[1].astype(F32)
@@ -118,16 +180,30 @@
 
 
 def places(nz):
-    me = lax.axis_index("front")
-    z, x, c = me // (NX * NC), (me // NC) % NX, me % NC
-    return jnp.stack(
-        [
-            (((z + k) % nz) * NX + (x ^ xr)) * NC + (c ^ cr)
-            for k in range(nz)
-            for xr in range(NX)
-            for cr in range(NC)
-        ]
-    ).astype(jnp.int32)
+    count = NX * nz
+    table = []
+    for me in range(count * NC):
+        z, x, c = me // (NX * NC), (me // NC) % NX, me % NC
+        near = [(x ^ xr) * NC + (c ^ cr) for xr in range(NX) for cr in range(NC)]
+        blocks = [(z + k) % nz for k in range(nz)]
+        row = [b * NX * NC + i for b in blocks for i in near]
+        spot = z if x == 0 else count - 1 - z
+        for j in range(count):
+            p = (spot + j) % count
+            row.append(p * NX if p < nz else (count - 1 - p) * NX + 1)
+        table.append(row + blocks + near + [c, 1 - c])
+    return lax.dynamic_index_in_dim(
+        jnp.asarray(np.array(table, np.int32)), lax.axis_index("front"), 0, keepdims=False
+    )
+
+
+class Spots:
+    def __init__(self, nz):
+        group = NX * NC
+        self.ring = nz * group
+        self.blocks = self.ring + NX * nz
+        self.near = self.blocks + nz
+        self.core = self.near + group
 
 
 def assemble(place, pieces, whole):
@@ -148,97 +224,168 @@
                 ].astype(out.dtype)
 
 
-def forward_kernel(count, place, *refs):
-    pieces, (matrix, out, out_b, whole) = refs[:count], refs[count:]
-    step = pl.program_id(0)
-    depth = matrix.shape[1]
-
-    @pl.when(step == 0)
+def row_step(rows):
+    for step in (352, 256, 128):
+        if rows % step == 0:
+            return step
+    return rows
+
+
+def unit_kernel(units, count, spots, place, *refs):
+    pieces, (matrix, acc, out, out_b, cols) = refs[: units * count], refs[units * count :]
+    rows = pieces[0].shape[0]
+    unit = pl.program_id(1)
+
+    @pl.when((pl.program_id(0) == 0) & (unit == 0))
     def _():
-        assemble(place, pieces, whole)
-        out[...] = jnp.zeros_like(out)
-
-    cols = whole[pl.ds(pl.multiple_of(step * depth, depth), depth), :]
-    out[...] += jnp.dot(matrix[...], cols, preferred_element_type=F32)
-
-    @pl.when(step == pl.num_programs(0) - 1)
+        for i, piece in enumerate(pieces):
+            at = place[spots + i % count]
+            cols[i // count, pl.ds(pl.multiple_of(at * rows, rows), rows), :] = piece[...]
+
+    product = jnp.dot(matrix[...], cols[unit], preferred_element_type=F32)
+
+    @pl.when(unit == 0)
+    def _():
+        out[...] = acc[...] + product
+
+    @pl.when(unit > 0)
+    def _():
+        out[...] += product
+
+    @pl.when(unit == units - 1)
     def _():
         out_b[...] = out[...].astype(BF16)
 
 
-def forward_product(place, pieces, matrix, depth):
-    rows, width = matrix.shape
-    n = pieces[0].shape[1]
-    whole_spec = lambda shape: pl.BlockSpec(shape, lambda i, *_: (0,) * len(shape))
+def unit_product(place, blocks, spots, units, matrix, acc):
+    rows = matrix.shape[0]
+    part, n = units[0][0].shape
+    count = len(units[0])
+    depth = count * part
+    step = row_step(rows)
+    first, then = blocks[0], blocks[-1]
     return pl.pallas_call(
-        functools.partial(forward_kernel, len(pieces)),
-        out_shape=(
-            jax.ShapeDtypeStruct((rows, n), F32),
-            jax.ShapeDtypeStruct((rows, n), BF16),
-        ),
+        functools.partial(unit_kernel, len(units), count, spots),
+        out_shape=(jax.ShapeDtypeStruct((rows, n), F32), jax.ShapeDtypeStruct((rows, n), BF16)),
         grid_spec=pltpu.PrefetchScalarGridSpec(
             num_scalar_prefetch=1,
-            grid=(width // depth,),
-            in_specs=[whole_spec(p.shape) for p in pieces]
-            + [pl.BlockSpec((rows, depth), lambda i, *_: (0, i))],
-            out_specs=(whole_spec((rows, n)), whole_spec((rows, n))),
-            scratch_shapes=[pltpu.VMEM((width, n), BF16)],
+            grid=(rows // step, len(units)),
+            in_specs=[pl.BlockSpec((part, n), lambda i, u, place: (0, 0))] * (count * len(units))
+            + [
+                pl.BlockSpec(
+                    (step, depth),
+                    lambda i, u, place: (i, jnp.where(u == 0, place[first], place[then])),
+                ),
+                pl.BlockSpec((step, n), lambda i, u, place: (i, 0)),
+            ],
+            out_specs=[pl.BlockSpec((step, n), lambda i, u, place: (i, 0))] * 2,
+            scratch_shapes=[pltpu.VMEM((len(units), depth, n), BF16)],
         ),
         compiler_params=pltpu.CompilerParams(vmem_limit_bytes=VMEM_LIMIT),
         cost_estimate=pl.CostEstimate(
-            flops=2 * rows * width * n, bytes_accessed=2 * rows * width, transcendentals=0
+            flops=2 * rows * depth * n * len(units),
+            bytes_accessed=2 * rows * depth * len(units),
+            transcendentals=0,
         ),
-        name="forward_product",
-    )(place, *pieces, matrix)
-
-
-def backward_kernel(nz, subtract, place, own, arrived, base, matrix, *refs):
-    keep, send, (vector, whole) = refs[:nz], refs[nz : 2 * nz], refs[2 * nz :]
+        name="unit_product",
+    )(place, *[piece for unit in units for piece in unit], in_hbm(matrix), acc)
+
+
+def backward_kernel(k, place, vector, matrix, keep, send, whole):
     step = pl.program_id(0)
     width = matrix.shape[1]
-
-    @pl.when(step == 0)
-    def _():
-        total = own[...] + arrived[...].astype(F32)
-        if subtract:
-            total = base[...] - total
-        vector[...] = total.T.astype(BF16)
-
+    part = keep.shape[1]
     product = jnp.dot(vector[...], matrix[...], preferred_element_type=F32)
     whole[pl.ds(pl.multiple_of(step * width, width), width), :] = product.T
 
     @pl.when(step == pl.num_programs(0) - 1)
     def _():
-        distribute(place, whole, keep, send)
-
-
-def backward_product(place, own, arrived, base, matrix, block, nz):
+        for xr in range(NX):
+            for cr, out in ((0, keep), (1, send)):
+                at = place[(k * NX + xr) * NC + cr] % (NX * NC)
+                out[xr] = whole[pl.ds(pl.multiple_of(at * part, part), part), :].astype(out.dtype)
+
+
+def backward_block(place, k, vector, matrix, nz):
     rows, width = matrix.shape
-    n = own.shape[1]
-    part = width // (nz * NX * NC)
-    subtract = base is not None
-    if base is None:
-        base = jnp.zeros((8, 128), F32)
-    whole_spec = lambda shape: pl.BlockSpec(shape, lambda i, *_: (0,) * len(shape))
-    outs = pl.pallas_call(
-        functools.partial(backward_kernel, nz, subtract),
-        out_shape=[jax.ShapeDtypeStruct((NX, part, n), F32)] * nz
-        + [jax.ShapeDtypeStruct((NX, part, n), BF16)] * nz,
+    n = vector.shape[0]
+    depth = width // nz
+    part = depth // (NX * NC)
+    step = depth // 2 if depth // 2 % 128 == 0 else depth // 11 if depth % (11 * 128) == 0 else depth
+    steps = depth // step
+    return pl.pallas_call(
+        functools.partial(backward_kernel, k),
+        out_shape=[
+            jax.ShapeDtypeStruct((NX, part, n), F32),
+            jax.ShapeDtypeStruct((NX, part, n), BF16),
+        ],
         grid_spec=pltpu.PrefetchScalarGridSpec(
             num_scalar_prefetch=1,
-            grid=(width // block,),
-            in_specs=[whole_spec(own.shape), whole_spec(own.shape), whole_spec(base.shape)]
-            + [pl.BlockSpec((rows, block), lambda i, *_: (0, i))],
-            out_specs=[whole_spec((NX, part, n))] * (2 * nz),
-            scratch_shapes=[pltpu.VMEM((n, rows), BF16), pltpu.VMEM((width, n), F32)],
+            grid=(steps,),
+            in_specs=[
+                pl.BlockSpec((n, rows), lambda i, *_: (0, 0)),
+                pl.BlockSpec(
+                    (rows, step),
+                    lambda i, place: (0, place[k * NX * NC] // (NX * NC) * steps + i),
+                ),
+            ],
+            out_specs=[pl.BlockSpec((NX, part, n), lambda i, *_: (0, 0, 0))] * 2,
+            scratch_shapes=[pltpu.VMEM((depth, n), F32)],
         ),
         compiler_params=pltpu.CompilerParams(vmem_limit_bytes=VMEM_LIMIT),
         cost_estimate=pl.CostEstimate(
-            flops=2 * rows * width * n, bytes_accessed=2 * rows * width, transcendentals=0
+            flops=2 * rows * depth * n, bytes_accessed=2 * rows * depth, transcendentals=0
         ),
-        name="backward_product",
-    )(place, own, arrived, base, matrix)
-    return outs[:nz], outs[nz:]
+        name="backward_block",
+    )(place, vector, in_hbm(matrix))
+
+
+def product_scatter(place, vector, matrix, nz):
+    order = far_first(nz)
+    blocks, stage_c, stage_x, stage_z = [], [], [], []
+    for i in range(nz + 2):
+        started = []
+        if 0 <= i - 2 < nz:
+            keep, arrived = blocks[i - 2][0], stage_c[i - 2]
+            far = (keep[1] + arrived[1].astype(F32)).astype(BF16)
+            started.append(far)
+            stage_x.append(x_swap(far, nz))
+        if 0 <= i - 3 < nz - 1:
+            partial = leave(blocks[i - 3][0], stage_c[i - 3], stage_x[i - 3])
+            started.append(partial)
+            stage_z.append(z_shift(partial, order[i - 3], nz).astype(F32))
+        if i < nz:
+            tied = after(vector, *started) if started else vector
+            blocks.append(backward_block(place, order[i], tied, matrix, nz))
+            stage_c.append(c_swap(blocks[i][1], nz))
+    total = blocks[-1][0][0] + stage_c[-1][0].astype(F32) + stage_x[-1].astype(F32)
+    for partial in stage_z:
+        total = total + partial
+    return total
+
+
+def leave(keep, arrived, across):
+    partial = keep[0] + arrived[0].astype(F32) + across.astype(F32)
+    return partial.astype(BF16)
+
+
+def turn_kernel(subtract, own, arrived, base, vector):
+    total = own[...] + arrived[...].astype(F32)
+    if subtract:
+        total = base[...] - total
+    vector[...] = total.T.astype(BF16)
+
+
+def turn(own, arrived, base=None):
+    rows, n = own.shape
+    subtract = base is not None
+    return pl.pallas_call(
+        functools.partial(turn_kernel, subtract),
+        out_shape=jax.ShapeDtypeStruct((n, rows), BF16),
+        in_specs=[VMEM] * 3,
+        out_specs=VMEM,
+        name="turn",
+    )(own, arrived, base if subtract else jnp.zeros((8, n), F32))
 
 
 def push_kernel(nz, place, block, own, arrived, coupling, *refs):
@@ -270,9 +417,9 @@
     return outs[0], outs[1 : nz + 1], outs[nz + 1 :]
 
 
-def pull_kernel(count, place, block, *refs):
-    pieces, (coupling, out, out_b, whole, picked) = refs[:count], refs[count:]
-    assemble(place, pieces, whole)
+def pull_kernel(order, place, block, *refs):
+    pieces, (coupling, out, out_b, whole, picked) = refs[: len(order)], refs[len(order) :]
+    assemble([place[i] for i in order], pieces, whole)
     for j in range(coupling.shape[1] // RB):
         start = pl.multiple_of(block[j] * RB, RB)
         picked[j * RB : (j + 1) * RB, :] = whole[pl.ds(start, RB), :]
@@ -280,11 +427,11 @@
     out_b[...] = out[...].astype(BF16)
 
 
-def pull_product(place, block, pieces, coupling):
+def pull_product(place, block, pieces, coupling, nz):
     rows, width = coupling.shape
     part, n = pieces[0].shape
     return pl.pallas_call(
-        functools.partial(pull_kernel, len(pieces)),
+        functools.partial(pull_kernel, by_arrival(range(len(pieces)), nz)),
         out_shape=(
             jax.ShapeDtypeStruct((rows, n), F32),
             jax.ShapeDtypeStruct((rows, n), BF16),
@@ -300,11 +447,8 @@
     )(place, block, *pieces, coupling)
 
 
-def column_block(width):
-    for parts in (8, 4, 2, 1):
-        if width % (parts * 128) == 0 and width // parts >= 1024:
-            return width // parts
-    return width
+def in_hbm(matrix):
+    return pltpu.with_memory_space_constraint(matrix, pltpu.HBM)
 
 
 def two_level_body(rhs_root, rhs_level, root_inverse, level_inverse, coupling_t, coupling_rows):
@@ -313,34 +457,22 @@
     place = places(nz)
     block = coupling_rows[0] % (width // RB)
 
-    level_pieces = gather_pieces(rhs_level.astype(BF16), nz)
-    own, own_b = forward_product(
-        place, level_pieces, level_inverse, column_block(level_inverse.shape[1])
-    )
+    own, own_b = gather_product(place, rhs_level.astype(BF16), level_inverse, nz)
     forward_level, keep, send = push_product(
         place, block, own, sub_swap(own_b), coupling_t, width, nz
     )
     shifted = rhs_root - scatter_sum(keep, send, nz)
 
-    root_pieces = gather_pieces(shifted.astype(BF16), nz)
-    own, own_b = forward_product(place, root_pieces, root_inverse, column_block(width))
-    keep, send = backward_product(
-        place, own, sub_swap(own_b), None, root_inverse, column_block(width), nz
-    )
-    root_potential = scatter_sum(keep, send, nz)
+    own, own_b = ring_product(place, shifted.astype(BF16), root_inverse, nz)
+    root_potential = product_scatter(place, turn(own, sub_swap(own_b)), root_inverse, nz)
 
     potential_pieces = gather_pieces(root_potential.astype(BF16), nz)
-    own, own_b = pull_product(place, block, potential_pieces, coupling_t)
-    keep, send = backward_product(
-        place,
-        own,
-        sub_swap(own_b),
-        forward_level,
-        level_inverse,
-        column_block(level_inverse.shape[1]),
-        nz,
-    )
-    level_potential = scatter_sum(keep, send, nz)
+    own, own_b = pull_product(
+        place, block, by_arrival(potential_pieces, nz), coupling_t, nz
+    )
+    level_potential = product_scatter(
+        place, turn(own, sub_swap(own_b), forward_level), level_inverse, nz
+    )
     return (root_potential, level_potential)
 
 
@@ -350,6 +482,8 @@
         and lax.axis_size("front") % (2 * NX * NC) == 0
         and all(a.shape[0] % 16 == 0 for a in (rhs_root, rhs_level, root_inverse, level_inverse))
         and all(a.shape[1] % 128 == 0 for a in (rhs_root, root_inverse, level_inverse, coupling_t))
+        and NC * rhs_root.shape[0] % 128 == 0
+        and NX * NC * rhs_level.shape[0] % 128 == 0
         and root_inverse.size * 2 <= 34 * 1024 * 1024
     )
     chosen = two_level_body if fits else general_body

time: 224 us -> 264 us (1.18)
  Pallas kernels: 47.2 us -> 108 us
  starting transfers between devices: 86.6 us -> 57.6 us
  local copies, waits for them, and re-layouts: 0.11 us -> 5.67 us
  waiting for transfers between devices: 84.5 us -> 87.2 us
    pallas_call x5 -> x20, Pallas kernels: 44.4 us -> 106 us  [the longest x8 51.5 us: backward_block(): pl.pallas_call(functools.partial(backward_kernel, k), out_shape=[jax.Shap...]
    ppermute x18 -> x15, starting transfers between devices: 47.2 us -> 17.7 us  [z_shift(): lax.ppermute(value, 'front', [(i, (i + shift * width) % count) for i in r...]
    ppermute x0 -> x7, starting transfers between devices: none -> 7.41 us  [ring_step(): return lax.ppermute(value, 'front', pairs)]
    ppermute x24 -> x20, starting transfers between devices: 27.9 us -> 21.1 us  [x_swap(): lax.ppermute(value, 'front', [(i, i ^ NC) for i in range(nz * NX * NC)])]
    unnamed x6 -> x20, local copies, waits for them, and re-layouts: 0.02 us -> 4.28 us
    ppermute x18 -> x15, waiting for transfers between devices: 30.8 us -> 32.9 us  [z_shift(): lax.ppermute(value, 'front', [(i, (i + shift * width) % count) for i in r...]
    ppermute x24 -> x20, waiting for transfers between devices: 28.9 us -> 30.9 us  [x_swap(): lax.ppermute(value, 'front', [(i, i ^ NC) for i in range(nz * NX * NC)])]
  transfers between devices with their start and end apart: 81 -> 81, of which waited for: 32 -> 30; matrix products, arithmetic and copies ran while one was open for 0% -> 1% of each run, Pallas kernels for 0% -> 30%
where the time goes in v3:
time: 264 us; the launch traced here: 263 us
  Pallas kernels  108 us (41%)
  waiting for transfers between devices  87.2 us (33%)
  starting transfers between devices  57.6 us (22%)
  local copies, waits for them, and re-layouts  5.67 us (2%)
  other arithmetic  3.71 us (1%)
    pallas_call x8, Pallas kernels, backward_block(): pl.pallas_call(functools.partial(backward_kernel, k), out_shape=[jax.Shap...  51.5 us
    pallas_call x9, Pallas kernels, unit_product(): pl.pallas_call(functools.partial(unit_kernel, len(units), count, spots),...  48.6 us
    ppermute x15, waiting for transfers between devices, z_shift(): lax.ppermute(value, 'front', [(i, (i + shift * width) % count) for i in r...  32.9 us
    ppermute x20, waiting for transfers between devices, x_swap(): lax.ppermute(value, 'front', [(i, i ^ NC) for i in range(nz * NX * NC)])  30.9 us
    ppermute x20, starting transfers between devices, x_swap(): lax.ppermute(value, 'front', [(i, i ^ NC) for i in range(nz * NX * NC)])  21.1 us
    ppermute x3, waiting for transfers between devices, sub_swap(): return lax.ppermute(value, 'sub', [(0, 1), (1, 0)])  19.6 us
    ppermute x15, starting transfers between devices, z_shift(): lax.ppermute(value, 'front', [(i, (i + shift * width) % count) for i in r...  17.7 us
    ppermute x7, starting transfers between devices, ring_step(): return lax.ppermute(value, 'front', pairs)  7.41 us
  transfers between devices with their start and end apart: 81, of which 30 were waited for; matrix products, arithmetic and copies ran while one was open for 1% of the time, Pallas kernels for 30%

profile of v3, /device:TPU:0, one launch (start us, length us, event | category | flops | bytes accessed | tf_op | source)
XLA Modules:
  0.0 262.8 jit_solution(18268921578384227338)
XLA Ops:
  1.6 3.0 %collective-permute-start.13 = (bf16[352,128]{1,0:T(8,128)(2,1)S(1)}, bf16[352,128]{1,0:T(8,128)(2,1)S(1)}, u32[]{:S(2)}, u32[]{:S(2)}) collective-permute-start(bf16[352,128]{1,0:T(8,128)(2,1)S(1)} %convert_element_type.267.refs_0_), channel_id=1, source_target_pairs={{0,2},{1,3},{2,0},{3,1},{4,6},{5,7},{6,4},{7,5},{8,10},{9,11},{10,... | collective-permute-start | bytes 270344 | tf_op jit(solution)/shard_map/ppermute | solution.py:88
  4.6 3.6 %collective-permute-start.8 = (bf16[352,128]{1,0:T(8,128)(2,1)S(1)}, bf16[352,128]{1,0:T(8,128)(2,1)S(1)}, u32[]{:S(2)}, u32[]{:S(2)}) collective-permute-start(bf16[352,128]{1,0:T(8,128)(2,1)S(1)} %convert_element_type.267.refs_0_), channel_id=1, source_target_pairs={{0,12},{1,13},{2,14},{3,15},{4,0},{5,1},{6,2},{7,3},{8,4},{9,5},{1... | collective-permute-start | bytes 270344 | tf_op jit(solution)/shard_map/ppermute | solution.py:82
  9.2 2.0 collective-permute-done.8.refs_0_
  11.7 3.8 %collective-permute-done.4.refs_0_ = bf16[352,128]{1,0:T(8,128)(2,1)S(1)} collective-permute-done((bf16[352,128]{1,0:T(8,128)(2,1)S(1)}, bf16[352,128]{1,0:T(8,128)(2,1)S(1)}, u32[]{:S(2)}, u32[]{:S(2)}) %collective-permute-start.4) | collective-permute-done | bytes 90144 | tf_op jit(solution)/shard_map/ppermute | solution.py:82
  16.0 1.9 collective-permute-done.refs_0_
  20.0 2.5 collective-permute-done.2.refs_2_
  23.2 3.3 %unit_product.9 = (f32[704,128]{1,0:T(8,128)S(1)}, bf16[704,128]{1,0:T(8,128)(2,1)}) custom-call(s32[34]{0:T(128)S(1)} %dynamic-slice_bitcast_fusion.place, bf16[352,128]{1,0:T(8,128)(2,1)S(1)} %convert_element_type.267.refs_0_, bf16[352,128]{1,0:T(8,128)(2,1)S(1)} %collective-permute-done.12.refs_1_, bf16[352,128]{1,0:T(8,128)(2,1)S(1)} %collective-permute-done.13.refs_2_, ...), custom_call_target="tpu_custom_call" | custom-call | flops 253755392 | bytes 1982464 | tf_op jit(solution)/shard_map/unit_product/pallas_call | solution.py:267
  26.6 3.3 %unit_product.10 = (f32[704,128]{1,0:T(8,128)S(1)}, bf16[704,128]{1,0:T(8,128)(2,1)}) custom-call(s32[34]{0:T(128)S(1)} %dynamic-slice_bitcast_fusion.place, bf16[352,128]{1,0:T(8,128)(2,1)S(1)} %collective-permute-done.8.refs_0_, bf16[352,128]{1,0:T(8,128)(2,1)S(1)} %collective-permute-done.9.refs_1_, bf16[352,128]{1,0:T(8,128)(2,1)S(1)} %collective-permute-done.10.refs_2_, ...), custom_call_target="tpu_custom_call" | custom-call | flops 253755392 | bytes 1982464 | tf_op jit(solution)/shard_map/unit_product/pallas_call | solution.py:267
  29.9 3.4 %unit_product.11 = (f32[704,128]{1,0:T(8,128)S(1)}, bf16[704,128]{1,0:T(8,128)(2,1)}) custom-call(s32[34]{0:T(128)S(1)} %dynamic-slice_bitcast_fusion.place, bf16[352,128]{1,0:T(8,128)(2,1)S(1)} %collective-permute-done.4.refs_0_, bf16[352,128]{1,0:T(8,128)(2,1)S(1)} %collective-permute-done.5.refs_1_, bf16[352,128]{1,0:T(8,128)(2,1)S(1)} %collective-permute-done.6.refs_2_, ...), custom_call_target="tpu_custom_call" | custom-call | flops 253755392 | bytes 1982464 | tf_op jit(solution)/shard_map/unit_product/pallas_call | solution.py:267
  33.3 2.7 %unit_product.12 = (f32[704,128]{1,0:T(8,128)S(1)}, bf16[704,128]{1,0:T(8,128)(2,1)S(1)}) custom-call(s32[34]{0:T(128)S(1)} %dynamic-slice_bitcast_fusion.place, bf16[352,128]{1,0:T(8,128)(2,1)S(1)} %collective-permute-done.refs_0_, bf16[352,128]{1,0:T(8,128)(2,1)S(1)} %collective-permute-done.1.refs_1_, ...), custom_call_target="tpu_custom_call" | custom-call | flops 253755392 | bytes 1982464 | tf_op jit(solution)/shard_map/unit_product/pallas_call | solution.py:267
  36.0 1.6 collective-permute-start.15
  37.6 5.4 %collective-permute-done.15.arrived = bf16[704,128]{1,0:T(8,128)(2,1)S(1)} collective-permute-done((bf16[704,128]{1,0:T(8,128)(2,1)S(1)}, bf16[704,128]{1,0:T(8,128)(2,1)S(1)}, u32[]{:S(2)}, u32[]{:S(2)}) %collective-permute-start.15) | collective-permute-done | bytes 180256 | tf_op jit(solution)/shard_map/ppermute | solution.py:96
  43.0 1.8 push_product.1
  49.6 1.6 collective-permute-start.26
  51.2 3.0 %collective-permute-done.17 = bf16[704,128]{1,0:T(8,128)(2,1)S(1)} collective-permute-done((bf16[704,128]{1,0:T(8,128)(2,1)S(1)}, bf16[704,128]{1,0:T(8,128)(2,1)S(1)}, u32[]{:S(2)}, u32[]{:S(2)}) %collective-permute-start.17) | collective-permute-done | bytes 180256 | tf_op jit(solution)/shard_map/ppermute | solution.py:88
  54.3 3.7 %collective-permute-done.20 = bf16[704,128]{1,0:T(8,128)(2,1)S(1)} collective-permute-done((bf16[704,128]{1,0:T(8,128)(2,1)S(1)}, bf16[704,128]{1,0:T(8,128)(2,1)S(1)}, u32[]{:S(2)}, u32[]{:S(2)}) %collective-permute-start.20) | collective-permute-done | bytes 180256 | tf_op jit(solution)/shard_map/ppermute | solution.py:88
  59.5 2.3 collective-permute-done.23
  62.0 2.9 %collective-permute-done.26 = bf16[704,128]{1,0:T(8,128)(2,1)S(1)} collective-permute-done((bf16[704,128]{1,0:T(8,128)(2,1)S(1)}, bf16[704,128]{1,0:T(8,128)(2,1)S(1)}, u32[]{:S(2)}, u32[]{:S(2)}) %collective-permute-start.26) | collective-permute-done | bytes 180256 | tf_op jit(solution)/shard_map/ppermute | solution.py:88
  64.9 5.2 %collective-permute-done.21 = bf16[704,128]{1,0:T(8,128)(2,1)S(1)} collective-permute-done((bf16[704,128]{1,0:T(8,128)(2,1)S(1)}, bf16[704,128]{1,0:T(8,128)(2,1)S(1)}, u32[]{:S(2)}, u32[]{:S(2)}) %collective-permute-start.21) | collective-permute-done | bytes 180256 | tf_op jit(solution)/shard_map/ppermute | solution.py:82
  72.5 5.2 %unit_product.13 = (f32[1408,128]{1,0:T(8,128)S(1)}, bf16[1408,128]{1,0:T(8,128)(2,1)}) custom-call(s32[34]{0:T(128)S(1)} %dynamic-slice_bitcast_fusion.place, bf16[704,128]{1,0:T(8,128)(2,1)S(1)} %fusion.8.refs_0_, bf16[704,128]{1,0:T(8,128)(2,1)S(1)} %collective-permute-done.28.refs_1_, bf16[1408,11264]{1,0:T(8,128)(2,1)} %matrix.11, ...), custom_call_target="tpu_custom_call" | custom-call | flops 507510784 | bytes 3964928 | tf_op jit(solution)/shard_map/unit_product/pallas_call | solution.py:267
  80.3 8.8 %unit_product.14 = (f32[1408,128]{1,0:T(8,128)S(1)}, bf16[1408,128]{1,0:T(8,128)(2,1)}) custom-call(s32[34]{0:T(128)S(1)} %dynamic-slice_bitcast_fusion.place, bf16[704,128]{1,0:T(8,128)(2,1)S(1)} %collective-permute-done.27.refs_0_, bf16[704,128]{1,0:T(8,128)(2,1)S(1)} %collective-permute-done.30.refs_1_, ...), custom_call_target="tpu_custom_call" | custom-call | flops 1015021568 | bytes 7929856 | tf_op jit(solution)/shard_map/unit_product/pallas_call | solution.py:267
  91.6 8.8 %unit_product.15 = (f32[1408,128]{1,0:T(8,128)S(1)}, bf16[1408,128]{1,0:T(8,128)(2,1)}) custom-call(s32[34]{0:T(128)S(1)} %dynamic-slice_bitcast_fusion.place, bf16[704,128]{1,0:T(8,128)(2,1)S(1)} %collective-permute-done.29.refs_0_, bf16[704,128]{1,0:T(8,128)(2,1)S(1)} %collective-permute-done.34.refs_1_, ...), custom_call_target="tpu_custom_call" | custom-call | flops 1015021568 | bytes 7929856 | tf_op jit(solution)/shard_map/unit_product/pallas_call | solution.py:267
  102.1 8.8 %unit_product.16 = (f32[1408,128]{1,0:T(8,128)S(1)}, bf16[1408,128]{1,0:T(8,128)(2,1)}) custom-call(s32[34]{0:T(128)S(1)} %dynamic-slice_bitcast_fusion.place, bf16[704,128]{1,0:T(8,128)(2,1)S(1)} %collective-permute-done.33.refs_0_, bf16[704,128]{1,0:T(8,128)(2,1)S(1)} %collective-permute-done.38.refs_1_, ...), custom_call_target="tpu_custom_call" | custom-call | flops 1015021568 | bytes 7929856 | tf_op jit(solution)/shard_map/unit_product/pallas_call | solution.py:267
  112.3 4.4 %unit_product.17 = (f32[1408,128]{1,0:T(8,128)S(1)}, bf16[1408,128]{1,0:T(8,128)(2,1)S(1)}) custom-call(s32[34]{0:T(128)S(1)} %dynamic-slice_bitcast_fusion.place, bf16[704,128]{1,0:T(8,128)(2,1)S(1)} %collective-permute-done.37.refs_0_, bf16[704,128]{1,0:T(8,128)(2,1)S(1)} %collective-permute-done.41.refs_1_, bf16[1408,11264]{1,0:T(8,128)(2,1)} %matrix.11, ...), custom_call_target="tpu_custom_call" | custom-call | flops 507510784 | bytes 3964928 | tf_op jit(solution)/shard_map/unit_product/pallas_call | solution.py:267
  119.1 8.9 %collective-permute-done.42.arrived = bf16[1408,128]{1,0:T(8,128)(2,1)S(1)} collective-permute-done((bf16[1408,128]{1,0:T(8,128)(2,1)S(1)}, bf16[1408,128]{1,0:T(8,128)(2,1)S(1)}, u32[]{:S(2)}, u32[]{:S(2)}) %collective-permute-start.42) | collective-permute-done | bytes 360480 | tf_op jit(solution)/shard_map/ppermute | solution.py:96
  128.8 2.1 turn.2.vector
  131.9 5.0 %backward_block.9 = (f32[2,704,128]{2,1,0:T(8,128)S(1)}, bf16[2,704,128]{2,1,0:T(8,128)(2,1)S(1)}) custom-call(s32[34]{0:T(128)S(1)} %dynamic-slice_bitcast_fusion.place, bf16[128,1408]{1,0:T(8,128)(2,1)S(1)} %copy-done, bf16[1408,11264]{1,0:T(8,128)(2,1)} %matrix.11), custom_call_target="tpu_custom_call" | custom-call | flops 1015021568 | bytes 7929856 | tf_op jit(solution)/shard_map/backward_block/pallas_call | solution.py:316
  137.0 4.9 %backward_block.8 = (f32[2,704,128]{2,1,0:T(8,128)S(1)}, bf16[2,704,128]{2,1,0:T(8,128)(2,1)S(1)}) custom-call(s32[34]{0:T(128)S(1)} %dynamic-slice_bitcast_fusion.place, bf16[128,1408]{1,0:T(8,128)(2,1)S(1)} %copy-done, bf16[1408,11264]{1,0:T(8,128)(2,1)} %matrix.11), custom_call_target="tpu_custom_call" | custom-call | flops 1015021568 | bytes 7929856 | tf_op jit(solution)/shard_map/backward_block/pallas_call | solution.py:316
  144.7 5.0 %backward_block.11 = (f32[2,704,128]{2,1,0:T(8,128)S(1)}, bf16[2,704,128]{2,1,0:T(8,128)(2,1)S(1)}) custom-call(s32[34]{0:T(128)S(1)} %dynamic-slice_bitcast_fusion.place, bf16[128,1408]{1,0:T(8,128)(2,1)S(1)} %copy-done, bf16[1408,11264]{1,0:T(8,128)(2,1)} %matrix.11), custom_call_target="tpu_custom_call" | custom-call | flops 1015021568 | bytes 7929856 | tf_op jit(solution)/shard_map/backward_block/pallas_call | solution.py:316
  150.1 2.1 collective-permute-start.48
  152.2 4.9 %backward_block.10 = (f32[2,704,128]{2,1,0:T(8,128)S(1)}, bf16[2,704,128]{2,1,0:T(8,128)(2,1)S(1)}) custom-call(s32[34]{0:T(128)S(1)} %dynamic-slice_bitcast_fusion.place, bf16[128,1408]{1,0:T(8,128)(2,1)S(1)} %copy-done, bf16[1408,11264]{1,0:T(8,128)(2,1)} %matrix.11), custom_call_target="tpu_custom_call" | custom-call | flops 1015021568 | bytes 7929856 | tf_op jit(solution)/shard_map/backward_block/pallas_call | solution.py:316
  161.1 5.2 %collective-permute-done.52 = bf16[704,128]{1,0:T(8,128)(2,1)S(1)} collective-permute-done((bf16[704,128]{1,0:T(8,128)(2,1)S(1)}, bf16[704,128]{1,0:T(8,128)(2,1)S(1)}, u32[]{:S(2)}, u32[]{:S(2)}) %collective-permute-start.52) | collective-permute-done | bytes 180256 | tf_op jit(solution)/shard_map/ppermute | solution.py:88
  167.0 2.5 collective-permute-done.47
  169.4 4.4 %collective-permute-done.53 = bf16[704,128]{1,0:T(8,128)(2,1)S(1)} collective-permute-done((bf16[704,128]{1,0:T(8,128)(2,1)S(1)}, bf16[704,128]{1,0:T(8,128)(2,1)S(1)}, u32[]{:S(2)}, u32[]{:S(2)}) %collective-permute-start.53) | collective-permute-done | bytes 180256 | tf_op jit(solution)/shard_map/ppermute | solution.py:82
  174.7 2.0 collective-permute-start.61
  178.0 4.1 %collective-permute-done.57.refs_4_ = bf16[704,128]{1,0:T(8,128)(2,1)S(1)} collective-permute-done((bf16[704,128]{1,0:T(8,128)(2,1)S(1)}, bf16[704,128]{1,0:T(8,128)(2,1)S(1)}, u32[]{:S(2)}, u32[]{:S(2)}) %collective-permute-start.57) | collective-permute-done | bytes 180256 | tf_op jit(solution)/shard_map/ppermute | solution.py:82
  185.1 4.7 %collective-permute-done.65.refs_12_ = bf16[704,128]{1,0:T(8,128)(2,1)S(1)} collective-permute-done((bf16[704,128]{1,0:T(8,128)(2,1)S(1)}, bf16[704,128]{1,0:T(8,128)(2,1)S(1)}, u32[]{:S(2)}, u32[]{:S(2)}) %collective-permute-start.65) | collective-permute-done | bytes 180256 | tf_op jit(solution)/shard_map/ppermute | solution.py:82
  192.0 3.4 %collective-permute-done.67.refs_14_ = bf16[704,128]{1,0:T(8,128)(2,1)S(1)} collective-permute-done((bf16[704,128]{1,0:T(8,128)(2,1)S(1)}, bf16[704,128]{1,0:T(8,128)(2,1)S(1)}, u32[]{:S(2)}, u32[]{:S(2)}) %collective-permute-start.67) | collective-permute-done | bytes 180256 | tf_op jit(solution)/shard_map/ppermute | solution.py:88
  201.0 5.2 %collective-permute-done.69.arrived = bf16[704,128]{1,0:T(8,128)(2,1)S(1)} collective-permute-done((bf16[704,128]{1,0:T(8,128)(2,1)S(1)}, bf16[704,128]{1,0:T(8,128)(2,1)S(1)}, u32[]{:S(2)}, u32[]{:S(2)}) %collective-permute-start.69) | collective-permute-done | bytes 180256 | tf_op jit(solution)/shard_map/ppermute | solution.py:96
  206.9 2.0 turn.3.vector
  209.8 7.9 %backward_block.13 = (f32[2,352,128]{2,1,0:T(8,128)S(1)}, bf16[2,352,128]{2,1,0:T(8,128)(2,1)S(1)}) custom-call(s32[34]{0:T(128)S(1)} %dynamic-slice_bitcast_fusion.place, bf16[128,704]{1,0:T(8,128)(2,1)S(1)} %copy-done.2, bf16[704,5632]{1,0:T(8,128)(2,1)} %matrix.15), custom_call_target="tpu_custom_call" | custom-call | flops 253755392 | bytes 1982464 | tf_op jit(solution)/shard_map/backward_block/pallas_call | solution.py:316
  217.8 7.9 %backward_block.12 = (f32[2,352,128]{2,1,0:T(8,128)S(1)}, bf16[2,352,128]{2,1,0:T(8,128)(2,1)S(1)}) custom-call(s32[34]{0:T(128)S(1)} %dynamic-slice_bitcast_fusion.place, bf16[128,704]{1,0:T(8,128)(2,1)S(1)} %copy-done.2, bf16[704,5632]{1,0:T(8,128)(2,1)} %matrix.15), custom_call_target="tpu_custom_call" | custom-call | flops 253755392 | bytes 1982464 | tf_op jit(solution)/shard_map/backward_block/pallas_call | solution.py:316
  228.5 7.9 %backward_block.15 = (f32[2,352,128]{2,1,0:T(8,128)S(1)}, bf16[2,352,128]{2,1,0:T(8,128)(2,1)S(1)}) custom-call(s32[34]{0:T(128)S(1)} %dynamic-slice_bitcast_fusion.place, bf16[128,704]{1,0:T(8,128)(2,1)S(1)} %copy-done.2, bf16[704,5632]{1,0:T(8,128)(2,1)} %matrix.15), custom_call_target="tpu_custom_call" | custom-call | flops 253755392 | bytes 1982464 | tf_op jit(solution)/shard_map/backward_block/pallas_call | solution.py:316
  236.6 2.8 %collective-permute-start.75 = (bf16[352,128]{1,0:T(8,128)(2,1)S(1)}, bf16[352,128]{1,0:T(8,128)(2,1)S(1)}, u32[]{:S(2)}, u32[]{:S(2)}) collective-permute-start(bf16[352,128]{1,0:T(8,128)(2,1)S(1)} %fusion.25), channel_id=1, source_target_pairs={{0,8},{1,9},{2,10},{3,11},{4,12},{5,13},{6,14},{7,15},{8,0},{9,1},... | collective-permute-start | bytes 270344 | tf_op jit(solution)/shard_map/ppermute | solution.py:82
  239.4 7.9 %backward_block.14 = (f32[2,352,128]{2,1,0:T(8,128)S(1)}, bf16[2,352,128]{2,1,0:T(8,128)(2,1)S(1)}) custom-call(s32[34]{0:T(128)S(1)} %dynamic-slice_bitcast_fusion.place, bf16[128,704]{1,0:T(8,128)(2,1)S(1)} %copy-done.2, bf16[704,5632]{1,0:T(8,128)(2,1)} %matrix.15), custom_call_target="tpu_custom_call" | custom-call | flops 253755392 | bytes 1982464 | tf_op jit(solution)/shard_map/backward_block/pallas_call | solution.py:316
  247.7 2.4 collective-permute-start.77
  252.3 3.4 %collective-permute-done.79 = bf16[352,128]{1,0:T(8,128)(2,1)S(1)} collective-permute-done((bf16[352,128]{1,0:T(8,128)(2,1)S(1)}, bf16[352,128]{1,0:T(8,128)(2,1)S(1)}, u32[]{:S(2)}, u32[]{:S(2)}) %collective-permute-start.79) | collective-permute-done | bytes 90144 | tf_op jit(solution)/shard_map/ppermute | solution.py:88
  256.6 5.4 %collective-permute-done.80 = bf16[352,128]{1,0:T(8,128)(2,1)S(1)} collective-permute-done((bf16[352,128]{1,0:T(8,128)(2,1)S(1)}, bf16[352,128]{1,0:T(8,128)(2,1)S(1)}, u32[]{:S(2)}, u32[]{:S(2)}) %collective-permute-start.80) | collective-permute-done | bytes 90144 | tf_op jit(solution)/shard_map/ppermute | solution.py:82
  (185 shorter events, 56.7 us)
Async XLA Ops:
  1.6 7.6 %collective-permute-start.13 = (bf16[352,128]{1,0:T(8,128)(2,1)S(1)}, bf16[352,128]{1,0:T(8,128)(2,1)S(1)}, u32[]{:S(2)}, u32[]{:S(2)}) collective-permute-start(bf16[352,128]{1,0:T(8,128)(2,1)S(1)} %convert_element_type.267.refs_0_), channel_id=1, source_target_pairs={{0,2},{1,3},{2,0},{3,1},{4,6},{5,7},{6,4},{7,5},{8,10},{9,11},{10,... | collective-permute-start | bytes 270344 | tf_op jit(solution)/shard_map/ppermute | solution.py:88
  8.2 7.3 %collective-permute-start.4 = (bf16[352,128]{1,0:T(8,128)(2,1)S(1)}, bf16[352,128]{1,0:T(8,128)(2,1)S(1)}, u32[]{:S(2)}, u32[]{:S(2)}) collective-permute-start(bf16[352,128]{1,0:T(8,128)(2,1)S(1)} %convert_element_type.267.refs_0_), channel_id=1, source_target_pairs={{0,4},{1,5},{2,6},{3,7},{4,8},{5,9},{6,10},{7,11},{8,12},{9,13},{1... | collective-permute-start | bytes 270344 | tf_op jit(solution)/shard_map/ppermute | solution.py:82
  8.2 9.8 %collective-permute-start = (bf16[352,128]{1,0:T(8,128)(2,1)S(1)}, bf16[352,128]{1,0:T(8,128)(2,1)S(1)}, u32[]{:S(2)}, u32[]{:S(2)}) collective-permute-start(bf16[352,128]{1,0:T(8,128)(2,1)S(1)} %convert_element_type.267.refs_0_), channel_id=1, source_target_pairs={{0,8},{1,9},{2,10},{3,11},{4,12},{5,13},{6,14},{7,15},{8,0},{9,1},... | collective-permute-start | bytes 270344 | tf_op jit(solution)/shard_map/ppermute | solution.py:82
  9.2 9.3 %collective-permute-start.14 = (bf16[352,128]{1,0:T(8,128)(2,1)S(1)}, bf16[352,128]{1,0:T(8,128)(2,1)S(1)}, u32[]{:S(2)}, u32[]{:S(2)}) collective-permute-start(bf16[352,128]{1,0:T(8,128)(2,1)S(1)} %collective-permute-done.13.refs_2_), channel_id=1, source_target_pairs={{0,1},{1,0},{2,3},{3,2},{4,5},{5,4},{6,7},{7,6},{8,9},{9,8},{10,11... | collective-permute-start | bytes 270344 | tf_op jit(solution)/shard_map/ppermute | solution.py:92
  11.2 7.3 %collective-permute-start.10 = (bf16[352,128]{1,0:T(8,128)(2,1)S(1)}, bf16[352,128]{1,0:T(8,128)(2,1)S(1)}, u32[]{:S(2)}, u32[]{:S(2)}) collective-permute-start(bf16[352,128]{1,0:T(8,128)(2,1)S(1)} %collective-permute-done.8.refs_0_), channel_id=1, source_target_pairs={{0,2},{1,3},{2,0},{3,1},{4,6},{5,7},{6,4},{7,5},{8,10},{9,11},{10,... | collective-permute-start | bytes 270344 | tf_op jit(solution)/shard_map/ppermute | solution.py:88
  11.7 7.3 %collective-permute-start.9 = (bf16[352,128]{1,0:T(8,128)(2,1)S(1)}, bf16[352,128]{1,0:T(8,128)(2,1)S(1)}, u32[]{:S(2)}, u32[]{:S(2)}) collective-permute-start(bf16[352,128]{1,0:T(8,128)(2,1)S(1)} %collective-permute-done.8.refs_0_), channel_id=1, source_target_pairs={{0,1},{1,0},{2,3},{3,2},{4,5},{5,4},{6,7},{7,6},{8,9},{9,8},{10,11... | collective-permute-start | bytes 270344 | tf_op jit(solution)/shard_map/ppermute | solution.py:92
  18.5 11.4 %collective-permute-start.5 = (bf16[352,128]{1,0:T(8,128)(2,1)S(1)}, bf16[352,128]{1,0:T(8,128)(2,1)S(1)}, u32[]{:S(2)}, u32[]{:S(2)}) collective-permute-start(bf16[352,128]{1,0:T(8,128)(2,1)S(1)} %collective-permute-done.4.refs_0_), channel_id=1, source_target_pairs={{0,1},{1,0},{2,3},{3,2},{4,5},{5,4},{6,7},{7,6},{8,9},{9,8},{10,11... | collective-permute-start | bytes 270344 | tf_op jit(solution)/shard_map/ppermute | solution.py:92
  18.5 14.8 %collective-permute-start.1 = (bf16[352,128]{1,0:T(8,128)(2,1)S(1)}, bf16[352,128]{1,0:T(8,128)(2,1)S(1)}, u32[]{:S(2)}, u32[]{:S(2)}) collective-permute-start(bf16[352,128]{1,0:T(8,128)(2,1)S(1)} %collective-permute-done.refs_0_), channel_id=1, source_target_pairs={{0,1},{1,0},{2,3},{3,2},{4,5},{5,4},{6,7},{7,6},{8,9},{9,8},{10,11... | collective-permute-start | bytes 270344 | tf_op jit(solution)/shard_map/ppermute | solution.py:92
  19.0 7.5 %collective-permute-start.11 = (bf16[352,128]{1,0:T(8,128)(2,1)S(1)}, bf16[352,128]{1,0:T(8,128)(2,1)S(1)}, u32[]{:S(2)}, u32[]{:S(2)}) collective-permute-start(bf16[352,128]{1,0:T(8,128)(2,1)S(1)} %collective-permute-done.10.refs_2_), channel_id=1, source_target_pairs={{0,1},{1,0},{2,3},{3,2},{4,5},{5,4},{6,7},{7,6},{8,9},{9,8},{10,11... | collective-permute-start | bytes 270344 | tf_op jit(solution)/shard_map/ppermute | solution.py:92
  20.0 9.9 %collective-permute-start.7 = (bf16[352,128]{1,0:T(8,128)(2,1)S(1)}, bf16[352,128]{1,0:T(8,128)(2,1)S(1)}, u32[]{:S(2)}, u32[]{:S(2)}) collective-permute-start(bf16[352,128]{1,0:T(8,128)(2,1)S(1)} %collective-permute-done.6.refs_2_), channel_id=1, source_target_pairs={{0,1},{1,0},{2,3},{3,2},{4,5},{5,4},{6,7},{7,6},{8,9},{9,8},{10,11... | collective-permute-start | bytes 270344 | tf_op jit(solution)/shard_map/ppermute | solution.py:92
  22.5 10.8 %collective-permute-start.3 = (bf16[352,128]{1,0:T(8,128)(2,1)S(1)}, bf16[352,128]{1,0:T(8,128)(2,1)S(1)}, u32[]{:S(2)}, u32[]{:S(2)}) collective-permute-start(bf16[352,128]{1,0:T(8,128)(2,1)S(1)} %collective-permute-done.2.refs_2_), channel_id=1, source_target_pairs={{0,1},{1,0},{2,3},{3,2},{4,5},{5,4},{6,7},{7,6},{8,9},{9,8},{10,11... | collective-permute-start | bytes 270344 | tf_op jit(solution)/shard_map/ppermute | solution.py:92
  36.0 7.0 %collective-permute-start.15 = (bf16[704,128]{1,0:T(8,128)(2,1)S(1)}, bf16[704,128]{1,0:T(8,128)(2,1)S(1)}, u32[]{:S(2)}, u32[]{:S(2)}) collective-permute-start(bf16[704,128]{1,0:T(8,128)(2,1)S(1)} %get-tuple-element.55), channel_id=1, source_target_pairs={{0,16},{16,0},{1,17},{17,1},{2,18},{18,2},{3,19},{19,3},{4,20},{20... | collective-permute-start | bytes 540680 | tf_op jit(solution)/shard_map/ppermute | solution.py:96
  46.7 7.5 %collective-permute-start.17 = (bf16[704,128]{1,0:T(8,128)(2,1)S(1)}, bf16[704,128]{1,0:T(8,128)(2,1)S(1)}, u32[]{:S(2)}, u32[]{:S(2)}) collective-permute-start(bf16[704,128]{1,0:T(8,128)(2,1)S(1)} %fusion.12), channel_id=1, source_target_pairs={{0,2},{1,3},{2,0},{3,1},{4,6},{5,7},{6,4},{7,5},{8,10},{9,11},{10,... | collective-permute-start | bytes 540680 | tf_op jit(solution)/shard_map/ppermute | solution.py:88
  47.3 10.7 %collective-permute-start.20 = (bf16[704,128]{1,0:T(8,128)(2,1)S(1)}, bf16[704,128]{1,0:T(8,128)(2,1)S(1)}, u32[]{:S(2)}, u32[]{:S(2)}) collective-permute-start(bf16[704,128]{1,0:T(8,128)(2,1)S(1)} %fusion.13), channel_id=1, source_target_pairs={{0,2},{1,3},{2,0},{3,1},{4,6},{5,7},{6,4},{7,5},{8,10},{9,11},{10,... | collective-permute-start | bytes 540680 | tf_op jit(solution)/shard_map/ppermute | solution.py:88
  48.9 12.9 %collective-permute-start.23 = (bf16[704,128]{1,0:T(8,128)(2,1)S(1)}, bf16[704,128]{1,0:T(8,128)(2,1)S(1)}, u32[]{:S(2)}, u32[]{:S(2)}) collective-permute-start(bf16[704,128]{1,0:T(8,128)(2,1)S(1)} %fusion.14), channel_id=1, source_target_pairs={{0,2},{1,3},{2,0},{3,1},{4,6},{5,7},{6,4},{7,5},{8,10},{9,11},{10,... | collective-permute-start | bytes 540680 | tf_op jit(solution)/shard_map/ppermute | solution.py:88
  49.6 15.3 %collective-permute-start.26 = (bf16[704,128]{1,0:T(8,128)(2,1)S(1)}, bf16[704,128]{1,0:T(8,128)(2,1)S(1)}, u32[]{:S(2)}, u32[]{:S(2)}) collective-permute-start(bf16[704,128]{1,0:T(8,128)(2,1)S(1)} %fusion.15), channel_id=1, source_target_pairs={{0,2},{1,3},{2,0},{3,1},{4,6},{5,7},{6,4},{7,5},{8,10},{9,11},{10,... | collective-permute-start | bytes 540680 | tf_op jit(solution)/shard_map/ppermute | solution.py:88
  54.2 10.7 %collective-permute-start.18 = (bf16[704,128]{1,0:T(8,128)(2,1)S(1)}, bf16[704,128]{1,0:T(8,128)(2,1)S(1)}, u32[]{:S(2)}, u32[]{:S(2)}) collective-permute-start(bf16[704,128]{1,0:T(8,128)(2,1)S(1)} %fusion.11), channel_id=1, source_target_pairs={{0,8},{1,9},{2,10},{3,11},{4,12},{5,13},{6,14},{7,15},{8,0},{9,1},... | collective-permute-start | bytes 540680 | tf_op jit(solution)/shard_map/ppermute | solution.py:82
  58.1 12.0 %collective-permute-start.21 = (bf16[704,128]{1,0:T(8,128)(2,1)S(1)}, bf16[704,128]{1,0:T(8,128)(2,1)S(1)}, u32[]{:S(2)}, u32[]{:S(2)}) collective-permute-start(bf16[704,128]{1,0:T(8,128)(2,1)S(1)} %fusion.10), channel_id=1, source_target_pairs={{0,12},{1,13},{2,14},{3,15},{4,0},{5,1},{6,2},{7,3},{8,4},{9,5},{1... | collective-permute-start | bytes 540680 | tf_op jit(solution)/shard_map/ppermute | solution.py:82
  61.9 8.2 %collective-permute-start.24 = (bf16[704,128]{1,0:T(8,128)(2,1)S(1)}, bf16[704,128]{1,0:T(8,128)(2,1)S(1)}, u32[]{:S(2)}, u32[]{:S(2)}) collective-permute-start(bf16[704,128]{1,0:T(8,128)(2,1)S(1)} %fusion.9), channel_id=1, source_target_pairs={{0,4},{1,5},{2,6},{3,7},{4,8},{5,9},{6,10},{7,11},{8,12},{9,13},{1... | collective-permute-start | bytes 540680 | tf_op jit(solution)/shard_map/ppermute | solution.py:82
  70.4 7.4 %collective-permute-start.31 = (bf16[704,128]{1,0:T(8,128)(2,1)S(1)}, bf16[704,128]{1,0:T(8,128)(2,1)S(1)}, u32[]{:S(2)}, u32[]{:S(2)}) collective-permute-start(bf16[704,128]{1,0:T(8,128)(2,1)S(1)} %fusion.8.refs_0_), channel_id=1, source_target_pairs={{0,2},{1,3},{4,0},{5,1},{8,4},{9,5},{12,8},{13,9},{14,12},{15,13},... | collective-permute-start | bytes 540680 | tf_op jit(solution)/shard_map/ppermute | solution.py:143
  71.0 6.7 %collective-permute-start.27 = (bf16[704,128]{1,0:T(8,128)(2,1)S(1)}, bf16[704,128]{1,0:T(8,128)(2,1)S(1)}, u32[]{:S(2)}, u32[]{:S(2)}) collective-permute-start(bf16[704,128]{1,0:T(8,128)(2,1)S(1)} %fusion.8.refs_0_), channel_id=1, source_target_pairs={{0,4},{1,5},{4,8},{5,9},{8,12},{9,13},{12,14},{13,15},{14,10},{15,... | collective-permute-start | bytes 540680 | tf_op jit(solution)/shard_map/ppermute | solution.py:143
  78.2 10.8 %collective-permute-start.35 = (bf16[704,128]{1,0:T(8,128)(2,1)S(1)}, bf16[704,128]{1,0:T(8,128)(2,1)S(1)}, u32[]{:S(2)}, u32[]{:S(2)}) collective-permute-start(bf16[704,128]{1,0:T(8,128)(2,1)S(1)} %collective-permute-done.31.refs_2_), channel_id=1, source_target_pairs={{0,2},{1,3},{4,0},{5,1},{8,4},{9,5},{12,8},{13,9},{14,12},{15,13},... | collective-permute-start | bytes 540680 | tf_op jit(solution)/shard_map/ppermute | solution.py:143
  78.9 10.2 %collective-permute-start.29 = (bf16[704,128]{1,0:T(8,128)(2,1)S(1)}, bf16[704,128]{1,0:T(8,128)(2,1)S(1)}, u32[]{:S(2)}, u32[]{:S(2)}) collective-permute-start(bf16[704,128]{1,0:T(8,128)(2,1)S(1)} %collective-permute-done.27.refs_0_), channel_id=1, source_target_pairs={{0,4},{1,5},{4,8},{5,9},{8,12},{9,13},{12,14},{13,15},{14,10},{15,... | collective-permute-start | bytes 540680 | tf_op jit(solution)/shard_map/ppermute | solution.py:143
  89.5 10.8 %collective-permute-start.39 = (bf16[704,128]{1,0:T(8,128)(2,1)S(1)}, bf16[704,128]{1,0:T(8,128)(2,1)S(1)}, u32[]{:S(2)}, u32[]{:S(2)}) collective-permute-start(bf16[704,128]{1,0:T(8,128)(2,1)S(1)} %collective-permute-done.35.refs_2_), channel_id=1, source_target_pairs={{0,2},{1,3},{4,0},{5,1},{8,4},{9,5},{12,8},{13,9},{14,12},{15,13},... | collective-permute-start | bytes 540680 | tf_op jit(solution)/shard_map/ppermute | solution.py:143
  90.2 10.2 %collective-permute-start.33 = (bf16[704,128]{1,0:T(8,128)(2,1)S(1)}, bf16[704,128]{1,0:T(8,128)(2,1)S(1)}, u32[]{:S(2)}, u32[]{:S(2)}) collective-permute-start(bf16[704,128]{1,0:T(8,128)(2,1)S(1)} %collective-permute-done.29.refs_0_), channel_id=1, source_target_pairs={{0,4},{1,5},{4,8},{5,9},{8,12},{9,13},{12,14},{13,15},{14,10},{15,... | collective-permute-start | bytes 540680 | tf_op jit(solution)/shard_map/ppermute | solution.py:143
  100.9 10.1 %collective-permute-start.37 = (bf16[704,128]{1,0:T(8,128)(2,1)S(1)}, bf16[704,128]{1,0:T(8,128)(2,1)S(1)}, u32[]{:S(2)}, u32[]{:S(2)}) collective-permute-start(bf16[704,128]{1,0:T(8,128)(2,1)S(1)} %collective-permute-done.33.refs_0_), channel_id=1, source_target_pairs={{0,4},{1,5},{4,8},{5,9},{8,12},{9,13},{12,14},{13,15},{14,10},{15,... | collective-permute-start | bytes 540680 | tf_op jit(solution)/shard_map/ppermute | solution.py:143
  117.6 10.5 %collective-permute-start.42 = (bf16[1408,128]{1,0:T(8,128)(2,1)S(1)}, bf16[1408,128]{1,0:T(8,128)(2,1)S(1)}, u32[]{:S(2)}, u32[]{:S(2)}) collective-permute-start(bf16[1408,128]{1,0:T(8,128)(2,1)S(1)} %get-tuple-element.76), channel_id=1, source_target_pairs={{0,16},{16,0},{1,17},{17,1},{2,18},{18,2},{3,19},{19,3},{4,20},{20... | collective-permute-start | bytes 1081352 | tf_op jit(solution)/shard_map/ppermute | solution.py:96
  142.5 7.5 %collective-permute-start.45 = (bf16[704,128]{1,0:T(8,128)(2,1)S(1)}, bf16[704,128]{1,0:T(8,128)(2,1)S(1)}, u32[]{:S(2)}, u32[]{:S(2)}) collective-permute-start(bf16[704,128]{1,0:T(8,128)(2,1)S(1)} %fusion.17), channel_id=1, source_target_pairs={{0,2},{1,3},{2,0},{3,1},{4,6},{5,7},{6,4},{7,5},{8,10},{9,11},{10,... | collective-permute-start | bytes 540680 | tf_op jit(solution)/shard_map/ppermute | solution.py:88
  143.8 13.3 %collective-permute-start.49 = (bf16[704,128]{1,0:T(8,128)(2,1)S(1)}, bf16[704,128]{1,0:T(8,128)(2,1)S(1)}, u32[]{:S(2)}, u32[]{:S(2)}) collective-permute-start(bf16[704,128]{1,0:T(8,128)(2,1)S(1)} %fusion.16), channel_id=1, source_target_pairs={{0,2},{1,3},{2,0},{3,1},{4,6},{5,7},{6,4},{7,5},{8,10},{9,11},{10,... | collective-permute-start | bytes 540680 | tf_op jit(solution)/shard_map/ppermute | solution.py:88
  149.7 9.1 %collective-permute-start.51 = (bf16[2,704,128]{2,1,0:T(8,128)(2,1)S(1)}, bf16[2,704,128]{2,1,0:T(8,128)(2,1)S(1)}, u32[]{:S(2)}, u32[]{:S(2)}) collective-permute-start(bf16[2,704,128]{2,1,0:T(8,128)(2,1)S(1)} %get-tuple-element.86), channel_id=1, source_target_pairs={{0,1},{1,0},{2,3},{3,2},{4,5},{5,4},{6,7},{7,6},{8,9},{9,8},{10,11... | collective-permute-start | bytes 1081352 | tf_op jit(solution)/shard_map/ppermute | solution.py:92
  150.1 16.9 %collective-permute-start.48 = (bf16[704,128]{1,0:T(8,128)(2,1)S(1)}, bf16[704,128]{1,0:T(8,128)(2,1)S(1)}, u32[]{:S(2)}, u32[]{:S(2)}) collective-permute-start(bf16[704,128]{1,0:T(8,128)(2,1)S(1)} %fusion.5), channel_id=1, source_target_pairs={{0,8},{1,9},{2,10},{3,11},{4,12},{5,13},{6,14},{7,15},{8,0},{9,1},... | collective-permute-start | bytes 540680 | tf_op jit(solution)/shard_map/ppermute | solution.py:82
  157.3 9.7 %collective-permute-start.50 = (bf16[704,128]{1,0:T(8,128)(2,1)S(1)}, bf16[704,128]{1,0:T(8,128)(2,1)S(1)}, u32[]{:S(2)}, u32[]{:S(2)}) collective-permute-start(bf16[704,128]{1,0:T(8,128)(2,1)S(1)} %fusion.1), channel_id=1, source_target_pairs={{0,12},{1,13},{2,14},{3,15},{4,0},{5,1},{6,2},{7,3},{8,4},{9,5},{1... | collective-permute-start | bytes 540680 | tf_op jit(solution)/shard_map/ppermute | solution.py:82
  158.9 7.5 %collective-permute-start.52 = (bf16[704,128]{1,0:T(8,128)(2,1)S(1)}, bf16[704,128]{1,0:T(8,128)(2,1)S(1)}, u32[]{:S(2)}, u32[]{:S(2)}) collective-permute-start(bf16[704,128]{1,0:T(8,128)(2,1)S(1)} %fusion.19), channel_id=1, source_target_pairs={{0,2},{1,3},{2,0},{3,1},{4,6},{5,7},{6,4},{7,5},{8,10},{9,11},{10,... | collective-permute-start | bytes 540680 | tf_op jit(solution)/shard_map/ppermute | solution.py:88
  160.2 9.2 %collective-permute-start.47 = (bf16[704,128]{1,0:T(8,128)(2,1)S(1)}, bf16[704,128]{1,0:T(8,128)(2,1)S(1)}, u32[]{:S(2)}, u32[]{:S(2)}) collective-permute-start(bf16[704,128]{1,0:T(8,128)(2,1)S(1)} %fusion.18), channel_id=1, source_target_pairs={{0,2},{1,3},{2,0},{3,1},{4,6},{5,7},{6,4},{7,5},{8,10},{9,11},{10,... | collective-permute-start | bytes 540680 | tf_op jit(solution)/shard_map/ppermute | solution.py:88
  166.4 7.4 %collective-permute-start.53 = (bf16[704,128]{1,0:T(8,128)(2,1)S(1)}, bf16[704,128]{1,0:T(8,128)(2,1)S(1)}, u32[]{:S(2)}, u32[]{:S(2)}) collective-permute-start(bf16[704,128]{1,0:T(8,128)(2,1)S(1)} %fusion), channel_id=1, source_target_pairs={{0,4},{1,5},{2,6},{3,7},{4,8},{5,9},{6,10},{7,11},{8,12},{9,13},{1... | collective-permute-start | bytes 540680 | tf_op jit(solution)/shard_map/ppermute | solution.py:82
  174.7 7.4 %collective-permute-start.57 = (bf16[704,128]{1,0:T(8,128)(2,1)S(1)}, bf16[704,128]{1,0:T(8,128)(2,1)S(1)}, u32[]{:S(2)}, u32[]{:S(2)}) collective-permute-start(bf16[704,128]{1,0:T(8,128)(2,1)S(1)} %get-tuple-element.100.refs_0_), channel_id=1, source_target_pairs={{0,12},{1,13},{2,14},{3,15},{4,0},{5,1},{6,2},{7,3},{8,4},{9,5},{1... | collective-permute-start | bytes 540680 | tf_op jit(solution)/shard_map/ppermute | solution.py:82
  174.7 9.5 %collective-permute-start.61 = (bf16[704,128]{1,0:T(8,128)(2,1)S(1)}, bf16[704,128]{1,0:T(8,128)(2,1)S(1)}, u32[]{:S(2)}, u32[]{:S(2)}) collective-permute-start(bf16[704,128]{1,0:T(8,128)(2,1)S(1)} %get-tuple-element.100.refs_0_), channel_id=1, source_target_pairs={{0,4},{1,5},{2,6},{3,7},{4,8},{5,9},{6,10},{7,11},{8,12},{9,13},{1... | collective-permute-start | bytes 540680 | tf_op jit(solution)/shard_map/ppermute | solution.py:82
  176.7 13.1 %collective-permute-start.65 = (bf16[704,128]{1,0:T(8,128)(2,1)S(1)}, bf16[704,128]{1,0:T(8,128)(2,1)S(1)}, u32[]{:S(2)}, u32[]{:S(2)}) collective-permute-start(bf16[704,128]{1,0:T(8,128)(2,1)S(1)} %get-tuple-element.100.refs_0_), channel_id=1, source_target_pairs={{0,8},{1,9},{2,10},{3,11},{4,12},{5,13},{6,14},{7,15},{8,0},{9,1},... | collective-permute-start | bytes 540680 | tf_op jit(solution)/shard_map/ppermute | solution.py:82
  176.7 14.2 %collective-permute-start.55 = (bf16[704,128]{1,0:T(8,128)(2,1)S(1)}, bf16[704,128]{1,0:T(8,128)(2,1)S(1)}, u32[]{:S(2)}, u32[]{:S(2)}) collective-permute-start(bf16[704,128]{1,0:T(8,128)(2,1)S(1)} %get-tuple-element.100.refs_0_), channel_id=1, source_target_pairs={{0,2},{1,3},{2,0},{3,1},{4,6},{5,7},{6,4},{7,5},{8,10},{9,11},{10,... | collective-permute-start | bytes 540680 | tf_op jit(solution)/shard_map/ppermute | solution.py:88
  178.0 12.9 %collective-permute-start.54 = (bf16[704,128]{1,0:T(8,128)(2,1)S(1)}, bf16[704,128]{1,0:T(8,128)(2,1)S(1)}, u32[]{:S(2)}, u32[]{:S(2)}) collective-permute-start(bf16[704,128]{1,0:T(8,128)(2,1)S(1)} %get-tuple-element.100.refs_0_), channel_id=1, source_target_pairs={{0,1},{1,0},{2,3},{3,2},{4,5},{5,4},{6,7},{7,6},{8,9},{9,8},{10,11... | collective-permute-start | bytes 540680 | tf_op jit(solution)/shard_map/ppermute | solution.py:92
  182.1 9.3 %collective-permute-start.59 = (bf16[704,128]{1,0:T(8,128)(2,1)S(1)}, bf16[704,128]{1,0:T(8,128)(2,1)S(1)}, u32[]{:S(2)}, u32[]{:S(2)}) collective-permute-start(bf16[704,128]{1,0:T(8,128)(2,1)S(1)} %collective-permute-done.57.refs_4_), channel_id=1, source_target_pairs={{0,2},{1,3},{2,0},{3,1},{4,6},{5,7},{6,4},{7,5},{8,10},{9,11},{10,... | collective-permute-start | bytes 540680 | tf_op jit(solution)/shard_map/ppermute | solution.py:88
  184.2 7.3 %collective-permute-start.63 = (bf16[704,128]{1,0:T(8,128)(2,1)S(1)}, bf16[704,128]{1,0:T(8,128)(2,1)S(1)}, u32[]{:S(2)}, u32[]{:S(2)}) collective-permute-start(bf16[704,128]{1,0:T(8,128)(2,1)S(1)} %collective-permute-done.61.refs_8_), channel_id=1, source_target_pairs={{0,2},{1,3},{2,0},{3,1},{4,6},{5,7},{6,4},{7,5},{8,10},{9,11},{10,... | collective-permute-start | bytes 540680 | tf_op jit(solution)/shard_map/ppermute | solution.py:88
  217.7 8.6 %collective-permute-start.71 = (bf16[2,352,128]{2,1,0:T(8,128)(2,1)S(1)}, bf16[2,352,128]{2,1,0:T(8,128)(2,1)S(1)}, u32[]{:S(2)}, u32[]{:S(2)}) collective-permute-start(bf16[2,352,128]{2,1,0:T(8,128)(2,1)S(1)} %get-tuple-element.93), channel_id=1, source_target_pairs={{0,1},{1,0},{2,3},{3,2},{4,5},{5,4},{6,7},{7,6},{8,9},{9,8},{10,11... | collective-permute-start | bytes 540680 | tf_op jit(solution)/shard_map/ppermute | solution.py:92
  226.3 10.3 %collective-permute-start.72 = (bf16[352,128]{1,0:T(8,128)(2,1)S(1)}, bf16[352,128]{1,0:T(8,128)(2,1)S(1)}, u32[]{:S(2)}, u32[]{:S(2)}) collective-permute-start(bf16[352,128]{1,0:T(8,128)(2,1)S(1)} %fusion.27), channel_id=1, source_target_pairs={{0,2},{1,3},{2,0},{3,1},{4,6},{5,7},{6,4},{7,5},{8,10},{9,11},{10,... | collective-permute-start | bytes 270344 | tf_op jit(solution)/shard_map/ppermute | solution.py:88
  227.5 20.1 %collective-permute-start.76 = (bf16[352,128]{1,0:T(8,128)(2,1)S(1)}, bf16[352,128]{1,0:T(8,128)(2,1)S(1)}, u32[]{:S(2)}, u32[]{:S(2)}) collective-permute-start(bf16[352,128]{1,0:T(8,128)(2,1)S(1)} %fusion.26), channel_id=1, source_target_pairs={{0,2},{1,3},{2,0},{3,1},{4,6},{5,7},{6,4},{7,5},{8,10},{9,11},{10,... | collective-permute-start | bytes 270344 | tf_op jit(solution)/shard_map/ppermute | solution.py:88
  236.5 13.6 %collective-permute-start.78 = (bf16[2,352,128]{2,1,0:T(8,128)(2,1)S(1)}, bf16[2,352,128]{2,1,0:T(8,128)(2,1)S(1)}, u32[]{:S(2)}, u32[]{:S(2)}) collective-permute-start(bf16[2,352,128]{2,1,0:T(8,128)(2,1)S(1)} %get-tuple-element.99), channel_id=1, source_target_pairs={{0,1},{1,0},{2,3},{3,2},{4,5},{5,4},{6,7},{7,6},{8,9},{9,8},{10,11... | collective-permute-start | bytes 540680 | tf_op jit(solution)/shard_map/ppermute | solution.py:92
  236.6 19.1 %collective-permute-start.75 = (bf16[352,128]{1,0:T(8,128)(2,1)S(1)}, bf16[352,128]{1,0:T(8,128)(2,1)S(1)}, u32[]{:S(2)}, u32[]{:S(2)}) collective-permute-start(bf16[352,128]{1,0:T(8,128)(2,1)S(1)} %fusion.25), channel_id=1, source_target_pairs={{0,8},{1,9},{2,10},{3,11},{4,12},{5,13},{6,14},{7,15},{8,0},{9,1},... | collective-permute-start | bytes 270344 | tf_op jit(solution)/shard_map/ppermute | solution.py:82
  247.7 8.1 %collective-permute-start.77 = (bf16[352,128]{1,0:T(8,128)(2,1)S(1)}, bf16[352,128]{1,0:T(8,128)(2,1)S(1)}, u32[]{:S(2)}, u32[]{:S(2)}) collective-permute-start(bf16[352,128]{1,0:T(8,128)(2,1)S(1)} %fusion.21), channel_id=1, source_target_pairs={{0,12},{1,13},{2,14},{3,15},{4,0},{5,1},{6,2},{7,3},{8,4},{9,5},{1... | collective-permute-start | bytes 270344 | tf_op jit(solution)/shard_map/ppermute | solution.py:82
  (43 other events, 206.6 us)

commit v4 on v3

--- a/solution.py
+++ b/solution.py
@@ -16,7 +16,9 @@
 HIGHEST_PRECISION = lax.Precision.HIGHEST
 VMEM = pl.BlockSpec(memory_space=pltpu.VMEM)
 SMEM = pl.BlockSpec(memory_space=pltpu.SMEM)
+HBM = pl.BlockSpec(memory_space=pltpu.HBM)
 VMEM_LIMIT = 32 * 1024 * 1024
+CHUNK = 512
 
 
 def transposed_product(matrix, vector):
@@ -125,11 +127,9 @@
     group = NX * NC
     at = Spots(nz)
     pieces = gather_pieces(own, nz)
-    acc = acc_b = jnp.zeros((matrix.shape[0], own.shape[1]), F32)
-    for k in near_first(nz):
-        block = pieces[k * group : (k + 1) * group]
-        acc, acc_b = unit_product(place, [at.blocks + k], at.near, [block], matrix, acc)
-    return acc, acc_b
+    order = near_first(nz)
+    units = [pieces[k * group : (k + 1) * group] for k in order]
+    return unit_product(place, [at.blocks + k for k in order], at.near, units, matrix, None, True)
 
 
 def ring_step(value, way, nz):
@@ -146,7 +146,7 @@
 def ring_product(place, own, matrix, nz):
     count = NX * nz
     at = Spots(nz)
-    acc = acc_b = jnp.zeros((matrix.shape[0], own.shape[1]), F32)
+    acc = None
     held = {0: own}
     for step in range(nz + 1):
         if step:
@@ -157,9 +157,10 @@
             following[(-step - 1) % count] = ring_step(held[(-step) % count], 1, nz)
             if step < nz - 1:
                 following[step + 1] = ring_step(held[step], -1, nz)
-        acc, acc_b = unit_product(place, [at.ring + j for j in held], at.core, units, matrix, acc)
+        blocks = [at.ring + j for j in held]
+        acc, *acc_b = unit_product(place, blocks, at.core, units, matrix, acc, step == nz)
         held = following
-    return acc, acc_b
+    return acc, acc_b[0]
 
 
 def far_first(nz):
@@ -199,6 +200,7 @@
 
 class Spots:
     def __init__(self, nz):
+        self.nz = nz
         group = NX * NC
         self.ring = nz * group
         self.blocks = self.ring + NX * nz
@@ -224,63 +226,79 @@
                 ].astype(out.dtype)
 
 
-def row_step(rows):
-    for step in (352, 256, 128):
-        if rows % step == 0:
-            return step
-    return rows
-
-
-def unit_kernel(units, count, spots, place, *refs):
-    pieces, (matrix, acc, out, out_b, cols) = refs[: units * count], refs[units * count :]
+def row_chunks(rows):
+    return [(start, min(CHUNK, rows - start)) for start in range(0, rows, CHUNK)]
+
+
+def start_blocks(matrix, firsts, buffer, arrived):
+    rows, depth = buffer.shape[1:]
+    copies = []
+    for u, first in enumerate(firsts):
+        cols = pl.ds(pl.multiple_of(first * depth, 128), depth)
+        copies.append(
+            [
+                pltpu.make_async_copy(
+                    matrix.at[pl.ds(start, height), cols],
+                    buffer.at[u, pl.ds(start, height), :],
+                    arrived.at[u, i],
+                )
+                for i, (start, height) in enumerate(row_chunks(rows))
+            ]
+        )
+    for column in copies:
+        for copy in column:
+            copy.start()
+    return copies
+
+
+def buffers(units, rows, depth, dtype):
+    return [
+        pltpu.VMEM((units, rows, depth), dtype),
+        pltpu.SemaphoreType.DMA((units, len(row_chunks(rows)))),
+    ]
+
+
+def unit_kernel(blocks, spots, count, fresh, last, place, *refs):
+    units = len(blocks)
+    pieces, refs = refs[: units * count], refs[units * count :]
+    if not fresh:
+        acc, refs = refs[0], refs[1:]
+    matrix, out = refs[0], refs[1]
+    cols, buffer, arrived = refs[-3:]
+    copies = start_blocks(matrix, [place[b] for b in blocks], buffer, arrived)
     rows = pieces[0].shape[0]
-    unit = pl.program_id(1)
-
-    @pl.when((pl.program_id(0) == 0) & (unit == 0))
-    def _():
-        for i, piece in enumerate(pieces):
-            at = place[spots + i % count]
-            cols[i // count, pl.ds(pl.multiple_of(at * rows, rows), rows), :] = piece[...]
-
-    product = jnp.dot(matrix[...], cols[unit], preferred_element_type=F32)
-
-    @pl.when(unit == 0)
-    def _():
-        out[...] = acc[...] + product
-
-    @pl.when(unit > 0)
-    def _():
-        out[...] += product
-
-    @pl.when(unit == units - 1)
-    def _():
-        out_b[...] = out[...].astype(BF16)
-
-
-def unit_product(place, blocks, spots, units, matrix, acc):
+    for i, piece in enumerate(pieces):
+        at = place[spots + i % count]
+        cols[i // count, pl.ds(pl.multiple_of(at * rows, rows), rows), :] = piece[...]
+    for u in range(units):
+        for i, (start, height) in enumerate(row_chunks(buffer.shape[1])):
+            copies[u][i].wait()
+            here = slice(start, start + height)
+            total = jnp.dot(buffer[u, here, :], cols[u], preferred_element_type=F32)
+            if u:
+                total += out[here, :]
+            elif not fresh:
+                total += acc[here, :]
+            out[here, :] = total
+            if last and u == units - 1:
+                refs[2][here, :] = total.astype(BF16)
+
+
+def unit_product(place, blocks, spots, units, matrix, acc, last):
     rows = matrix.shape[0]
     part, n = units[0][0].shape
     count = len(units[0])
     depth = count * part
-    step = row_step(rows)
-    first, then = blocks[0], blocks[-1]
+    pieces = [piece for unit in units for piece in unit]
+    start = [] if acc is None else [acc]
     return pl.pallas_call(
-        functools.partial(unit_kernel, len(units), count, spots),
-        out_shape=(jax.ShapeDtypeStruct((rows, n), F32), jax.ShapeDtypeStruct((rows, n), BF16)),
-        grid_spec=pltpu.PrefetchScalarGridSpec(
-            num_scalar_prefetch=1,
-            grid=(rows // step, len(units)),
-            in_specs=[pl.BlockSpec((part, n), lambda i, u, place: (0, 0))] * (count * len(units))
-            + [
-                pl.BlockSpec(
-                    (step, depth),
-                    lambda i, u, place: (i, jnp.where(u == 0, place[first], place[then])),
-                ),
-                pl.BlockSpec((step, n), lambda i, u, place: (i, 0)),
-            ],
-            out_specs=[pl.BlockSpec((step, n), lambda i, u, place: (i, 0))] * 2,
-            scratch_shapes=[pltpu.VMEM((len(units), depth, n), BF16)],
-        ),
+        functools.partial(unit_kernel, blocks, spots, count, acc is None, last),
+        out_shape=[jax.ShapeDtypeStruct((rows, n), F32)]
+        + [jax.ShapeDtypeStruct((rows, n), BF16)] * last,
+        in_specs=[SMEM] + [VMEM] * (len(pieces) + len(start)) + [HBM],
+        out_specs=[VMEM] * (1 + last),
+        scratch_shapes=[pltpu.VMEM((len(units), depth, n), BF16)]
+        + buffers(len(units), rows, depth, matrix.dtype),
         compiler_params=pltpu.CompilerParams(vmem_limit_bytes=VMEM_LIMIT),
         cost_estimate=pl.CostEstimate(
             flops=2 * rows * depth * n * len(units),
@@ -288,104 +306,94 @@
             transcendentals=0,
         ),
         name="unit_product",
-    )(place, *[piece for unit in units for piece in unit], in_hbm(matrix), acc)
-
-
-def backward_kernel(k, place, vector, matrix, keep, send, whole):
-    step = pl.program_id(0)
-    width = matrix.shape[1]
-    part = keep.shape[1]
-    product = jnp.dot(vector[...], matrix[...], preferred_element_type=F32)
-    whole[pl.ds(pl.multiple_of(step * width, width), width), :] = product.T
-
-    @pl.when(step == pl.num_programs(0) - 1)
-    def _():
+    )(place, *pieces, *start, in_hbm(matrix))
+
+
+def backward_kernel(ks, at, count, place, *refs):
+    inputs, refs = refs[:count], refs[count:]
+    matrix, outs = refs[0], refs[1 : 1 + 2 * len(ks)]
+    whole, buffer, arrived = refs[-3:]
+    copies = start_blocks(matrix, [place[at.blocks + k] for k in ks], buffer, arrived)
+    if count == 1:
+        vector = inputs[0]
+    else:
+        vector = refs[1 + 2 * len(ks)]
+        total = inputs[0][...] + inputs[1][...].astype(F32)
+        if count == 3:
+            total = inputs[2][...] - total
+        vector[...] = total.T.astype(BF16)
+    for u, k in enumerate(ks):
+        total = None
+        for i, (start, height) in enumerate(row_chunks(buffer.shape[1])):
+            copies[u][i].wait()
+            here = slice(start, start + height)
+            product = jnp.dot(vector[:, here], buffer[u, here, :], preferred_element_type=F32)
+            total = product if total is None else total + product
+        whole[...] = total.T
+        part = outs[2 * u].shape[1]
         for xr in range(NX):
-            for cr, out in ((0, keep), (1, send)):
-                at = place[(k * NX + xr) * NC + cr] % (NX * NC)
-                out[xr] = whole[pl.ds(pl.multiple_of(at * part, part), part), :].astype(out.dtype)
-
-
-def backward_block(place, k, vector, matrix, nz):
+            for cr in range(NC):
+                out = outs[2 * u + cr]
+                spot = place[at.near + xr * NC + cr]
+                out[xr] = whole[pl.ds(pl.multiple_of(spot * part, part), part), :].astype(out.dtype)
+
+
+def backward_blocks(place, ks, inputs, matrix, nz):
     rows, width = matrix.shape
-    n = vector.shape[0]
+    n = inputs[0].shape[0] if len(inputs) == 1 else inputs[0].shape[1]
     depth = width // nz
     part = depth // (NX * NC)
-    step = depth // 2 if depth // 2 % 128 == 0 else depth // 11 if depth % (11 * 128) == 0 else depth
-    steps = depth // step
-    return pl.pallas_call(
-        functools.partial(backward_kernel, k),
+    fresh = len(inputs) > 1
+    outs = pl.pallas_call(
+        functools.partial(backward_kernel, ks, Spots(nz), len(inputs)),
         out_shape=[
             jax.ShapeDtypeStruct((NX, part, n), F32),
             jax.ShapeDtypeStruct((NX, part, n), BF16),
-        ],
-        grid_spec=pltpu.PrefetchScalarGridSpec(
-            num_scalar_prefetch=1,
-            grid=(steps,),
-            in_specs=[
-                pl.BlockSpec((n, rows), lambda i, *_: (0, 0)),
-                pl.BlockSpec(
-                    (rows, step),
-                    lambda i, place: (0, place[k * NX * NC] // (NX * NC) * steps + i),
-                ),
-            ],
-            out_specs=[pl.BlockSpec((NX, part, n), lambda i, *_: (0, 0, 0))] * 2,
-            scratch_shapes=[pltpu.VMEM((depth, n), F32)],
-        ),
+        ]
+        * len(ks)
+        + [jax.ShapeDtypeStruct((n, rows), BF16)] * fresh,
+        in_specs=[SMEM] + [VMEM] * len(inputs) + [HBM],
+        out_specs=[VMEM] * (2 * len(ks) + fresh),
+        scratch_shapes=[pltpu.VMEM((depth, n), F32)]
+        + buffers(len(ks), rows, depth, matrix.dtype),
         compiler_params=pltpu.CompilerParams(vmem_limit_bytes=VMEM_LIMIT),
         cost_estimate=pl.CostEstimate(
-            flops=2 * rows * depth * n, bytes_accessed=2 * rows * depth, transcendentals=0
+            flops=2 * rows * depth * n * len(ks),
+            bytes_accessed=2 * rows * depth * len(ks),
+            transcendentals=0,
         ),
-        name="backward_block",
-    )(place, vector, in_hbm(matrix))
-
-
-def product_scatter(place, vector, matrix, nz):
-    order = far_first(nz)
-    blocks, stage_c, stage_x, stage_z = [], [], [], []
-    for i in range(nz + 2):
+        name="backward_blocks",
+    )(place, *inputs, in_hbm(matrix))
+    pairs = {k: (outs[2 * u], outs[2 * u + 1]) for u, k in enumerate(ks)}
+    return pairs, outs[-1] if fresh else inputs[0]
+
+
+def product_scatter(place, inputs, matrix, groups, nz):
+    keep, moved, across, left = {}, {}, {}, {}
+    for g in range(len(groups) + 3):
         started = []
-        if 0 <= i - 2 < nz:
-            keep, arrived = blocks[i - 2][0], stage_c[i - 2]
-            far = (keep[1] + arrived[1].astype(F32)).astype(BF16)
+        for k in groups[g - 2] if 0 <= g - 2 < len(groups) else []:
+            far = (keep[k][1] + moved[k][1].astype(F32)).astype(BF16)
             started.append(far)
-            stage_x.append(x_swap(far, nz))
-        if 0 <= i - 3 < nz - 1:
-            partial = leave(blocks[i - 3][0], stage_c[i - 3], stage_x[i - 3])
-            started.append(partial)
-            stage_z.append(z_shift(partial, order[i - 3], nz).astype(F32))
-        if i < nz:
-            tied = after(vector, *started) if started else vector
-            blocks.append(backward_block(place, order[i], tied, matrix, nz))
-            stage_c.append(c_swap(blocks[i][1], nz))
-    total = blocks[-1][0][0] + stage_c[-1][0].astype(F32) + stage_x[-1].astype(F32)
-    for partial in stage_z:
-        total = total + partial
+            across[k] = x_swap(far, nz)
+        for k in groups[g - 3] if 0 <= g - 3 < len(groups) else []:
+            partial = keep[k][0] + moved[k][0].astype(F32) + across[k].astype(F32)
+            if k:
+                partial = partial.astype(BF16)
+                started.append(partial)
+                partial = z_shift(partial, k, nz).astype(F32)
+            left[k] = partial
+        if g < len(groups):
+            tied = [after(inputs[0], *started), *inputs[1:]] if started else inputs
+            pairs, vector = backward_blocks(place, groups[g], tied, matrix, nz)
+            inputs = [vector]
+            for k, (mine, sent) in pairs.items():
+                keep[k] = mine
+                moved[k] = c_swap(sent, nz)
+    total = left[0]
+    for k in far_first(nz)[:-1]:
+        total = total + left[k]
     return total
-
-
-def leave(keep, arrived, across):
-    partial = keep[0] + arrived[0].astype(F32) + across.astype(F32)
-    return partial.astype(BF16)
-
-
-def turn_kernel(subtract, own, arrived, base, vector):
-    total = own[...] + arrived[...].astype(F32)
-    if subtract:
-        total = base[...] - total
-    vector[...] = total.T.astype(BF16)
-
-
-def turn(own, arrived, base=None):
-    rows, n = own.shape
-    subtract = base is not None
-    return pl.pallas_call(
-        functools.partial(turn_kernel, subtract),
-        out_shape=jax.ShapeDtypeStruct((n, rows), BF16),
-        in_specs=[VMEM] * 3,
-        out_specs=VMEM,
-        name="turn",
-    )(own, arrived, base if subtract else jnp.zeros((8, n), F32))
 
 
 def push_kernel(nz, place, block, own, arrived, coupling, *refs):
@@ -464,14 +472,21 @@
     shifted = rhs_root - scatter_sum(keep, send, nz)
 
     own, own_b = ring_product(place, shifted.astype(BF16), root_inverse, nz)
-    root_potential = product_scatter(place, turn(own, sub_swap(own_b)), root_inverse, nz)
+    root_potential = product_scatter(
+        place, [own, sub_swap(own_b)], root_inverse, [[k] for k in far_first(nz)], nz
+    )
 
     potential_pieces = gather_pieces(root_potential.astype(BF16), nz)
     own, own_b = pull_product(
         place, block, by_arrival(potential_pieces, nz), coupling_t, nz
     )
+    far = far_first(nz)
     level_potential = product_scatter(
-        place, turn(own, sub_swap(own_b), forward_level), level_inverse, nz
+        place,
+        [own, sub_swap(own_b), forward_level],
+        level_inverse,
+        [far[: nz // 2], far[nz // 2 :]],
+        nz,
     )
     return (root_potential, level_potential)
 

time: 264 us -> 218 us (0.83)
  Pallas kernels: 108 us -> 64.4 us
  starting transfers between devices: 57.6 us -> 68.7 us
  waiting for transfers between devices: 87.2 us -> 79.5 us
  local copies, waits for them, and re-layouts: 5.67 us -> 0.7 us
    pallas_call x19 -> x12, Pallas kernels: 104 us -> 61.1 us  [the longest x6 34.9 us: unit_product(): pl.pallas_call(functools.partial(unit_kernel, blocks, spots, count, acc i...]
    ppermute x15, starting transfers between devices: 17.7 us -> 25.1 us  [z_shift(): lax.ppermute(value, 'front', [(i, (i + shift * width) % count) for i in r...]
    ppermute x15, waiting for transfers between devices: 32.9 us -> 25.7 us  [z_shift(): lax.ppermute(value, 'front', [(i, (i + shift * width) % count) for i in r...]
    unnamed x20 -> x6, local copies, waits for them, and re-layouts: 4.28 us -> 0.01 us
    ppermute x20, starting transfers between devices: 21.1 us -> 25.1 us  [x_swap(): lax.ppermute(value, 'front', [(i, i ^ NC) for i in range(nz * NX * NC)])]
    ppermute x20, waiting for transfers between devices: 30.9 us -> 28.1 us  [x_swap(): lax.ppermute(value, 'front', [(i, i ^ NC) for i in range(nz * NX * NC)])]
  transfers between devices with their start and end apart: 81 -> 81, of which waited for: 30 -> 32; matrix products, arithmetic and copies ran while one was open for 1% -> 1% of each run, Pallas kernels for 30% -> 19%
where the time goes in v4:
time: 218 us
  waiting for transfers between devices  79.5 us (36%)
  starting transfers between devices  68.7 us (32%)
  Pallas kernels  64.4 us (30%)
  other arithmetic  3.82 us (2%)
    pallas_call x6, Pallas kernels, unit_product(): pl.pallas_call(functools.partial(unit_kernel, blocks, spots, count, acc i...  34.9 us
    ppermute x20, waiting for transfers between devices, x_swap(): lax.ppermute(value, 'front', [(i, i ^ NC) for i in range(nz * NX * NC)])  28.1 us
    pallas_call x6, Pallas kernels, backward_blocks(): pl.pallas_call(functools.partial(backward_kernel, ks, Spots(nz), len(inpu...  26.2 us
    ppermute x15, waiting for transfers between devices, z_shift(): lax.ppermute(value, 'front', [(i, (i + shift * width) % count) for i in r...  25.7 us
    ppermute x15, starting transfers between devices, z_shift(): lax.ppermute(value, 'front', [(i, (i + shift * width) % count) for i in r...  25.1 us
    ppermute x20, starting transfers between devices, x_swap(): lax.ppermute(value, 'front', [(i, i ^ NC) for i in range(nz * NX * NC)])  25.1 us
    ppermute x3, waiting for transfers between devices, sub_swap(): return lax.ppermute(value, 'sub', [(0, 1), (1, 0)])  19.2 us
    ppermute x36, starting transfers between devices, c_swap(): lax.ppermute(value, 'front', [(i, i ^ 1) for i in range(nz * NX * NC)])  7.09 us
  transfers between devices with their start and end apart: 81, of which 32 were waited for; matrix products, arithmetic and copies ran while one was open for 1% of the time, Pallas kernels for 19%

profile of v4, /device:TPU:0, one launch (start us, length us, event | category | flops | bytes accessed | tf_op | source)
XLA Modules:
  0.0 218.2 jit_solution(13448154211467636333)
XLA Ops:
  1.7 4.1 %collective-permute-start.11 = (bf16[352,128]{1,0:T(8,128)(2,1)S(1)}, bf16[352,128]{1,0:T(8,128)(2,1)S(1)}, u32[]{:S(2)}, u32[]{:S(2)}) collective-permute-start(bf16[352,128]{1,0:T(8,128)(2,1)S(1)} %convert_element_type.267.refs_0_), channel_id=1, source_target_pairs={{0,8},{1,9},{2,10},{3,11},{4,12},{5,13},{6,14},{7,15},{8,0},{9,1},... | collective-permute-start | bytes 270344 | tf_op jit(solution)/shard_map/ppermute | solution.py:84
  7.4 2.2 %collective-permute-start.3 = (bf16[352,128]{1,0:T(8,128)(2,1)S(1)}, bf16[352,128]{1,0:T(8,128)(2,1)S(1)}, u32[]{:S(2)}, u32[]{:S(2)}) collective-permute-start(bf16[352,128]{1,0:T(8,128)(2,1)S(1)} %convert_element_type.267.refs_0_), channel_id=1, source_target_pairs={{0,12},{1,13},{2,14},{3,15},{4,0},{5,1},{6,2},{7,3},{8,4},{9,5},{1... | collective-permute-start | bytes 270344 | tf_op jit(solution)/shard_map/ppermute | solution.py:84
  11.2 1.9 collective-permute-done.11.refs_12_
  13.1 1.7 collective-permute-start.13
  18.3 2.0 collective-permute-done.9.refs_10_
  23.0 7.0 %unit_product.6 = (f32[704,128]{1,0:T(8,128)S(1)}, bf16[704,128]{1,0:T(8,128)(2,1)S(1)}) custom-call(s32[34]{0:T(128)S(1)} %dynamic-slice_bitcast_fusion.place, bf16[352,128]{1,0:T(8,128)(2,1)S(1)} %convert_element_type.267.refs_0_, bf16[352,128]{1,0:T(8,128)(2,1)S(1)} %collective-permute-done.refs_1_, bf16[352,128]{1,0:T(8,128)(2,1)S(1)} %collective-permute-done.1.refs_2_, ...), custom_call_target="tpu_custom_call" | custom-call | flops 1015021568 | bytes 7929856 | tf_op jit(solution)/shard_map/unit_product/pallas_call | solution.py:294
  30.0 1.6 collective-permute-start.15
  31.6 5.1 %collective-permute-done.15.arrived = bf16[704,128]{1,0:T(8,128)(2,1)S(1)} collective-permute-done((bf16[704,128]{1,0:T(8,128)(2,1)S(1)}, bf16[704,128]{1,0:T(8,128)(2,1)S(1)}, u32[]{:S(2)}, u32[]{:S(2)}) %collective-permute-start.15) | collective-permute-done | bytes 180256 | tf_op jit(solution)/shard_map/ppermute | solution.py:98
  36.7 1.8 push_product.1
  44.8 3.0 %collective-permute-done.17 = bf16[704,128]{1,0:T(8,128)(2,1)S(1)} collective-permute-done((bf16[704,128]{1,0:T(8,128)(2,1)S(1)}, bf16[704,128]{1,0:T(8,128)(2,1)S(1)}, u32[]{:S(2)}, u32[]{:S(2)}) %collective-permute-start.17) | collective-permute-done | bytes 180256 | tf_op jit(solution)/shard_map/ppermute | solution.py:90
  47.8 2.2 %collective-permute-start.18 = (bf16[704,128]{1,0:T(8,128)(2,1)S(1)}, bf16[704,128]{1,0:T(8,128)(2,1)S(1)}, u32[]{:S(2)}, u32[]{:S(2)}) collective-permute-start(bf16[704,128]{1,0:T(8,128)(2,1)S(1)} %fusion.11), channel_id=1, source_target_pairs={{0,8},{1,9},{2,10},{3,11},{4,12},{5,13},{6,14},{7,15},{8,0},{9,1},... | collective-permute-start | bytes 540680 | tf_op jit(solution)/shard_map/ppermute | solution.py:84
  53.3 2.2 %collective-permute-done.23 = bf16[704,128]{1,0:T(8,128)(2,1)S(1)} collective-permute-done((bf16[704,128]{1,0:T(8,128)(2,1)S(1)}, bf16[704,128]{1,0:T(8,128)(2,1)S(1)}, u32[]{:S(2)}, u32[]{:S(2)}) %collective-permute-start.23) | collective-permute-done | bytes 180256 | tf_op jit(solution)/shard_map/ppermute | solution.py:90
  55.8 2.7 %collective-permute-done.26 = bf16[704,128]{1,0:T(8,128)(2,1)S(1)} collective-permute-done((bf16[704,128]{1,0:T(8,128)(2,1)S(1)}, bf16[704,128]{1,0:T(8,128)(2,1)S(1)}, u32[]{:S(2)}, u32[]{:S(2)}) %collective-permute-start.26) | collective-permute-done | bytes 180256 | tf_op jit(solution)/shard_map/ppermute | solution.py:90
  58.5 5.4 %collective-permute-done.21 = bf16[704,128]{1,0:T(8,128)(2,1)S(1)} collective-permute-done((bf16[704,128]{1,0:T(8,128)(2,1)S(1)}, bf16[704,128]{1,0:T(8,128)(2,1)S(1)}, u32[]{:S(2)}, u32[]{:S(2)}) %collective-permute-start.21) | collective-permute-done | bytes 180256 | tf_op jit(solution)/shard_map/ppermute | solution.py:84
  66.2 4.0 %unit_product.7.refs_4_ = f32[1408,128]{1,0:T(8,128)S(1)} custom-call(s32[34]{0:T(128)S(1)} %dynamic-slice_bitcast_fusion.place, bf16[704,128]{1,0:T(8,128)(2,1)S(1)} %fusion.8.refs_0_, bf16[704,128]{1,0:T(8,128)(2,1)S(1)} %collective-permute-done.28.refs_1_, bf16[1408,11264]{1,0:T(8,128)(2,1)} %refs_1_.6), custom_call_target="tpu_custom_call" | custom-call | flops 507510784 | bytes 3964928 | tf_op jit(solution)/shard_map/unit_product/pallas_call | solution.py:294
  72.8 1.7 collective-permute-start.35
  74.8 6.6 %unit_product.8.refs_4_ = f32[1408,128]{1,0:T(8,128)S(1)} custom-call(s32[34]{0:T(128)S(1)} %dynamic-slice_bitcast_fusion.place, bf16[704,128]{1,0:T(8,128)(2,1)S(1)} %collective-permute-done.27.refs_0_, bf16[704,128]{1,0:T(8,128)(2,1)S(1)} %collective-permute-done.30.refs_1_, bf16[704,128]{1,0:T(8,128)(2,1)S(1)} %collective-permute-done.31.refs_2_, ...), custom_call_target="tpu_custom_call" | custom-call | flops 1015021568 | bytes 7929856 | tf_op jit(solution)/shard_map/unit_product/pallas_call | solution.py:294
  82.0 1.7 collective-permute-start.39
  84.1 6.6 %unit_product.9.refs_4_ = f32[1408,128]{1,0:T(8,128)S(1)} custom-call(s32[34]{0:T(128)S(1)} %dynamic-slice_bitcast_fusion.place, bf16[704,128]{1,0:T(8,128)(2,1)S(1)} %collective-permute-done.29.refs_0_, bf16[704,128]{1,0:T(8,128)(2,1)S(1)} %collective-permute-done.34.refs_1_, bf16[704,128]{1,0:T(8,128)(2,1)S(1)} %collective-permute-done.35.refs_2_, ...), custom_call_target="tpu_custom_call" | custom-call | flops 1015021568 | bytes 7929856 | tf_op jit(solution)/shard_map/unit_product/pallas_call | solution.py:294
  92.4 6.6 %unit_product.10.refs_2_ = f32[1408,128]{1,0:T(8,128)S(1)} custom-call(s32[34]{0:T(128)S(1)} %dynamic-slice_bitcast_fusion.place, bf16[704,128]{1,0:T(8,128)(2,1)S(1)} %collective-permute-done.33.refs_0_, bf16[704,128]{1,0:T(8,128)(2,1)S(1)} %collective-permute-done.38.refs_1_, bf16[704,128]{1,0:T(8,128)(2,1)S(1)} %collective-permute-done.39.refs_2_, ...), custom_call_target="tpu_custom_call" | custom-call | flops 1015021568 | bytes 7929856 | tf_op jit(solution)/shard_map/unit_product/pallas_call | solution.py:294
  100.6 4.1 %unit_product.11 = (f32[1408,128]{1,0:T(8,128)S(1)}, bf16[1408,128]{1,0:T(8,128)(2,1)S(1)}) custom-call(s32[34]{0:T(128)S(1)} %dynamic-slice_bitcast_fusion.place, bf16[704,128]{1,0:T(8,128)(2,1)S(1)} %collective-permute-done.37.refs_0_, bf16[704,128]{1,0:T(8,128)(2,1)S(1)} %collective-permute-done.41.refs_1_, f32[1408,128]{1,0:T(8,128)S(1)} %unit_product.10.refs_2_, ...), custom_call_target="tpu_custom_call" | custom-call | flops 507510784 | bytes 3964928 | tf_op jit(solution)/shard_map/unit_product/pallas_call | solution.py:294
  104.6 1.6 collective-permute-start.42
  106.2 9.0 %collective-permute-done.42.refs_1_ = bf16[1408,128]{1,0:T(8,128)(2,1)S(1)} collective-permute-done((bf16[1408,128]{1,0:T(8,128)(2,1)S(1)}, bf16[1408,128]{1,0:T(8,128)(2,1)S(1)}, u32[]{:S(2)}, u32[]{:S(2)}) %collective-permute-start.42) | collective-permute-done | bytes 360480 | tf_op jit(solution)/shard_map/ppermute | solution.py:98
  115.2 4.9 %backward_blocks.6 = (f32[2,704,128]{2,1,0:T(8,128)S(1)}, bf16[2,704,128]{2,1,0:T(8,128)(2,1)S(1)}, bf16[128,1408]{1,0:T(8,128)(2,1)S(1)}) custom-call(s32[34]{0:T(128)S(1)} %dynamic-slice_bitcast_fusion.place, f32[1408,128]{1,0:T(8,128)S(1)} %get-tuple-element.61.refs_0_, bf16[1408,128]{1,0:T(8,128)(2,1)S(1)} %collective-permute-done.42.refs_1_, ...), custom_call_target="tpu_custom_call" | custom-call | flops 1015021568 | bytes 7929856 | tf_op jit(solution)/shard_map/backward_blocks/pallas_call | solution.py:347
  120.2 4.8 %backward_blocks.7 = (f32[2,704,128]{2,1,0:T(8,128)S(1)}, bf16[2,704,128]{2,1,0:T(8,128)(2,1)S(1)}) custom-call(s32[34]{0:T(128)S(1)} %dynamic-slice_bitcast_fusion.place, bf16[128,1408]{1,0:T(8,128)(2,1)S(1)} %get-tuple-element.69.refs_0_, bf16[1408,11264]{1,0:T(8,128)(2,1)} %refs_1_.6), custom_call_target="tpu_custom_call" | custom-call | flops 1015021568 | bytes 7929856 | tf_op jit(solution)/shard_map/backward_blocks/pallas_call | solution.py:347
  125.7 1.8 collective-permute-start.45
  127.5 4.8 %backward_blocks.9 = (f32[2,704,128]{2,1,0:T(8,128)S(1)}, bf16[2,704,128]{2,1,0:T(8,128)(2,1)S(1)}) custom-call(s32[34]{0:T(128)S(1)} %dynamic-slice_bitcast_fusion.place, bf16[128,1408]{1,0:T(8,128)(2,1)S(1)} %get-tuple-element.69.refs_0_, bf16[1408,11264]{1,0:T(8,128)(2,1)} %refs_1_.6), custom_call_target="tpu_custom_call" | custom-call | flops 1015021568 | bytes 7929856 | tf_op jit(solution)/shard_map/backward_blocks/pallas_call | solution.py:347
  132.9 1.8 collective-permute-start.48
  134.7 4.9 %backward_blocks.8 = (f32[2,704,128]{2,1,0:T(8,128)S(1)}, bf16[2,704,128]{2,1,0:T(8,128)(2,1)S(1)}) custom-call(s32[34]{0:T(128)S(1)} %dynamic-slice_bitcast_fusion.place, bf16[128,1408]{1,0:T(8,128)(2,1)S(1)} %get-tuple-element.69.refs_0_, bf16[1408,11264]{1,0:T(8,128)(2,1)} %refs_1_.6), custom_call_target="tpu_custom_call" | custom-call | flops 1015021568 | bytes 7929856 | tf_op jit(solution)/shard_map/backward_blocks/pallas_call | solution.py:347
  139.7 1.8 collective-permute-start.52
  143.1 3.6 %collective-permute-done.52 = bf16[704,128]{1,0:T(8,128)(2,1)S(1)} collective-permute-done((bf16[704,128]{1,0:T(8,128)(2,1)S(1)}, bf16[704,128]{1,0:T(8,128)(2,1)S(1)}, u32[]{:S(2)}, u32[]{:S(2)}) %collective-permute-start.52) | collective-permute-done | bytes 180256 | tf_op jit(solution)/shard_map/ppermute | solution.py:90
  149.7 5.4 %collective-permute-done.53 = bf16[704,128]{1,0:T(8,128)(2,1)S(1)} collective-permute-done((bf16[704,128]{1,0:T(8,128)(2,1)S(1)}, bf16[704,128]{1,0:T(8,128)(2,1)S(1)}, u32[]{:S(2)}, u32[]{:S(2)}) %collective-permute-start.53) | collective-permute-done | bytes 180256 | tf_op jit(solution)/shard_map/ppermute | solution.py:84
  156.1 2.2 %collective-permute-start.61 = (bf16[704,128]{1,0:T(8,128)(2,1)S(1)}, bf16[704,128]{1,0:T(8,128)(2,1)S(1)}, u32[]{:S(2)}, u32[]{:S(2)}) collective-permute-start(bf16[704,128]{1,0:T(8,128)(2,1)S(1)} %get-tuple-element.86.refs_0_), channel_id=1, source_target_pairs={{0,4},{1,5},{2,6},{3,7},{4,8},{5,9},{6,10},{7,11},{8,12},{9,13},{1... | collective-permute-start | bytes 540680 | tf_op jit(solution)/shard_map/ppermute | solution.py:84
  158.4 1.6 collective-permute-start.57
  160.0 1.6 collective-permute-start.55
  161.6 7.3 %collective-permute-done.65.refs_12_ = bf16[704,128]{1,0:T(8,128)(2,1)S(1)} collective-permute-done((bf16[704,128]{1,0:T(8,128)(2,1)S(1)}, bf16[704,128]{1,0:T(8,128)(2,1)S(1)}, u32[]{:S(2)}, u32[]{:S(2)}) %collective-permute-start.65) | collective-permute-done | bytes 180256 | tf_op jit(solution)/shard_map/ppermute | solution.py:84
  168.9 1.7 collective-permute-start.67
  172.8 3.5 %collective-permute-done.67.refs_14_ = bf16[704,128]{1,0:T(8,128)(2,1)S(1)} collective-permute-done((bf16[704,128]{1,0:T(8,128)(2,1)S(1)}, bf16[704,128]{1,0:T(8,128)(2,1)S(1)}, u32[]{:S(2)}, u32[]{:S(2)}) %collective-permute-start.67) | collective-permute-done | bytes 180256 | tf_op jit(solution)/shard_map/ppermute | solution.py:90
  176.8 3.3 %collective-permute-done.63.refs_10_ = bf16[704,128]{1,0:T(8,128)(2,1)S(1)} collective-permute-done((bf16[704,128]{1,0:T(8,128)(2,1)S(1)}, bf16[704,128]{1,0:T(8,128)(2,1)S(1)}, u32[]{:S(2)}, u32[]{:S(2)}) %collective-permute-start.63) | collective-permute-done | bytes 180256 | tf_op jit(solution)/shard_map/ppermute | solution.py:90
  180.7 2.3 %collective-permute-done.59.refs_6_ = bf16[704,128]{1,0:T(8,128)(2,1)S(1)} collective-permute-done((bf16[704,128]{1,0:T(8,128)(2,1)S(1)}, bf16[704,128]{1,0:T(8,128)(2,1)S(1)}, u32[]{:S(2)}, u32[]{:S(2)}) %collective-permute-start.59) | collective-permute-done | bytes 180256 | tf_op jit(solution)/shard_map/ppermute | solution.py:90
  187.4 5.1 %collective-permute-done.69.refs_1_ = bf16[704,128]{1,0:T(8,128)(2,1)S(1)} collective-permute-done((bf16[704,128]{1,0:T(8,128)(2,1)S(1)}, bf16[704,128]{1,0:T(8,128)(2,1)S(1)}, u32[]{:S(2)}, u32[]{:S(2)}) %collective-permute-start.69) | collective-permute-done | bytes 180256 | tf_op jit(solution)/shard_map/ppermute | solution.py:98
  192.5 3.4 %backward_blocks.10 = (f32[2,352,128]{2,1,0:T(8,128)S(1)}, bf16[2,352,128]{2,1,0:T(8,128)(2,1)S(1)}, f32[2,352,128]{2,1,0:T(8,128)S(1)}, bf16[2,352,128]{2,1,0:T(8,128)(2,1)S(1)}, bf16[128,704]{1,0:T(8,128)(2,1)S(1)}) custom-call(s32[34]{0:T(128)S(1)} %dynamic-slice_bitcast_fusion.place, f32[704,128]{1,0:T(8,128)S(1)} %get-tuple-element.74.refs_0_, ...), custom_call_target="tpu_custom_call" | custom-call | flops 507510784 | bytes 3964928 | tf_op jit(solution)/shard_map/backward_blocks/pallas_call | solution.py:347
  196.5 3.4 %backward_blocks.11 = (f32[2,352,128]{2,1,0:T(8,128)S(1)}, bf16[2,352,128]{2,1,0:T(8,128)(2,1)S(1)}, f32[2,352,128]{2,1,0:T(8,128)S(1)}, bf16[2,352,128]{2,1,0:T(8,128)(2,1)S(1)}) custom-call(s32[34]{0:T(128)S(1)} %dynamic-slice_bitcast_fusion.place, bf16[128,704]{1,0:T(8,128)(2,1)S(1)} %get-tuple-element.77.refs_0_, bf16[704,5632]{1,0:T(8,128)(2,1)} %refs_1_.7), custom_call_target="tpu_custom_call" | custom-call | flops 507510784 | bytes 3964928 | tf_op jit(solution)/shard_map/backward_blocks/pallas_call | solution.py:347
  200.5 1.8 collective-permute-start.73
  202.8 1.8 collective-permute-start.71
  205.7 1.9 collective-permute-start.74
  208.0 1.8 collective-permute-start.77
  213.3 4.2 %collective-permute-done.80 = bf16[352,128]{1,0:T(8,128)(2,1)S(1)} collective-permute-done((bf16[352,128]{1,0:T(8,128)(2,1)S(1)}, bf16[352,128]{1,0:T(8,128)(2,1)S(1)}, u32[]{:S(2)}, u32[]{:S(2)}) %collective-permute-start.80) | collective-permute-done | bytes 90144 | tf_op jit(solution)/shard_map/ppermute | solution.py:84
  (161 shorter events, 51.5 us)
Async XLA Ops:
  1.7 11.3 %collective-permute-start.11 = (bf16[352,128]{1,0:T(8,128)(2,1)S(1)}, bf16[352,128]{1,0:T(8,128)(2,1)S(1)}, u32[]{:S(2)}, u32[]{:S(2)}) collective-permute-start(bf16[352,128]{1,0:T(8,128)(2,1)S(1)} %convert_element_type.267.refs_0_), channel_id=1, source_target_pairs={{0,8},{1,9},{2,10},{3,11},{4,12},{5,13},{6,14},{7,15},{8,0},{9,1},... | collective-permute-start | bytes 270344 | tf_op jit(solution)/shard_map/ppermute | solution.py:84
  5.8 8.9 %collective-permute-start.7 = (bf16[352,128]{1,0:T(8,128)(2,1)S(1)}, bf16[352,128]{1,0:T(8,128)(2,1)S(1)}, u32[]{:S(2)}, u32[]{:S(2)}) collective-permute-start(bf16[352,128]{1,0:T(8,128)(2,1)S(1)} %convert_element_type.267.refs_0_), channel_id=1, source_target_pairs={{0,4},{1,5},{2,6},{3,7},{4,8},{5,9},{6,10},{7,11},{8,12},{9,13},{1... | collective-permute-start | bytes 270344 | tf_op jit(solution)/shard_map/ppermute | solution.py:84
  7.4 7.3 %collective-permute-start.3 = (bf16[352,128]{1,0:T(8,128)(2,1)S(1)}, bf16[352,128]{1,0:T(8,128)(2,1)S(1)}, u32[]{:S(2)}, u32[]{:S(2)}) collective-permute-start(bf16[352,128]{1,0:T(8,128)(2,1)S(1)} %convert_element_type.267.refs_0_), channel_id=1, source_target_pairs={{0,12},{1,13},{2,14},{3,15},{4,0},{5,1},{6,2},{7,3},{8,4},{9,5},{1... | collective-permute-start | bytes 270344 | tf_op jit(solution)/shard_map/ppermute | solution.py:84
  9.7 5.8 %collective-permute-start.1 = (bf16[352,128]{1,0:T(8,128)(2,1)S(1)}, bf16[352,128]{1,0:T(8,128)(2,1)S(1)}, u32[]{:S(2)}, u32[]{:S(2)}) collective-permute-start(bf16[352,128]{1,0:T(8,128)(2,1)S(1)} %convert_element_type.267.refs_0_), channel_id=1, source_target_pairs={{0,2},{1,3},{2,0},{3,1},{4,6},{5,7},{6,4},{7,5},{8,10},{9,11},{10,... | collective-permute-start | bytes 270344 | tf_op jit(solution)/shard_map/ppermute | solution.py:90
  15.4 6.3 %collective-permute-start.5 = (bf16[352,128]{1,0:T(8,128)(2,1)S(1)}, bf16[352,128]{1,0:T(8,128)(2,1)S(1)}, u32[]{:S(2)}, u32[]{:S(2)}) collective-permute-start(bf16[352,128]{1,0:T(8,128)(2,1)S(1)} %collective-permute-done.3.refs_4_), channel_id=1, source_target_pairs={{0,2},{1,3},{2,0},{3,1},{4,6},{5,7},{6,4},{7,5},{8,10},{9,11},{10,... | collective-permute-start | bytes 270344 | tf_op jit(solution)/shard_map/ppermute | solution.py:90
  30.0 6.7 %collective-permute-start.15 = (bf16[704,128]{1,0:T(8,128)(2,1)S(1)}, bf16[704,128]{1,0:T(8,128)(2,1)S(1)}, u32[]{:S(2)}, u32[]{:S(2)}) collective-permute-start(bf16[704,128]{1,0:T(8,128)(2,1)S(1)} %get-tuple-element.45), channel_id=1, source_target_pairs={{0,16},{16,0},{1,17},{17,1},{2,18},{18,2},{3,19},{19,3},{4,20},{20... | collective-permute-start | bytes 540680 | tf_op jit(solution)/shard_map/ppermute | solution.py:98
  40.3 7.5 %collective-permute-start.17 = (bf16[704,128]{1,0:T(8,128)(2,1)S(1)}, bf16[704,128]{1,0:T(8,128)(2,1)S(1)}, u32[]{:S(2)}, u32[]{:S(2)}) collective-permute-start(bf16[704,128]{1,0:T(8,128)(2,1)S(1)} %fusion.12), channel_id=1, source_target_pairs={{0,2},{1,3},{2,0},{3,1},{4,6},{5,7},{6,4},{7,5},{8,10},{9,11},{10,... | collective-permute-start | bytes 540680 | tf_op jit(solution)/shard_map/ppermute | solution.py:90
  41.7 9.9 %collective-permute-start.20 = (bf16[704,128]{1,0:T(8,128)(2,1)S(1)}, bf16[704,128]{1,0:T(8,128)(2,1)S(1)}, u32[]{:S(2)}, u32[]{:S(2)}) collective-permute-start(bf16[704,128]{1,0:T(8,128)(2,1)S(1)} %fusion.13), channel_id=1, source_target_pairs={{0,2},{1,3},{2,0},{3,1},{4,6},{5,7},{6,4},{7,5},{8,10},{9,11},{10,... | collective-permute-start | bytes 540680 | tf_op jit(solution)/shard_map/ppermute | solution.py:90
  42.6 12.9 %collective-permute-start.23 = (bf16[704,128]{1,0:T(8,128)(2,1)S(1)}, bf16[704,128]{1,0:T(8,128)(2,1)S(1)}, u32[]{:S(2)}, u32[]{:S(2)}) collective-permute-start(bf16[704,128]{1,0:T(8,128)(2,1)S(1)} %fusion.14), channel_id=1, source_target_pairs={{0,2},{1,3},{2,0},{3,1},{4,6},{5,7},{6,4},{7,5},{8,10},{9,11},{10,... | collective-permute-start | bytes 540680 | tf_op jit(solution)/shard_map/ppermute | solution.py:90
  44.0 14.6 %collective-permute-start.26 = (bf16[704,128]{1,0:T(8,128)(2,1)S(1)}, bf16[704,128]{1,0:T(8,128)(2,1)S(1)}, u32[]{:S(2)}, u32[]{:S(2)}) collective-permute-start(bf16[704,128]{1,0:T(8,128)(2,1)S(1)} %fusion.15), channel_id=1, source_target_pairs={{0,2},{1,3},{2,0},{3,1},{4,6},{5,7},{6,4},{7,5},{8,10},{9,11},{10,... | collective-permute-start | bytes 540680 | tf_op jit(solution)/shard_map/ppermute | solution.py:90
  47.8 10.7 %collective-permute-start.18 = (bf16[704,128]{1,0:T(8,128)(2,1)S(1)}, bf16[704,128]{1,0:T(8,128)(2,1)S(1)}, u32[]{:S(2)}, u32[]{:S(2)}) collective-permute-start(bf16[704,128]{1,0:T(8,128)(2,1)S(1)} %fusion.11), channel_id=1, source_target_pairs={{0,8},{1,9},{2,10},{3,11},{4,12},{5,13},{6,14},{7,15},{8,0},{9,1},... | collective-permute-start | bytes 540680 | tf_op jit(solution)/shard_map/ppermute | solution.py:84
  51.7 12.2 %collective-permute-start.21 = (bf16[704,128]{1,0:T(8,128)(2,1)S(1)}, bf16[704,128]{1,0:T(8,128)(2,1)S(1)}, u32[]{:S(2)}, u32[]{:S(2)}) collective-permute-start(bf16[704,128]{1,0:T(8,128)(2,1)S(1)} %fusion.10), channel_id=1, source_target_pairs={{0,12},{1,13},{2,14},{3,15},{4,0},{5,1},{6,2},{7,3},{8,4},{9,5},{1... | collective-permute-start | bytes 540680 | tf_op jit(solution)/shard_map/ppermute | solution.py:84
  55.6 8.3 %collective-permute-start.24 = (bf16[704,128]{1,0:T(8,128)(2,1)S(1)}, bf16[704,128]{1,0:T(8,128)(2,1)S(1)}, u32[]{:S(2)}, u32[]{:S(2)}) collective-permute-start(bf16[704,128]{1,0:T(8,128)(2,1)S(1)} %fusion.9), channel_id=1, source_target_pairs={{0,4},{1,5},{2,6},{3,7},{4,8},{5,9},{6,10},{7,11},{8,12},{9,13},{1... | collective-permute-start | bytes 540680 | tf_op jit(solution)/shard_map/ppermute | solution.py:84
  64.2 7.0 %collective-permute-start.31 = (bf16[704,128]{1,0:T(8,128)(2,1)S(1)}, bf16[704,128]{1,0:T(8,128)(2,1)S(1)}, u32[]{:S(2)}, u32[]{:S(2)}) collective-permute-start(bf16[704,128]{1,0:T(8,128)(2,1)S(1)} %fusion.8.refs_0_), channel_id=1, source_target_pairs={{0,2},{1,3},{4,0},{5,1},{8,4},{9,5},{12,8},{13,9},{14,12},{15,13},... | collective-permute-start | bytes 540680 | tf_op jit(solution)/shard_map/ppermute | solution.py:143
  65.5 6.8 %collective-permute-start.27 = (bf16[704,128]{1,0:T(8,128)(2,1)S(1)}, bf16[704,128]{1,0:T(8,128)(2,1)S(1)}, u32[]{:S(2)}, u32[]{:S(2)}) collective-permute-start(bf16[704,128]{1,0:T(8,128)(2,1)S(1)} %fusion.8.refs_0_), channel_id=1, source_target_pairs={{0,4},{1,5},{4,8},{5,9},{8,12},{9,13},{12,14},{13,15},{14,10},{15,... | collective-permute-start | bytes 540680 | tf_op jit(solution)/shard_map/ppermute | solution.py:143
  72.8 8.7 %collective-permute-start.35 = (bf16[704,128]{1,0:T(8,128)(2,1)S(1)}, bf16[704,128]{1,0:T(8,128)(2,1)S(1)}, u32[]{:S(2)}, u32[]{:S(2)}) collective-permute-start(bf16[704,128]{1,0:T(8,128)(2,1)S(1)} %collective-permute-done.31.refs_2_), channel_id=1, source_target_pairs={{0,2},{1,3},{4,0},{5,1},{8,4},{9,5},{12,8},{13,9},{14,12},{15,13},... | collective-permute-start | bytes 540680 | tf_op jit(solution)/shard_map/ppermute | solution.py:143
  74.5 6.9 %collective-permute-start.29 = (bf16[704,128]{1,0:T(8,128)(2,1)S(1)}, bf16[704,128]{1,0:T(8,128)(2,1)S(1)}, u32[]{:S(2)}, u32[]{:S(2)}) collective-permute-start(bf16[704,128]{1,0:T(8,128)(2,1)S(1)} %collective-permute-done.27.refs_0_), channel_id=1, source_target_pairs={{0,4},{1,5},{4,8},{5,9},{8,12},{9,13},{12,14},{13,15},{14,10},{15,... | collective-permute-start | bytes 540680 | tf_op jit(solution)/shard_map/ppermute | solution.py:143
  82.0 8.6 %collective-permute-start.39 = (bf16[704,128]{1,0:T(8,128)(2,1)S(1)}, bf16[704,128]{1,0:T(8,128)(2,1)S(1)}, u32[]{:S(2)}, u32[]{:S(2)}) collective-permute-start(bf16[704,128]{1,0:T(8,128)(2,1)S(1)} %collective-permute-done.35.refs_2_), channel_id=1, source_target_pairs={{0,2},{1,3},{4,0},{5,1},{8,4},{9,5},{12,8},{13,9},{14,12},{15,13},... | collective-permute-start | bytes 540680 | tf_op jit(solution)/shard_map/ppermute | solution.py:143
  83.8 6.9 %collective-permute-start.33 = (bf16[704,128]{1,0:T(8,128)(2,1)S(1)}, bf16[704,128]{1,0:T(8,128)(2,1)S(1)}, u32[]{:S(2)}, u32[]{:S(2)}) collective-permute-start(bf16[704,128]{1,0:T(8,128)(2,1)S(1)} %collective-permute-done.29.refs_0_), channel_id=1, source_target_pairs={{0,4},{1,5},{4,8},{5,9},{8,12},{9,13},{12,14},{13,15},{14,10},{15,... | collective-permute-start | bytes 540680 | tf_op jit(solution)/shard_map/ppermute | solution.py:143
  91.3 7.8 %collective-permute-start.37 = (bf16[704,128]{1,0:T(8,128)(2,1)S(1)}, bf16[704,128]{1,0:T(8,128)(2,1)S(1)}, u32[]{:S(2)}, u32[]{:S(2)}) collective-permute-start(bf16[704,128]{1,0:T(8,128)(2,1)S(1)} %collective-permute-done.33.refs_0_), channel_id=1, source_target_pairs={{0,4},{1,5},{4,8},{5,9},{8,12},{9,13},{12,14},{13,15},{14,10},{15,... | collective-permute-start | bytes 540680 | tf_op jit(solution)/shard_map/ppermute | solution.py:143
  104.6 10.6 %collective-permute-start.42 = (bf16[1408,128]{1,0:T(8,128)(2,1)S(1)}, bf16[1408,128]{1,0:T(8,128)(2,1)S(1)}, u32[]{:S(2)}, u32[]{:S(2)}) collective-permute-start(bf16[1408,128]{1,0:T(8,128)(2,1)S(1)} %get-tuple-element.62), channel_id=1, source_target_pairs={{0,16},{16,0},{1,17},{17,1},{2,18},{18,2},{3,19},{19,3},{4,20},{20... | collective-permute-start | bytes 1081352 | tf_op jit(solution)/shard_map/ppermute | solution.py:98
  125.1 7.3 %collective-permute-start.44 = (bf16[2,704,128]{2,1,0:T(8,128)(2,1)S(1)}, bf16[2,704,128]{2,1,0:T(8,128)(2,1)S(1)}, u32[]{:S(2)}, u32[]{:S(2)}) collective-permute-start(bf16[2,704,128]{2,1,0:T(8,128)(2,1)S(1)} %get-tuple-element.68), channel_id=1, source_target_pairs={{0,1},{1,0},{2,3},{3,2},{4,5},{5,4},{6,7},{7,6},{8,9},{9,8},{10,11... | collective-permute-start | bytes 1081352 | tf_op jit(solution)/shard_map/ppermute | solution.py:94
  125.7 7.1 %collective-permute-start.45 = (bf16[704,128]{1,0:T(8,128)(2,1)S(1)}, bf16[704,128]{1,0:T(8,128)(2,1)S(1)}, u32[]{:S(2)}, u32[]{:S(2)}) collective-permute-start(bf16[704,128]{1,0:T(8,128)(2,1)S(1)} %fusion.16), channel_id=1, source_target_pairs={{0,2},{1,3},{2,0},{3,1},{4,6},{5,7},{6,4},{7,5},{8,10},{9,11},{10,... | collective-permute-start | bytes 540680 | tf_op jit(solution)/shard_map/ppermute | solution.py:90
  132.3 7.3 %collective-permute-start.51 = (bf16[2,704,128]{2,1,0:T(8,128)(2,1)S(1)}, bf16[2,704,128]{2,1,0:T(8,128)(2,1)S(1)}, u32[]{:S(2)}, u32[]{:S(2)}) collective-permute-start(bf16[2,704,128]{2,1,0:T(8,128)(2,1)S(1)} %get-tuple-element.73), channel_id=1, source_target_pairs={{0,1},{1,0},{2,3},{3,2},{4,5},{5,4},{6,7},{7,6},{8,9},{9,8},{10,11... | collective-permute-start | bytes 1081352 | tf_op jit(solution)/shard_map/ppermute | solution.py:94
  132.5 9.1 %collective-permute-start.49 = (bf16[704,128]{1,0:T(8,128)(2,1)S(1)}, bf16[704,128]{1,0:T(8,128)(2,1)S(1)}, u32[]{:S(2)}, u32[]{:S(2)}) collective-permute-start(bf16[704,128]{1,0:T(8,128)(2,1)S(1)} %fusion.17), channel_id=1, source_target_pairs={{0,2},{1,3},{2,0},{3,1},{4,6},{5,7},{6,4},{7,5},{8,10},{9,11},{10,... | collective-permute-start | bytes 540680 | tf_op jit(solution)/shard_map/ppermute | solution.py:90
  132.9 16.8 %collective-permute-start.48 = (bf16[704,128]{1,0:T(8,128)(2,1)S(1)}, bf16[704,128]{1,0:T(8,128)(2,1)S(1)}, u32[]{:S(2)}, u32[]{:S(2)}) collective-permute-start(bf16[704,128]{1,0:T(8,128)(2,1)S(1)} %fusion.5), channel_id=1, source_target_pairs={{0,8},{1,9},{2,10},{3,11},{4,12},{5,13},{6,14},{7,15},{8,0},{9,1},... | collective-permute-start | bytes 540680 | tf_op jit(solution)/shard_map/ppermute | solution.py:84
  139.6 8.6 %collective-permute-start.46 = (bf16[2,704,128]{2,1,0:T(8,128)(2,1)S(1)}, bf16[2,704,128]{2,1,0:T(8,128)(2,1)S(1)}, u32[]{:S(2)}, u32[]{:S(2)}) collective-permute-start(bf16[2,704,128]{2,1,0:T(8,128)(2,1)S(1)} %get-tuple-element.71), channel_id=1, source_target_pairs={{0,1},{1,0},{2,3},{3,2},{4,5},{5,4},{6,7},{7,6},{8,9},{9,8},{10,11... | collective-permute-start | bytes 1081352 | tf_op jit(solution)/shard_map/ppermute | solution.py:94
  139.7 7.0 %collective-permute-start.52 = (bf16[704,128]{1,0:T(8,128)(2,1)S(1)}, bf16[704,128]{1,0:T(8,128)(2,1)S(1)}, u32[]{:S(2)}, u32[]{:S(2)}) collective-permute-start(bf16[704,128]{1,0:T(8,128)(2,1)S(1)} %fusion.19), channel_id=1, source_target_pairs={{0,2},{1,3},{2,0},{3,1},{4,6},{5,7},{6,4},{7,5},{8,10},{9,11},{10,... | collective-permute-start | bytes 540680 | tf_op jit(solution)/shard_map/ppermute | solution.py:90
  141.6 8.1 %collective-permute-start.50 = (bf16[704,128]{1,0:T(8,128)(2,1)S(1)}, bf16[704,128]{1,0:T(8,128)(2,1)S(1)}, u32[]{:S(2)}, u32[]{:S(2)}) collective-permute-start(bf16[704,128]{1,0:T(8,128)(2,1)S(1)} %fusion.1), channel_id=1, source_target_pairs={{0,12},{1,13},{2,14},{3,15},{4,0},{5,1},{6,2},{7,3},{8,4},{9,5},{1... | collective-permute-start | bytes 540680 | tf_op jit(solution)/shard_map/ppermute | solution.py:84
  146.8 8.3 %collective-permute-start.53 = (bf16[704,128]{1,0:T(8,128)(2,1)S(1)}, bf16[704,128]{1,0:T(8,128)(2,1)S(1)}, u32[]{:S(2)}, u32[]{:S(2)}) collective-permute-start(bf16[704,128]{1,0:T(8,128)(2,1)S(1)} %fusion), channel_id=1, source_target_pairs={{0,4},{1,5},{2,6},{3,7},{4,8},{5,9},{6,10},{7,11},{8,12},{9,13},{1... | collective-permute-start | bytes 540680 | tf_op jit(solution)/shard_map/ppermute | solution.py:84
  148.2 6.9 %collective-permute-start.47 = (bf16[704,128]{1,0:T(8,128)(2,1)S(1)}, bf16[704,128]{1,0:T(8,128)(2,1)S(1)}, u32[]{:S(2)}, u32[]{:S(2)}) collective-permute-start(bf16[704,128]{1,0:T(8,128)(2,1)S(1)} %fusion.18), channel_id=1, source_target_pairs={{0,2},{1,3},{2,0},{3,1},{4,6},{5,7},{6,4},{7,5},{8,10},{9,11},{10,... | collective-permute-start | bytes 540680 | tf_op jit(solution)/shard_map/ppermute | solution.py:90
  156.0 12.9 %collective-permute-start.65 = (bf16[704,128]{1,0:T(8,128)(2,1)S(1)}, bf16[704,128]{1,0:T(8,128)(2,1)S(1)}, u32[]{:S(2)}, u32[]{:S(2)}) collective-permute-start(bf16[704,128]{1,0:T(8,128)(2,1)S(1)} %get-tuple-element.86.refs_0_), channel_id=1, source_target_pairs={{0,8},{1,9},{2,10},{3,11},{4,12},{5,13},{6,14},{7,15},{8,0},{9,1},... | collective-permute-start | bytes 540680 | tf_op jit(solution)/shard_map/ppermute | solution.py:84
  156.1 14.4 %collective-permute-start.61 = (bf16[704,128]{1,0:T(8,128)(2,1)S(1)}, bf16[704,128]{1,0:T(8,128)(2,1)S(1)}, u32[]{:S(2)}, u32[]{:S(2)}) collective-permute-start(bf16[704,128]{1,0:T(8,128)(2,1)S(1)} %get-tuple-element.86.refs_0_), channel_id=1, source_target_pairs={{0,4},{1,5},{2,6},{3,7},{4,8},{5,9},{6,10},{7,11},{8,12},{9,13},{1... | collective-permute-start | bytes 540680 | tf_op jit(solution)/shard_map/ppermute | solution.py:84
  158.4 12.2 %collective-permute-start.57 = (bf16[704,128]{1,0:T(8,128)(2,1)S(1)}, bf16[704,128]{1,0:T(8,128)(2,1)S(1)}, u32[]{:S(2)}, u32[]{:S(2)}) collective-permute-start(bf16[704,128]{1,0:T(8,128)(2,1)S(1)} %get-tuple-element.86.refs_0_), channel_id=1, source_target_pairs={{0,12},{1,13},{2,14},{3,15},{4,0},{5,1},{6,2},{7,3},{8,4},{9,5},{1... | collective-permute-start | bytes 540680 | tf_op jit(solution)/shard_map/ppermute | solution.py:84
  160.0 12.2 %collective-permute-start.55 = (bf16[704,128]{1,0:T(8,128)(2,1)S(1)}, bf16[704,128]{1,0:T(8,128)(2,1)S(1)}, u32[]{:S(2)}, u32[]{:S(2)}) collective-permute-start(bf16[704,128]{1,0:T(8,128)(2,1)S(1)} %get-tuple-element.86.refs_0_), channel_id=1, source_target_pairs={{0,2},{1,3},{2,0},{3,1},{4,6},{5,7},{6,4},{7,5},{8,10},{9,11},{10,... | collective-permute-start | bytes 540680 | tf_op jit(solution)/shard_map/ppermute | solution.py:90
  161.6 10.6 %collective-permute-start.54 = (bf16[704,128]{1,0:T(8,128)(2,1)S(1)}, bf16[704,128]{1,0:T(8,128)(2,1)S(1)}, u32[]{:S(2)}, u32[]{:S(2)}) collective-permute-start(bf16[704,128]{1,0:T(8,128)(2,1)S(1)} %get-tuple-element.86.refs_0_), channel_id=1, source_target_pairs={{0,1},{1,0},{2,3},{3,2},{4,5},{5,4},{6,7},{7,6},{8,9},{9,8},{10,11... | collective-permute-start | bytes 540680 | tf_op jit(solution)/shard_map/ppermute | solution.py:94
  168.9 7.4 %collective-permute-start.67 = (bf16[704,128]{1,0:T(8,128)(2,1)S(1)}, bf16[704,128]{1,0:T(8,128)(2,1)S(1)}, u32[]{:S(2)}, u32[]{:S(2)}) collective-permute-start(bf16[704,128]{1,0:T(8,128)(2,1)S(1)} %collective-permute-done.65.refs_12_), channel_id=1, source_target_pairs={{0,2},{1,3},{2,0},{3,1},{4,6},{5,7},{6,4},{7,5},{8,10},{9,11},{10,... | collective-permute-start | bytes 540680 | tf_op jit(solution)/shard_map/ppermute | solution.py:90
  170.6 9.6 %collective-permute-start.63 = (bf16[704,128]{1,0:T(8,128)(2,1)S(1)}, bf16[704,128]{1,0:T(8,128)(2,1)S(1)}, u32[]{:S(2)}, u32[]{:S(2)}) collective-permute-start(bf16[704,128]{1,0:T(8,128)(2,1)S(1)} %collective-permute-done.61.refs_8_), channel_id=1, source_target_pairs={{0,2},{1,3},{2,0},{3,1},{4,6},{5,7},{6,4},{7,5},{8,10},{9,11},{10,... | collective-permute-start | bytes 540680 | tf_op jit(solution)/shard_map/ppermute | solution.py:90
  172.2 8.0 %collective-permute-start.62 = (bf16[704,128]{1,0:T(8,128)(2,1)S(1)}, bf16[704,128]{1,0:T(8,128)(2,1)S(1)}, u32[]{:S(2)}, u32[]{:S(2)}) collective-permute-start(bf16[704,128]{1,0:T(8,128)(2,1)S(1)} %collective-permute-done.61.refs_8_), channel_id=1, source_target_pairs={{0,1},{1,0},{2,3},{3,2},{4,5},{5,4},{6,7},{7,6},{8,9},{9,8},{10,11... | collective-permute-start | bytes 540680 | tf_op jit(solution)/shard_map/ppermute | solution.py:94
  172.2 10.8 %collective-permute-start.59 = (bf16[704,128]{1,0:T(8,128)(2,1)S(1)}, bf16[704,128]{1,0:T(8,128)(2,1)S(1)}, u32[]{:S(2)}, u32[]{:S(2)}) collective-permute-start(bf16[704,128]{1,0:T(8,128)(2,1)S(1)} %collective-permute-done.57.refs_4_), channel_id=1, source_target_pairs={{0,2},{1,3},{2,0},{3,1},{4,6},{5,7},{6,4},{7,5},{8,10},{9,11},{10,... | collective-permute-start | bytes 540680 | tf_op jit(solution)/shard_map/ppermute | solution.py:90
  176.3 6.7 %collective-permute-start.58 = (bf16[704,128]{1,0:T(8,128)(2,1)S(1)}, bf16[704,128]{1,0:T(8,128)(2,1)S(1)}, u32[]{:S(2)}, u32[]{:S(2)}) collective-permute-start(bf16[704,128]{1,0:T(8,128)(2,1)S(1)} %collective-permute-done.57.refs_4_), channel_id=1, source_target_pairs={{0,1},{1,0},{2,3},{3,2},{4,5},{5,4},{6,7},{7,6},{8,9},{9,8},{10,11... | collective-permute-start | bytes 540680 | tf_op jit(solution)/shard_map/ppermute | solution.py:94
  176.3 6.7 %collective-permute-start.56 = (bf16[704,128]{1,0:T(8,128)(2,1)S(1)}, bf16[704,128]{1,0:T(8,128)(2,1)S(1)}, u32[]{:S(2)}, u32[]{:S(2)}) collective-permute-start(bf16[704,128]{1,0:T(8,128)(2,1)S(1)} %collective-permute-done.55.refs_2_), channel_id=1, source_target_pairs={{0,1},{1,0},{2,3},{3,2},{4,5},{5,4},{6,7},{7,6},{8,9},{9,8},{10,11... | collective-permute-start | bytes 540680 | tf_op jit(solution)/shard_map/ppermute | solution.py:94
  185.8 6.7 %collective-permute-start.69 = (bf16[704,128]{1,0:T(8,128)(2,1)S(1)}, bf16[704,128]{1,0:T(8,128)(2,1)S(1)}, u32[]{:S(2)}, u32[]{:S(2)}) collective-permute-start(bf16[704,128]{1,0:T(8,128)(2,1)S(1)} %get-tuple-element.75), channel_id=1, source_target_pairs={{0,16},{16,0},{1,17},{17,1},{2,18},{18,2},{3,19},{19,3},{4,20},{20... | collective-permute-start | bytes 540680 | tf_op jit(solution)/shard_map/ppermute | solution.py:98
  196.0 6.3 %collective-permute-start.75 = (bf16[2,352,128]{2,1,0:T(8,128)(2,1)S(1)}, bf16[2,352,128]{2,1,0:T(8,128)(2,1)S(1)}, u32[]{:S(2)}, u32[]{:S(2)}) collective-permute-start(bf16[2,352,128]{2,1,0:T(8,128)(2,1)S(1)} %get-tuple-element.83), channel_id=1, source_target_pairs={{0,1},{1,0},{2,3},{3,2},{4,5},{5,4},{6,7},{7,6},{8,9},{9,8},{10,11... | collective-permute-start | bytes 540680 | tf_op jit(solution)/shard_map/ppermute | solution.py:94
  202.8 8.9 %collective-permute-start.71 = (bf16[352,128]{1,0:T(8,128)(2,1)S(1)}, bf16[352,128]{1,0:T(8,128)(2,1)S(1)}, u32[]{:S(2)}, u32[]{:S(2)}) collective-permute-start(bf16[352,128]{1,0:T(8,128)(2,1)S(1)} %fusion.26), channel_id=1, source_target_pairs={{0,2},{1,3},{2,0},{3,1},{4,6},{5,7},{6,4},{7,5},{8,10},{9,11},{10,... | collective-permute-start | bytes 270344 | tf_op jit(solution)/shard_map/ppermute | solution.py:90
  204.6 6.5 %collective-permute-start.79 = (bf16[352,128]{1,0:T(8,128)(2,1)S(1)}, bf16[352,128]{1,0:T(8,128)(2,1)S(1)}, u32[]{:S(2)}, u32[]{:S(2)}) collective-permute-start(bf16[352,128]{1,0:T(8,128)(2,1)S(1)} %fusion.29), channel_id=1, source_target_pairs={{0,2},{1,3},{2,0},{3,1},{4,6},{5,7},{6,4},{7,5},{8,10},{9,11},{10,... | collective-permute-start | bytes 270344 | tf_op jit(solution)/shard_map/ppermute | solution.py:90
  205.7 7.2 %collective-permute-start.74 = (bf16[352,128]{1,0:T(8,128)(2,1)S(1)}, bf16[352,128]{1,0:T(8,128)(2,1)S(1)}, u32[]{:S(2)}, u32[]{:S(2)}) collective-permute-start(bf16[352,128]{1,0:T(8,128)(2,1)S(1)} %fusion.22), channel_id=1, source_target_pairs={{0,8},{1,9},{2,10},{3,11},{4,12},{5,13},{6,14},{7,15},{8,0},{9,1},... | collective-permute-start | bytes 270344 | tf_op jit(solution)/shard_map/ppermute | solution.py:84
  211.1 6.4 %collective-permute-start.80 = (bf16[352,128]{1,0:T(8,128)(2,1)S(1)}, bf16[352,128]{1,0:T(8,128)(2,1)S(1)}, u32[]{:S(2)}, u32[]{:S(2)}) collective-permute-start(bf16[352,128]{1,0:T(8,128)(2,1)S(1)} %fusion.20), channel_id=1, source_target_pairs={{0,4},{1,5},{2,6},{3,7},{4,8},{5,9},{6,10},{7,11},{8,12},{9,13},{1... | collective-permute-start | bytes 270344 | tf_op jit(solution)/shard_map/ppermute | solution.py:84
  (36 other events, 221.9 us)
